TPU v7x, 32 devices: a whole 2x2x4 slice. The times are simulated.
32 devices in a mesh: dp: 8 (over z, core), space: 4 (over y, x).
Axes of the slice: x: 2, y: 2, z: 4, core: 2. Of those that a mesh axis runs over, the one named last changes fastest.
Arguments:
- features: bfloat16 [1024, 6272], P(('dp', 'space')), may hold values from -6 to 6
- grad_out: bfloat16 [1024, 6272], P(('dp', 'space')), may hold values from -6 to 6
- wigner: bfloat16 [455, 4096], P(None, ('dp', 'space')), may hold values from -1.5 to 1.5
- sources: int32 [4096], P(('dp', 'space')), may hold values from 0 to 47
- targets: int32 [4096], P(('dp', 'space')), may hold values from 0 to 31
- ghost_index: int32 [32, 2, 8], P(('dp', 'space')), may hold values from 0 to 31
- edge_count: int32 [8, 4], P('dp', 'space'), may hold values from 1 to 128, 384 in all within a row
- mixture: float32 [8, 32], replicated, may hold values from 0.25 to 2
- w_zero: bfloat16 [32, 896, 896], P('dp', 'space'), may hold values from -0.03125 to 0.03125
- w_one: bfloat16 [32, 2, 768, 768], P('dp', None, 'space'), may hold values from -0.02734375 to 0.02734375
- w_two: bfloat16 [32, 2, 640, 640], P('dp', None, 'space'), may hold values from -0.03125 to 0.03125
Outputs:
- updated: bfloat16 [1024, 6272], P(('dp', 'space'))
- grad_features: bfloat16 [1024, 6272], P(('dp', 'space'))
- grad_mix0: bfloat16 [8, 896, 896], P('dp', 'space')
- grad_mix1: bfloat16 [8, 2, 768, 768], P('dp', None, 'space')
- grad_mix2: bfloat16 [8, 2, 640, 640], P('dp', None, 'space')
Inputs may be any that keep to these rules, and one draw needn't show every extreme that they name: `edge_count`: the counts of one system sum to 384, and some device of every system has all 128 slots live.
All inputs are finite; a program needn't handle non-finite values.
Results may differ from a plain program's by a relative error of at most 0.015.
Values may be sent and summed in bfloat16 or wider, within the bound.
No kernel may reach another device: no remote copies, remote signals or barrier semaphores. Data moves between devices by JAX's collectives and lax.ppermute only.
A program may use at most 128 MiB of HBM per device.

v0:
```python
import jax
import jax.numpy as jnp
from jax import lax
from jax.sharding import PartitionSpec as P

CHANNELS = 128
LMAX = 6
MMAX = 2


message_scale = 0.25


def with_halo(shard, sides, width):
    for axis, dim in sides:
        size, length = (lax.axis_size(axis), shard.shape[dim])
        up = [(i, (i + 1) % size) for i in range(size)]
        down = [(j, i) for i, j in up]
        last = lax.slice_in_dim(shard, length - width, length, axis=dim)
        initial = lax.slice_in_dim(shard, 0, width, axis=dim)
        before = lax.ppermute(last, axis, up)
        after = lax.ppermute(initial, axis, down)
        shard = jnp.concatenate([before, shard, after], axis=dim)
    return shard


def as_sent(shard):
    return jax.tree.map(lambda a: a.astype(jnp.bfloat16) if a.dtype == jnp.float32 else a, shard)


def degree_start(degree):
    return degree * (2 * degree - 1) * (2 * degree + 1) // 3


def rotate_into(wigner, edge_rows):
    row_count = edge_rows.shape[0]
    blocks = []
    for degree in range(LMAX + 1):
        extent = 2 * degree + 1
        kept_order = min(degree, MMAX)
        offset = degree_start(degree)
        matrix = wigner[offset : offset + extent * extent].reshape(extent, extent, row_count)[
            degree - kept_order : degree + kept_order + 1
        ]
        segment = edge_rows[
            :, degree * degree * CHANNELS : (degree + 1) * (degree + 1) * CHANNELS
        ].reshape(row_count, extent, CHANNELS)
        blocks.append(
            jnp.einsum("jne,enc->ejc", matrix, segment, preferred_element_type=jnp.float32).astype(
                jnp.bfloat16
            )
        )
    return blocks


def rotate_back(wigner, blocks):
    row_count = blocks[0].shape[0]
    pieces = []
    for degree in range(LMAX + 1):
        extent = 2 * degree + 1
        kept_order = min(degree, MMAX)
        offset = degree_start(degree)
        matrix = wigner[offset : offset + extent * extent].reshape(extent, extent, row_count)[
            degree - kept_order : degree + kept_order + 1
        ]
        pieces.append(
            jnp.einsum(
                "jne,ejc->enc", matrix, blocks[degree], preferred_element_type=jnp.float32
            ).reshape(row_count, extent * CHANNELS)
        )
    return jnp.concatenate(pieces, 1)


def split_frame(blocks):
    row_count = blocks[0].shape[0]
    frame_zero = jnp.stack([blocks[d][:, min(d, MMAX)] for d in range(LMAX + 1)], 1).reshape(
        row_count, -1
    )
    frame_pairs = []
    for order_m in range(1, MMAX + 1):
        plus_part = jnp.stack(
            [blocks[d][:, min(d, MMAX) + order_m] for d in range(order_m, LMAX + 1)], 1
        ).reshape(row_count, -1)
        minus_part = jnp.stack(
            [blocks[d][:, min(d, MMAX) - order_m] for d in range(order_m, LMAX + 1)], 1
        ).reshape(row_count, -1)
        frame_pairs.append((plus_part, minus_part))
    return (frame_zero, frame_pairs)


def join_frame(frame_zero, frame_pairs):
    row_count = frame_zero.shape[0]
    zero_rows = frame_zero.reshape(row_count, LMAX + 1, CHANNELS)
    reshaped = [
        (p.reshape(row_count, -1, CHANNELS), q.reshape(row_count, -1, CHANNELS))
        for p, q in frame_pairs
    ]
    blocks = []
    for degree in range(LMAX + 1):
        kept_order = min(degree, MMAX)
        row_list = []
        for order_m in range(-kept_order, kept_order + 1):
            if order_m == 0:
                row_list.append(zero_rows[:, degree])
            elif order_m > 0:
                row_list.append(reshaped[order_m - 1][0][:, degree - order_m])
            else:
                row_list.append(reshaped[-order_m - 1][1][:, degree + order_m])
        blocks.append(jnp.stack(row_list, 1))
    return blocks


def convolve(frame_zero, frame_pairs, mix_set):
    out_zero = jnp.dot(frame_zero, mix_set[0], preferred_element_type=jnp.float32).astype(
        jnp.bfloat16
    )
    out_pairs = []
    for index_m, (plus_part, minus_part) in enumerate(frame_pairs):
        real_weight = mix_set[index_m + 1][0]
        imag_weight = mix_set[index_m + 1][1]
        out_plus = jnp.dot(plus_part, real_weight, preferred_element_type=jnp.float32) - jnp.dot(
            minus_part, imag_weight, preferred_element_type=jnp.float32
        )
        out_minus = jnp.dot(plus_part, imag_weight, preferred_element_type=jnp.float32) + jnp.dot(
            minus_part, real_weight, preferred_element_type=jnp.float32
        )
        out_pairs.append((out_plus.astype(jnp.bfloat16), out_minus.astype(jnp.bfloat16)))
    return (out_zero, out_pairs)


def transposed(left_side, right_side):
    return lax.dot_general(
        left_side, right_side, (((1,), (1,)), ((), ())), preferred_element_type=jnp.float32
    )


def outer_product(left_side, right_side):
    return lax.dot_general(
        left_side, right_side, (((0,), (0,)), ((), ())), preferred_element_type=jnp.float32
    )


def convolve_back(frame_zero, frame_pairs, mix_set):
    grad_zero = transposed(frame_zero, mix_set[0]).astype(jnp.bfloat16)
    grad_pairs = []
    for index_m, (plus_part, minus_part) in enumerate(frame_pairs):
        real_weight = mix_set[index_m + 1][0]
        imag_weight = mix_set[index_m + 1][1]
        grad_plus = transposed(plus_part, real_weight) + transposed(minus_part, imag_weight)
        grad_minus = transposed(minus_part, real_weight) - transposed(plus_part, imag_weight)
        grad_pairs.append((grad_plus.astype(jnp.bfloat16), grad_minus.astype(jnp.bfloat16)))
    return (grad_zero, grad_pairs)


def weight_terms(frame_zero, frame_pairs, back_zero, back_pairs, weight_scale):
    result = [(weight_scale * outer_product(frame_zero, back_zero))[None]]
    for (plus_part, minus_part), (back_plus, back_minus) in zip(frame_pairs, back_pairs):
        real_grad = outer_product(plus_part, back_plus) + outer_product(minus_part, back_minus)
        imag_grad = outer_product(plus_part, back_minus) - outer_product(minus_part, back_plus)
        result.append(weight_scale * jnp.stack([real_grad, imag_grad]))
    return tuple(result)


def on_device(
    features,
    grad_out,
    wigner,
    sources,
    targets,
    ghost_index,
    edge_count,
    mixture,
    w_zero,
    w_one,
    w_two,
):
    own_rows = features.shape[0]
    edge_total = sources.shape[0]
    ghosts = ghost_index.shape[2]
    spaces = lax.axis_size("space")
    system = lax.axis_index("dp")
    per_group = w_zero.shape[0]
    cut_one = w_zero[0].size
    cut_two = cut_one + w_one[0].size
    local_flat = jnp.concatenate(
        [w_zero.reshape(per_group, -1), w_one.reshape(per_group, -1), w_two.reshape(per_group, -1)],
        1,
    )
    mix_row = lax.dynamic_index_in_dim(mixture, system, 0, keepdims=False)
    outgoing = jnp.concatenate([features[ghost_index[0, 1]], features[ghost_index[0, 0]]], 0)
    extended = with_halo(outgoing, (("space", 0),), ghosts)
    node_table = jnp.concatenate([features, extended[:ghosts], extended[3 * ghosts :]], 0)
    every_expert = lax.all_gather(local_flat, "dp", axis=0, tiled=True)
    grouped = every_expert.reshape(-1, per_group, every_expert.shape[1]).astype(jnp.float32)
    partial_mix = jnp.einsum(
        "ge,gep->gp", mix_row.reshape(-1, per_group), grouped, precision=lax.Precision.HIGHEST
    )
    rounded = lax.optimization_barrier(partial_mix.astype(jnp.bfloat16)).astype(jnp.float32)
    mixed_flat = jnp.sum(rounded, 0).astype(jnp.bfloat16)
    shard_zero = mixed_flat[:cut_one].reshape((1,) + w_zero.shape[1:])
    shard_one = mixed_flat[cut_one:cut_two].reshape(w_one.shape[1:])
    shard_two = mixed_flat[cut_two:].reshape(w_two.shape[1:])
    full_zero, full_one, full_two = (
        lax.all_gather(shard_zero, "space", axis=1, tiled=True),
        lax.all_gather(shard_one, "space", axis=1, tiled=True),
        lax.all_gather(shard_two, "space", axis=1, tiled=True),
    )
    mix_set = (full_zero[0], full_one, full_two)
    edge_rows = node_table[sources]
    frame_zero, frame_pairs = split_frame(rotate_into(wigner, edge_rows))
    out_zero, out_pairs = convolve(frame_zero, frame_pairs, mix_set)
    messages = rotate_back(wigner, join_frame(out_zero, out_pairs)).astype(jnp.bfloat16)
    is_live = jnp.arange(edge_total, dtype=jnp.int32) < edge_count[0, 0]
    target_hot = (
        (targets[None, :] == jnp.arange(own_rows, dtype=jnp.int32)[:, None]) & is_live[None, :]
    ).astype(jnp.bfloat16)
    gathered = jnp.dot(target_hot, messages, preferred_element_type=jnp.float32)
    updated = (features.astype(jnp.float32) + message_scale * gathered).astype(jnp.bfloat16)
    back_msg = (message_scale * outer_product(target_hot, grad_out)).astype(jnp.bfloat16)
    back_zero, back_pairs = split_frame(rotate_into(wigner, back_msg))
    grad_zero, grad_pairs = convolve_back(back_zero, back_pairs, mix_set)
    weight_scale = float(edge_total * spaces) ** (-0.5)
    partials = weight_terms(frame_zero, frame_pairs, back_zero, back_pairs, weight_scale)
    summed = jax.tree.map(
        lambda part: part.astype(jnp.float32),
        lax.psum_scatter(as_sent(partials), "space", scatter_dimension=1, tiled=True),
    )
    grad_mix0 = summed[0].astype(jnp.bfloat16)
    grad_mix1 = summed[1].astype(jnp.bfloat16)[None]
    grad_mix2 = summed[2].astype(jnp.bfloat16)[None]
    back_rows = rotate_back(wigner, join_frame(grad_zero, grad_pairs)).astype(jnp.bfloat16)
    source_hot = (
        sources[:, None] == jnp.arange(own_rows + 2 * ghosts, dtype=jnp.int32)[None, :]
    ).astype(jnp.bfloat16)
    table_grad = outer_product(source_hot, back_rows)
    returning = table_grad[own_rows:].astype(jnp.bfloat16)
    arriving = with_halo(returning, (("space", 0),), ghosts)
    prev_hot = (
        ghost_index[0, 1][:, None] == jnp.arange(own_rows, dtype=jnp.int32)[None, :]
    ).astype(jnp.bfloat16)
    next_hot = (
        ghost_index[0, 0][:, None] == jnp.arange(own_rows, dtype=jnp.int32)[None, :]
    ).astype(jnp.bfloat16)
    combined = grad_out.astype(jnp.float32) + table_grad[:own_rows]
    combined = (
        combined
        + outer_product(prev_hot, arriving[:ghosts])
        + outer_product(next_hot, arriving[3 * ghosts :])
    )
    grad_features = combined.astype(jnp.bfloat16)
    return (updated, grad_features, grad_mix0, grad_mix1, grad_mix2)


def solution(mesh):
    return jax.shard_map(
        on_device,
        mesh=mesh,
        in_specs=(
            P(("dp", "space"), None),
            P(("dp", "space"), None),
            P(None, ("dp", "space")),
            P(("dp", "space")),
            P(("dp", "space")),
            P(("dp", "space"), None, None),
            P("dp", "space"),
            P(),
            P("dp", "space", None),
            P("dp", None, "space", None),
            P("dp", None, "space", None),
        ),
        out_specs=(
            P(("dp", "space"), None),
            P(("dp", "space"), None),
            P("dp", "space", None),
            P("dp", None, "space", None),
            P("dp", None, "space", None),
        ),
        check_vma=False,
    )
```

profile of v0, /device:TPU:0, one launch (start us, length us, event | category | flops | bytes accessed | tf_op | source)
XLA Modules:
  0.0 814.2 jit_solution(2488848049592475312)
XLA Ops:
  7.2 2.8 copy.402
  10.1 1.8 copy.401
  12.8 53.1 %maximum_bitcast_fusion = bf16[1,4,700416]{2,1,0:T(4,128)(2,1)} fusion(bf16[4,204800]{1,0:T(4,128)(2,1)S(1)} %bitcast.277, bf16[4,294912]{1,0:T(4,128)(2,1)S(1)} %bitcast.276, bf16[4,200704]{1,0:T(4,128)(2,1)S(1)} %bitcast.278), kind=kLoop, calls=%fused_computation.12 | loop fusion | flops 16809984 | bytes 11206656
  66.1 385.2 %all-gather.12.cloned.1.call-done = bf16[8,4,700416]{2,1,0:T(4,128)(2,1)} async-done(((bf16[1,4,700416]{2,1,0:T(4,128)(2,1)}), bf16[8,4,700416]{2,1,0:T(4,128)(2,1)}) %all-gather.12.cloned.1.call-update) | async-done | bytes 44826640 | tf_op jit(solution)/shard_map/all_gather | solution.py:193
  451.3 77.1 %fusion.108 = bf16[8,1,700416]{2,1,0:T(2,128)(2,1)} fusion(f32[8,4,1]{1,2,0:T(1,128)S(1)} %bitcast.358, bf16[8,4,700416]{2,1,0:T(4,128)(2,1)} %all-gather.12.cloned.1.call-done), kind=kOutput, calls=%fused_computation.216 | convolution fusion | flops 268959744 | bytes 56033408 | tf_op jit(solution)/shard_map/ge,gep->gp/dot_general | solution.py:195
  528.4 16.9 %copy.422 = bf16[8,1,700416]{2,0,1:T(8,128)(2,1)} copy(bf16[8,1,700416]{2,1,0:T(2,128)(2,1)} %fusion.108) | data formatting | bytes 22413312 | tf_op jit(solution)/shard_map/ge,gep->gp/dot_general | solution.py:195
  545.3 24.9 %reduce_sum.12 = bf16[700416]{0:T(1024)(128)(2,1)S(1)} reduce(bf16[8,700416]{1,0:T(8,128)(2,1)} %bitcast.275, bf16[]{:T(256)} %constant.6.clone.1), dimensions={0}, to_apply=%region_0.1 | reduce | flops 4902912 | bytes 12607490 | tf_op jit(solution)/shard_map/reduce_sum | solution.py:199
  572.8 2.4 collective-permute-start.1
  600.9 1.8 copy.288
  646.6 2.0 fusion.5
  648.6 2.9 fusion.21
  656.3 2.1 fusion.18
  672.8 2.2 fusion.37
  712.7 2.5 fusion.25
  722.4 1.8 copy.217
  736.1 2.0 stack.92
  738.1 2.2 fusion.12
  743.3 2.1 stack.93
  745.4 2.1 fusion.13
  750.5 2.0 stack.94
  752.5 2.2 fusion.14
  793.2 2.4 fusion.107
  795.6 3.0 collective-permute-start.3
  801.9 4.0 collective-permute-done.2
  (534 shorter events, 195.7 us)
Async XLA Ops:
  7.2 58.8 %copy-start = (f32[8,32]{1,0:T(8,128)S(1)}, f32[8,32]{1,0:T(8,128)}, u32[]{:S(2)}) copy-start(f32[8,32]{1,0:T(8,128)} %param.18) | copy-start | bytes 3076
  7.2 444.1 %all-gather.12.cloned.1.call-start = ((), (), s32[]{:S(2)}) async-start(), calls=%async_computation.9 | async-start | bytes 50429952 | tf_op jit(solution)/shard_map/all_gather | solution.py:193
  65.9 582.6 %all-gather.6.cloned.1.call-start = ((), (), s32[]{:S(2)}) async-start(), calls=%async_computation.3 | async-start | bytes 2007040 | tf_op jit(solution)/shard_map/all_gather | solution.py:204
  570.2 7.2 copy-start.33
  570.2 7.2 copy-start.105
  571.4 99.7 %all-gather.10.cloned.1.call-start = ((), (), s32[]{:S(2)}) async-start(), calls=%async_computation.5 | async-start | bytes 2048000 | tf_op jit(solution)/shard_map/all_gather | solution.py:206
  572.8 29.9 %collective-permute-start.1 = (bf16[8,6272]{1,0:T(8,128)(2,1)}, bf16[8,6272]{1,0:T(8,128)(2,1)}, u32[]{:S(2)}, u32[]{:S(2)}) collective-permute-start(bf16[8,6272]{1,0:T(8,128)(2,1)} %gather_fusion.1), channel_id=1, source_target_pairs={{1,0},{2,1},{3,2},{0,3},{5,4},{6,5},{7,6},{4,7},{9,8},{10,9},{11,1... | collective-permute-start | bytes 301064 | tf_op jit(solution)/shard_map/ppermute | solution.py:22
  576.4 26.3 %collective-permute-start = (bf16[8,6272]{1,0:T(8,128)(2,1)}, bf16[8,6272]{1,0:T(8,128)(2,1)}, u32[]{:S(2)}, u32[]{:S(2)}) collective-permute-start(bf16[8,6272]{1,0:T(8,128)(2,1)} %gather_fusion), channel_id=1, source_target_pairs={{0,1},{1,2},{2,3},{3,0},{4,5},{5,6},{6,7},{7,4},{8,9},{9,10},{10,1... | collective-permute-start | bytes 301064 | tf_op jit(solution)/shard_map/ppermute | solution.py:21
  587.0 124.1 %all-gather.8.cloned.1.call-start = ((), (), s32[]{:S(2)}) async-start(), calls=%async_computation.4 | async-start | bytes 2949120 | tf_op jit(solution)/shard_map/all_gather | solution.py:205
  600.6 206.5 %reduce-scatter.4.cloned.1.call-start = ((), (), s32[]{:S(2)}) async-start(), calls=%async_computation.6 | async-start | bytes 2007040 | tf_op jit(solution)/shard_map/reduce_scatter | solution.py:226
  629.8 177.4 %reduce-scatter.8.cloned.1.call-start = ((), (), s32[]{:S(2)}) async-start(), calls=%async_computation.8 | async-start | bytes 2048000 | tf_op jit(solution)/shard_map/reduce_scatter | solution.py:226
  636.8 7.0 copy-start.49
  636.8 170.3 %reduce-scatter.6.cloned.1.call-start = ((), (), s32[]{:S(2)}) async-start(), calls=%async_computation.7 | async-start | bytes 2949120 | tf_op jit(solution)/shard_map/reduce_scatter | solution.py:226
  643.7 67.3 %copy-start.16 = (bf16[128,6,128]{0,2,1:T(8,128)(2,1)}, bf16[128,6,128]{0,2,1:T(8,128)(2,1)S(1)}, u32[]{:S(2)}) copy-start(bf16[128,6,128]{0,2,1:T(8,128)(2,1)S(1)} %copy.215) | copy-start | bytes 589828
  648.6 7.7 copy-start.5
  658.4 8.3 %copy-start.86 = (bf16[128,1,128]{0,2,1:T(8,128)(2,1)S(1)}, bf16[128,1,128]{0,2,1:T(8,128)(2,1)}, u32[]{:S(2)}) copy-start(bf16[128,1,128]{0,2,1:T(8,128)(2,1)} %get-tuple-element.36) | copy-start | bytes 98308
  658.4 9.0 %copy-start.85 = (bf16[128,1,128]{0,2,1:T(8,128)(2,1)S(1)}, bf16[128,1,128]{0,2,1:T(8,128)(2,1)}, u32[]{:S(2)}) copy-start(bf16[128,1,128]{0,2,1:T(8,128)(2,1)} %get-tuple-element.35) | copy-start | bytes 98308
  658.4 9.8 %copy-start.84 = (bf16[128,1,128]{0,2,1:T(8,128)(2,1)S(1)}, bf16[128,1,128]{0,2,1:T(8,128)(2,1)}, u32[]{:S(2)}) copy-start(bf16[128,1,128]{0,2,1:T(8,128)(2,1)} %get-tuple-element.34) | copy-start | bytes 98308
  658.4 10.5 %copy-start.83 = (bf16[128,1,128]{0,2,1:T(8,128)(2,1)S(1)}, bf16[128,1,128]{0,2,1:T(8,128)(2,1)}, u32[]{:S(2)}) copy-start(bf16[128,1,128]{0,2,1:T(8,128)(2,1)} %get-tuple-element.33) | copy-start | bytes 98308
  671.2 8.5 %copy-start.3 = (bf16[2,640,640]{2,1,0:T(8,128)(2,1)S(1)}, bf16[2,640,640]{2,1,0:T(8,128)(2,1)}, u32[]{:S(2)}) copy-start(bf16[2,640,640]{2,1,0:T(8,128)(2,1)} %all-gather.10.cloned.1.call-done) | copy-start | bytes 4915204
  712.7 7.3 copy-start.2
  795.6 5.9 collective-permute-start.3
  799.0 7.0 copy-start.34
  800.4 5.5 collective-permute-start.2
  (110 other events, 386.3 us)
Sparse Core Ops, SparseCore 0:
  66.0 385.1 all-gather.11
  571.6 29.6 all-gather.5
  603.1 31.5 all-gather.9
  636.3 37.5 all-gather.7
  677.3 31.1 reduce-scatter.3
  711.9 31.4 reduce-scatter.7
  747.0 37.3 reduce-scatter.5
where the time goes:
time: 822 us; the launch traced here: 814 us
  waiting for transfers between devices  390 us (47%)
  local copies, waits for them, and re-layouts  182 us (22%)
  matrix products  133 us (16%)
  other arithmetic  85 us (10%)
  between operations  17.1 us (2%)
    all_gather x1, waiting for transfers between devices, on_device(): every_expert = lax.all_gather(local_flat, 'dp', axis=0, tiled=True)  385 us
    dot_general x1, matrix products, on_device(): jnp.einsum('ge,gep->gp', mix_row.reshape(-1, per_group), grouped, precisi...  77.1 us
    unnamed x304, local copies, waits for them, and re-layouts  73.2 us
    unnamed x2, other arithmetic  53.8 us
    reduce_sum x1, other arithmetic, on_device(): mixed_flat = jnp.sum(rounded, 0).astype(jnp.bfloat16)  24.9 us
    dot_general x1, local copies, waits for them, and re-layouts, on_device(): jnp.einsum('ge,gep->gp', mix_row.reshape(-1, per_group), grouped, precisi...  16.9 us
  transfers between devices with their start and end apart: 11, of which 3 were waited for; matrix products, arithmetic and copies ran while one was open for 27% of the time, Pallas kernels for 0%

commit v1 on v0

v1 whole, which is shorter than its diff:
```python
import functools

import jax
import jax.numpy as jnp
from jax import lax
from jax.experimental import pallas as pl
from jax.experimental.pallas import tpu as pltpu
from jax.sharding import PartitionSpec as P

CHANNELS = 128
LMAX = 6
MMAX = 2
MESSAGE_SCALE = 0.25

BLOCK_COUNTS = (LMAX + 1, LMAX, LMAX, LMAX - 1, LMAX - 1)
FRAME_BLOCKS = sum(BLOCK_COUNTS)
FRAME_W = FRAME_BLOCKS * CHANNELS
COEFFS = (LMAX + 1) ** 2
NODE_W = COEFFS * CHANNELS

NN = (((1,), (0,)), ((), ()))
NT = (((1,), (1,)), ((), ()))
TN = (((0,), (0,)), ((), ()))

PARAMS = pltpu.CompilerParams(vmem_limit_bytes=48 * 1024 * 1024)
VMEM = pl.BlockSpec(memory_space=pltpu.VMEM)
SMEM = pl.BlockSpec(memory_space=pltpu.SMEM)
ANY = pl.BlockSpec(memory_space=pl.ANY)
HBM = pl.BlockSpec(memory_space=pltpu.HBM)


def dot(a, b, dims=NN):
    return lax.dot_general(a, b, dims, preferred_element_type=jnp.float32)


def degree_start(degree):
    return degree * (2 * degree - 1) * (2 * degree + 1) // 3


def frame_block(degree, order):
    if order == 0:
        return degree
    group = 2 * abs(order) - (1 if order > 0 else 0)
    return sum(BLOCK_COUNTS[:group]) + degree - abs(order)


def identity():
    rows = lax.broadcasted_iota(jnp.int32, (CHANNELS, CHANNELS), 0)
    cols = lax.broadcasted_iota(jnp.int32, (CHANNELS, CHANNELS), 1)
    return jnp.where(rows == cols, 1.0, 0.0).astype(jnp.bfloat16)


def mix_kernel(offset, other_offset, place_ref, mixture_ref, own_ref, other_ref, *refs):
    (both, across, here), (own, other, sems) = refs[:3], refs[3:]
    per_group, rows, width = own.shape
    outs = (both.at[:rows], both.at[rows:], across, here)
    blocks = sems.shape[1]
    block = rows // blocks
    copies = []
    for b in range(blocks):
        span = pl.ds(b * block, block)
        source = pl.ds(offset + b * block, block)
        copies.append(
            (
                pltpu.make_async_copy(own_ref.at[:, source, :], own.at[:, span, :], sems.at[0, b]),
                pltpu.make_async_copy(
                    other_ref.at[:, pl.ds(other_offset + b * block, block), :],
                    other.at[:, span, :],
                    sems.at[1, b],
                ),
            )
        )
    for pair in copies:
        for copy in pair:
            copy.start()
    dp = place_ref[0]
    z = dp // 2
    core = dp % 2
    beside = z + 1 - 2 * (z % 2)
    dests = (beside, 3 - beside, 3 - z, z)
    partner = dp + 1 - 2 * core
    coefs = []
    for dest in dests:
        system = 2 * dest + core
        coefs.append(
            [mixture_ref[system, dp * per_group + e] for e in range(per_group)]
            + [mixture_ref[system, partner * per_group + e] for e in range(per_group)]
        )

    def body(step, carry):
        row = pl.multiple_of(step * 16, 16)
        for column in range(0, width, CHANNELS):
            span = pl.ds(column, CHANNELS)
            parts = [own[e, pl.ds(row, 16), span].astype(jnp.float32) for e in range(per_group)]
            parts += [other[e, pl.ds(row, 16), span].astype(jnp.float32) for e in range(per_group)]
            for out, coef in zip(outs, coefs):
                total = coef[0] * parts[0]
                for c, part in zip(coef[1:], parts[1:]):
                    total = total + c * part
                out[pl.ds(row, 16), span] = total.astype(jnp.bfloat16)
        return carry

    for b, pair in enumerate(copies):
        for copy in pair:
            copy.wait()
        lax.fori_loop(b * block // 16, (b + 1) * block // 16, body, 0)


def mix(place, mixture, own, other, offset, other_offset, rows):
    per_group, _, width = other.shape
    blocks = 2 if rows % 32 == 0 else 1
    pair = jax.ShapeDtypeStruct((2 * rows, width), jnp.bfloat16)
    single = jax.ShapeDtypeStruct((rows, width), jnp.bfloat16)
    return pl.pallas_call(
        functools.partial(mix_kernel, offset, other_offset),
        in_specs=[SMEM, SMEM, HBM, ANY],
        out_specs=[VMEM] * 3,
        out_shape=[pair, single, single],
        scratch_shapes=[
            pltpu.VMEM((per_group, rows, width), jnp.bfloat16),
            pltpu.VMEM((per_group, rows, width), jnp.bfloat16),
            pltpu.SemaphoreType.DMA((2, blocks)),
        ],
        compiler_params=PARAMS,
        name="mix",
    )(place, mixture, pltpu.with_memory_space_constraint(own, pltpu.HBM), other)


def pick_kernel(index_ref, features_ref, next_ref, prev_ref):
    own = features_ref.shape[0]
    ghosts = index_ref.shape[2]
    columns = lax.broadcasted_iota(jnp.int32, (ghosts, own), 1)
    for place, out in ((0, next_ref), (1, prev_ref)):
        rows = lax.broadcasted_iota(jnp.int32, (ghosts, own), 0)
        wanted = jnp.zeros((ghosts, own), jnp.int32)
        for g in range(ghosts):
            wanted = jnp.where(rows == g, index_ref[0, place, g], wanted)
        hot = jnp.where(columns == wanted, 1.0, 0.0).astype(jnp.bfloat16)
        out[...] = dot(hot, features_ref[...]).astype(jnp.bfloat16)


def pick_ghosts(index, features):
    out = jax.ShapeDtypeStruct((index.shape[2], features.shape[1]), jnp.bfloat16)
    return pl.pallas_call(
        pick_kernel,
        in_specs=[SMEM, VMEM],
        out_specs=[VMEM] * 2,
        out_shape=[out, out],
        compiler_params=PARAMS,
        name="pick_ghosts",
    )(index, features)


def hot_rows(index, count, values=1.0, start=0):
    rows = lax.broadcasted_iota(jnp.int32, (count, index.shape[1]), 0) + start
    return jnp.where(index == rows, values, 0.0).astype(jnp.bfloat16)


def turn_into(wide, sources, targets):
    step_rows = 32

    def body(step, carry):
        base = pl.multiple_of(step * step_rows, step_rows)
        for degree in range(LMAX + 1):
            extent = 2 * degree + 1
            kept = min(degree, MMAX)
            for order in range(-kept, kept + 1):
                start = degree_start(degree) + extent * (degree + order)
                totals = [0.0] * len(sources)
                for n in range(extent):
                    row = pl.ds((degree * degree + n) * CHANNELS + base, step_rows)
                    factor = wide[pl.ds(start + n, 1), :]
                    totals = [t + factor * s[row, :] for t, s in zip(totals, sources)]
                place = pl.ds(frame_block(degree, order) * CHANNELS + base, step_rows)
                for target, total in zip(targets, totals):
                    target[place, :] = total.astype(jnp.bfloat16)
        return carry

    lax.fori_loop(0, CHANNELS // step_rows, body, 0)


BAND = 16


def packed_rows(own, wigner_rows, slab_rows):
    rotations = COEFFS * own
    targets = rotations + BAND * -(-wigner_rows // BAND)
    slab = targets + BAND
    return rotations, targets, slab, slab + slab_rows


def enter_kernel(
    place_ref, count_ref, features_ref, ghosts_ref, grad_ref, sources_ref, targets_ref, wigner_ref,
    frame_ref, back_ref, slab_ref, *rest,
):
    packs, (wide, forward, backward, turned, turned_back) = rest[:-5], rest[-5:]
    own = features_ref.shape[0]
    edges = sources_ref.shape[1]
    extra = ghosts_ref.shape[0]
    wig_rows = wigner_ref.shape[0]
    wide[...] = wigner_ref[...].astype(jnp.float32)
    sources = sources_ref[...]
    live = lax.broadcasted_iota(jnp.int32, (1, edges), 1) < count_ref[0, 0]
    targets = jnp.where(live, targets_ref[...], -1)
    from_own = hot_rows(sources, own)
    from_ghost = hot_rows(sources, extra, start=own)
    to_own = hot_rows(targets, own, MESSAGE_SCALE)
    for n in range(COEFFS):
        span = pl.ds(n * CHANNELS, CHANNELS)
        forward[span, :] = dot(features_ref[:, span], from_own, TN) + dot(
            ghosts_ref[:, span], from_ghost, TN
        )
        backward[span, :] = dot(grad_ref[:, span], to_own, TN)
    turn_into(wide, (forward, backward), (turned, turned_back))
    eye = identity()
    for k in range(FRAME_BLOCKS):
        span = pl.ds(k * CHANNELS, CHANNELS)
        frame_ref[:, span] = dot(eye, turned[span, :], NT).astype(jnp.bfloat16)
        back_ref[:, span] = dot(eye, turned_back[span, :], NT).astype(jnp.bfloat16)
    spaces = len(packs) + 1
    rotations_at, targets_at, slab_at, _ = packed_rows(own, wig_rows, slab_ref.shape[0])
    for peer in range(spaces):
        position = lax.bitwise_xor(place_ref[1], jnp.int32(peer))
        out, at = (slab_ref, 0) if peer == 0 else (packs[peer - 1], slab_at)
        first = 0
        for blocks in BLOCK_COUNTS:
            rows = blocks * CHANNELS // spaces
            begin = pl.multiple_of(first + position * rows, BAND)
            out[at : at + rows, :] = turned[pl.ds(begin, rows), :]
            at += rows
            first += blocks * CHANNELS
    padding = jnp.zeros((targets_at - rotations_at - wig_rows, edges), jnp.float32)
    rotations = jnp.concatenate([wide[...], padding], 0).astype(jnp.bfloat16)
    marks = jnp.broadcast_to(targets.astype(jnp.float32), (BAND, edges)).astype(jnp.bfloat16)
    for pack in packs:
        for n in range(COEFFS):
            pack[n * own : (n + 1) * own, :] = grad_ref[:, n * CHANNELS : (n + 1) * CHANNELS]
        pack[rotations_at:targets_at, :] = rotations
        pack[targets_at:slab_at, :] = marks


def enter(place, count, features, ghosts, grad_out, sources, targets, wigner, spaces):
    edges = sources.shape[1]
    frame = jax.ShapeDtypeStruct((edges, FRAME_W), jnp.bfloat16)
    slab = jax.ShapeDtypeStruct((FRAME_W // spaces, edges), jnp.bfloat16)
    pack_rows = packed_rows(features.shape[0], wigner.shape[0], FRAME_W // spaces)[-1]
    pack = jax.ShapeDtypeStruct((pack_rows, edges), jnp.bfloat16)
    return pl.pallas_call(
        enter_kernel,
        in_specs=[SMEM, SMEM] + [VMEM] * 6,
        out_specs=[VMEM] * (2 + spaces),
        out_shape=[frame, frame, slab] + [pack] * (spaces - 1),
        scratch_shapes=[
            pltpu.VMEM((wigner.shape[0], edges), jnp.float32),
            pltpu.VMEM((NODE_W, edges), jnp.float32),
            pltpu.VMEM((NODE_W, edges), jnp.float32),
            pltpu.VMEM((FRAME_W, edges), jnp.bfloat16),
            pltpu.VMEM((FRAME_W, edges), jnp.bfloat16),
        ],
        compiler_params=PARAMS,
        name="enter_frame",
    )(place, count, features, ghosts, grad_out, sources, targets, wigner)


def peer_frames_kernel(own, wig_rows, slab_rows, *refs):
    packs, (out, wide, backward, turned_back) = refs[:-4], refs[-4:]
    rotations_at, targets_at, slab_at, _ = packed_rows(own, wig_rows, slab_rows)
    eye = identity()
    for peer, pack in enumerate(packs):
        wide[...] = pack[rotations_at:targets_at, :].astype(jnp.float32)
        targets = pack[targets_at:slab_at, :].astype(jnp.float32)[:1].astype(jnp.int32)
        to_own = hot_rows(targets, own, MESSAGE_SCALE)
        for n in range(COEFFS):
            backward[n * CHANNELS : (n + 1) * CHANNELS, :] = dot(
                pack[n * own : (n + 1) * own, :], to_own, TN
            )
        turn_into(wide, (backward,), (turned_back,))
        for k in range(FRAME_BLOCKS):
            span = pl.ds(k * CHANNELS, CHANNELS)
            out[peer, :, span] = dot(eye, turned_back[span, :], NT).astype(jnp.bfloat16)


def peer_frames(packs, own, wig_rows, slab_rows):
    edges = packs[0].shape[1]
    return pl.pallas_call(
        functools.partial(peer_frames_kernel, own, wig_rows, slab_rows),
        in_specs=[VMEM] * len(packs),
        out_specs=VMEM,
        out_shape=jax.ShapeDtypeStruct((len(packs), edges, FRAME_W), jnp.bfloat16),
        scratch_shapes=[
            pltpu.VMEM((BAND * -(-wig_rows // BAND), edges), jnp.float32),
            pltpu.VMEM((NODE_W, edges), jnp.float32),
            pltpu.VMEM((FRAME_W, edges), jnp.bfloat16),
        ],
        compiler_params=PARAMS,
        name="peer_frames",
    )(*packs)


def weight_grad_kernel(scale, slab_ref, back_ref, backs, *refs):
    packs, (out_zero, out_one, out_two) = refs[:-3], refs[-3:]
    spaces = len(packs) + 1
    end = packs[0].shape[0]
    all_slabs = [slab_ref] + [pack.at[end - slab_ref.shape[0] : end] for pack in packs]
    all_backs = [back_ref] + [backs.at[k] for k in range(spaces - 1)]
    rows = [blocks * CHANNELS // spaces for blocks in BLOCK_COUNTS]
    widths = [blocks * CHANNELS for blocks in BLOCK_COUNTS]

    def product(a, b):
        left = slice(sum(rows[:a]), sum(rows[: a + 1]))
        right = slice(sum(widths[:b]), sum(widths[: b + 1]))
        return sum(dot(s[left, :], d[:, right]) for s, d in zip(all_slabs, all_backs))

    out_zero[...] = (scale * product(0, 0)).astype(jnp.bfloat16)
    for out, group in ((out_one, 1), (out_two, 3)):
        out[0] = (scale * (product(group, group) + product(group + 1, group + 1))).astype(jnp.bfloat16)
        out[1] = (scale * (product(group, group + 1) - product(group + 1, group))).astype(jnp.bfloat16)


def weight_grads(slab, back, backs, packs, scale):
    spaces = len(packs) + 1
    k0, k1, _, k2, _ = [blocks * CHANNELS for blocks in BLOCK_COUNTS]
    return pl.pallas_call(
        functools.partial(weight_grad_kernel, scale),
        in_specs=[VMEM] * (2 + spaces),
        out_specs=[VMEM] * 3,
        out_shape=[
            jax.ShapeDtypeStruct((k0 // spaces, k0), jnp.bfloat16),
            jax.ShapeDtypeStruct((2, k1 // spaces, k1), jnp.bfloat16),
            jax.ShapeDtypeStruct((2, k2 // spaces, k2), jnp.bfloat16),
        ],
        compiler_params=PARAMS,
        name="weight_grads",
    )(slab, back, backs, *packs)


def apply_kernel(group, places, local_rows, place_ref, frame_ref, back_ref, *refs):
    shards, (out_ref, grad_ref, full) = refs[:-3], refs[-3:]
    parts = 1 if group == 0 else 2
    for (peer, first_part, count, offset), shard in zip(places, shards):
        position = lax.bitwise_xor(place_ref[1], jnp.int32(peer))
        rows = shard.shape[0] // count
        begin = pl.multiple_of(position * local_rows + offset, 16)
        for k in range(count):
            full[first_part + k, pl.ds(begin, rows), :] = shard[k * rows : (k + 1) * rows, :]
    first = sum(BLOCK_COUNTS[:group]) * CHANNELS
    width = BLOCK_COUNTS[group] * CHANNELS
    eye = identity()
    edges = frame_ref.shape[0]

    def put_turned(value, offset):
        value = value.astype(jnp.bfloat16)
        for k in range(0, width, CHANNELS):
            out_ref[offset + k : offset + k + CHANNELS, :] = dot(
                eye, value[:, k : k + CHANNELS], NT
            ).astype(jnp.bfloat16)

    if parts == 1:
        grad_ref[...] = dot(full[0], back_ref[:, first : first + width], NT).astype(jnp.bfloat16)
        put_turned(dot(frame_ref[:, first : first + width], full[0]), 0)
        return
    second = first + width
    back = jnp.concatenate([back_ref[:, first:second], back_ref[:, second : second + width]], 0)
    real = dot(full[0], back, NT)
    imag = dot(full[1], back, NT)
    grad_ref[:width, :] = (real[:, :edges] + imag[:, edges:]).astype(jnp.bfloat16)
    grad_ref[width:, :] = (real[:, edges:] - imag[:, :edges]).astype(jnp.bfloat16)
    frame = jnp.concatenate([frame_ref[:, first:second], frame_ref[:, second : second + width]], 0)
    real = dot(frame, full[0])
    imag = dot(frame, full[1])
    put_turned(real[:edges] - imag[edges:], 0)
    put_turned(imag[:edges] + real[edges:], width)


def apply_weights(group, place, frame, back, pieces, spaces):
    places, shards = zip(*pieces)
    edges = frame.shape[0]
    width = BLOCK_COUNTS[group] * CHANNELS
    parts = 1 if group == 0 else 2
    out = jax.ShapeDtypeStruct((parts * width, edges), jnp.bfloat16)
    return pl.pallas_call(
        functools.partial(apply_kernel, group, places, width // spaces),
        in_specs=[SMEM] + [VMEM] * (2 + len(shards)),
        out_specs=[VMEM] * 2,
        out_shape=[out, out],
        scratch_shapes=[pltpu.VMEM((parts, width, width), jnp.bfloat16)],
        compiler_params=PARAMS,
        name=f"apply_weights_{group}",
    )(place, frame, back, *shards)


def leave(frames, wigner_ref, wide, turned):
    wide[...] = wigner_ref[...].astype(jnp.float32)
    step_rows = 32

    def body(step, carry):
        base = pl.multiple_of(step * step_rows, step_rows)
        for degree in range(LMAX + 1):
            extent = 2 * degree + 1
            kept = min(degree, MMAX)
            values = []
            for order in range(-kept, kept + 1):
                source = frames[abs(order)]
                block = degree - abs(order)
                if order < 0:
                    block += BLOCK_COUNTS[2 * -order]
                values.append(
                    source[pl.ds(block * CHANNELS + base, step_rows), :].astype(jnp.float32)
                )
            for n in range(extent):
                total = 0.0
                for order, value in zip(range(-kept, kept + 1), values):
                    start = degree_start(degree) + extent * (degree + order) + n
                    total = total + wide[pl.ds(start, 1), :] * value
                row = pl.ds((degree * degree + n) * CHANNELS + base, step_rows)
                turned[row, :] = total.astype(jnp.bfloat16)
        return carry

    lax.fori_loop(0, CHANNELS // step_rows, body, 0)


def leave_back_kernel(
    zero_ref, one_ref, two_ref, wigner_ref, sources_ref, grad_ref, base_ref, ghost_ref, wide, turned
):
    leave((zero_ref, one_ref, two_ref), wigner_ref, wide, turned)
    own = grad_ref.shape[0]
    extra = ghost_ref.shape[0]
    edges = sources_ref.shape[1]
    rows = lax.broadcasted_iota(jnp.int32, (own + extra, edges), 0)
    hot = jnp.where(sources_ref[...] == rows, 1.0, 0.0).astype(jnp.bfloat16)
    for n in range(COEFFS):
        span = pl.ds(n * CHANNELS, CHANNELS)
        table = dot(hot, turned[span, :], NT)
        base_ref[:, span] = grad_ref[:, span].astype(jnp.float32) + table[:own]
        ghost_ref[:, span] = table[own:].astype(jnp.bfloat16)


def leave_kernel(
    zero_ref, one_ref, two_ref, wigner_ref, count_ref, targets_ref, features_ref, out_ref, wide, turned
):
    leave((zero_ref, one_ref, two_ref), wigner_ref, wide, turned)
    own = features_ref.shape[0]
    edges = targets_ref.shape[1]
    rows = lax.broadcasted_iota(jnp.int32, (own, edges), 0)
    live = lax.broadcasted_iota(jnp.int32, (own, edges), 1) < count_ref[0, 0]
    hot = jnp.where((targets_ref[...] == rows) & live, MESSAGE_SCALE, 0.0).astype(jnp.bfloat16)
    for n in range(COEFFS):
        span = pl.ds(n * CHANNELS, CHANNELS)
        out_ref[:, span] = (
            features_ref[:, span].astype(jnp.float32) + dot(hot, turned[span, :], NT)
        ).astype(jnp.bfloat16)


def leave_scratch(wigner):
    rows, edges = wigner.shape
    return [pltpu.VMEM((rows, edges), jnp.float32), pltpu.VMEM((NODE_W, edges), jnp.bfloat16)]


def leave_back(frames, wigner, sources, grad_out, extra):
    own = grad_out.shape[0]
    return pl.pallas_call(
        leave_back_kernel,
        in_specs=[VMEM] * 6,
        out_specs=[VMEM] * 2,
        out_shape=[
            jax.ShapeDtypeStruct((own, NODE_W), jnp.float32),
            jax.ShapeDtypeStruct((extra, NODE_W), jnp.bfloat16),
        ],
        scratch_shapes=leave_scratch(wigner),
        compiler_params=PARAMS,
        name="leave_frame_back",
    )(*frames, wigner, sources, grad_out)


def leave_forward(frames, wigner, count, targets, features):
    return pl.pallas_call(
        leave_kernel,
        in_specs=[VMEM] * 4 + [SMEM] + [VMEM] * 2,
        out_specs=VMEM,
        out_shape=jax.ShapeDtypeStruct(features.shape, jnp.bfloat16),
        scratch_shapes=leave_scratch(wigner),
        compiler_params=PARAMS,
        name="leave_frame",
    )(*frames, wigner, count, targets, features)


def settle_kernel(base_ref, next_ref, prev_ref, index_ref, out_ref):
    own = base_ref.shape[0]
    ghosts = next_ref.shape[0]
    rows = lax.broadcasted_iota(jnp.int32, (own, ghosts), 0)
    total = base_ref[...]
    for place, ref in ((0, next_ref), (1, prev_ref)):
        hot = jnp.where(index_ref[place : place + 1, :] == rows, 1.0, 0.0)
        total = total + dot(hot, ref[...].astype(jnp.float32))
    out_ref[...] = total.astype(jnp.bfloat16)


def settle(base, from_next, from_prev, index):
    return pl.pallas_call(
        settle_kernel,
        in_specs=[VMEM] * 4,
        out_specs=VMEM,
        out_shape=jax.ShapeDtypeStruct(base.shape, jnp.bfloat16),
        compiler_params=PARAMS,
        name="settle_ghosts",
    )(base, from_next, from_prev, index)


def together(*values):
    return lax.optimization_barrier(values)


CORES = [(i, i ^ 1) for i in range(8)]
BESIDE = [(2 * z + c, 2 * (z ^ 1) + c) for z in range(4) for c in range(2)]
OPPOSITE = [(2 * z + c, 2 * (3 - z) + c) for z in range(4) for c in range(2)]


def add(*parts):
    return sum(part.astype(jnp.float32) for part in parts).astype(jnp.bfloat16)


def mixed_general(mixture, own):
    per_group = own.shape[0]
    columns = lax.dynamic_slice_in_dim(mixture, lax.axis_index("dp") * per_group, per_group, 1)
    sums = jnp.einsum(
        "se,erk->srk", columns, own.astype(jnp.float32), precision=lax.Precision.HIGHEST
    ).astype(jnp.bfloat16)
    return lax.psum_scatter(sums, "dp", scatter_dimension=0, tiled=False)


def to_peer(array, spaces, k):
    return lax.ppermute(array, "space", [(i, i ^ k) for i in range(spaces)])


def on_device(
    features,
    grad_out,
    wigner,
    sources,
    targets,
    ghost_index,
    edge_count,
    mixture,
    w_zero,
    w_one,
    w_two,
):
    edges = sources.shape[0]
    own_rows = features.shape[0]
    ghosts = ghost_index.shape[2]
    spaces = lax.axis_size("space")
    place = jnp.stack([lax.axis_index("dp"), lax.axis_index("space")]).astype(jnp.int32)
    up = [(i, (i + 1) % spaces) for i in range(spaces)]
    down = [(j, i) for i, j in up]
    per_group, rows_zero = w_zero.shape[:2]
    rows_one, rows_two = w_one.shape[2], w_two.shape[2]
    sources = sources.reshape(1, edges)
    targets = targets.reshape(1, edges)
    w_one = w_one.reshape(per_group, -1, w_one.shape[-1])
    w_two = w_two.reshape(per_group, -1, w_two.shape[-1])
    scale = float(edges * spaces) ** (-0.5)

    def frames(from_prev, from_next):
        return enter(
            place,
            edge_count,
            features,
            jnp.concatenate([from_prev, from_next], 0),
            grad_out,
            sources,
            targets,
            wigner,
            spaces,
        )

    to_next, to_prev = pick_ghosts(ghost_index, features)

    if lax.axis_size("dp") == 8 and spaces == 4:
        half = rows_zero // 2
        chunks = [
            (0, w_zero, 0, half, (0, 1, 0)),
            (3, w_two, 0, 2 * rows_two, (0, 2, 0)),
            (1, w_one, 0, rows_one, (0, 1, 0)),
            (1, w_one, rows_one, rows_one, (1, 1, 0)),
            (0, w_zero, half, rows_zero - half, (0, 1, half)),
        ]

        def swap_cores(array):
            return lax.ppermute(array, "dp", CORES)

        def mix_chunk(j, other, other_first=0):
            _, own, first, rows, _ = chunks[j]
            return mix(place, mixture, own, other, first, other_first, rows)

        def swap_beside(both):
            return lax.ppermute(both, "dp", BESIDE)

        def total_opposite(j, across, beside):
            return add(across, beside[chunks[j][3] :])

        def swap_opposite(total):
            return lax.ppermute(total, "dp", OPPOSITE)

        def total_here(j, here, beside, opposite):
            return add(here, beside[: chunks[j][3]], opposite)

        def to_sides(shard):
            return to_peer(shard, spaces, 1), to_peer(shard, spaces, 2)

        def forward(j, sides):
            along = 2 - j % 2
            return to_peer(sides[(3 ^ along) - 1], spaces, along)

        def pieces(j, shard, sides, last):
            return [((k,) + chunks[j][4], a) for k, a in enumerate((shard, *sides, last))]

        other0 = swap_cores(w_zero)
        other0, to_next, to_prev = together(other0, to_next, to_prev)
        both0, across0, here0 = mix_chunk(0, other0)
        beside0 = swap_beside(both0)
        from_prev = lax.ppermute(to_next, "space", up)
        from_next = lax.ppermute(to_prev, "space", down)
        sent, other0 = together(w_two, other0)
        other1 = swap_cores(sent)
        both1, across1, here1 = mix_chunk(1, other1)
        beside1 = swap_beside(both1)
        beside0, here1, from_prev, from_next = together(beside0, here1, from_prev, from_next)
        total0 = total_opposite(0, across0, beside0)
        opposite0 = swap_opposite(total0)
        sent, other1, here1 = together(w_one, other1, here1)
        other2 = swap_cores(sent)
        total0, from_prev, from_next = together(total0, from_prev, from_next)
        frame, back, slab, *packs = frames(from_prev, from_next)
        opposite0, frame = together(opposite0, frame)
        shard0 = total_here(0, here0, beside0, opposite0)
        shard0, packs[0], packs[1], other2 = together(shard0, packs[0], packs[1], other2)
        sides0 = to_sides(shard0)
        side_packs = [to_peer(packs[0], spaces, 1), to_peer(packs[1], spaces, 2)]
        other2, frame = together(other2, frame)
        both2, across2, here2 = mix_chunk(2, other2)
        beside2 = swap_beside(both2)
        both3, across3, here3 = mix_chunk(3, other2, rows_one)
        beside1, here2, here3, *sides0 = together(beside1, here2, here3, *sides0)
        total1 = total_opposite(1, across1, beside1)
        opposite1 = swap_opposite(total1)
        both3, beside2, here3 = together(both3, beside2, here3)
        beside3 = swap_beside(both3)
        total2 = total_opposite(2, across2, beside2)
        opposite2 = swap_opposite(total2)
        last_pack, total2, *side_packs = together(packs[2], total2, *side_packs)
        last_pack = to_peer(last_pack, spaces, 3)
        other0, total2 = together(other0, total2)
        both4, across4, here4 = mix_chunk(4, other0, half)
        opposite1, here4 = together(opposite1, here4)
        shard1 = total_here(1, here1, beside1, opposite1)
        shard1, *sides0 = together(shard1, *sides0)
        sides1 = to_sides(shard1)
        forward0 = forward(0, sides0)
        both4, beside3, here4, shard1 = together(both4, beside3, here4, shard1)
        beside4 = swap_beside(both4)
        total3 = total_opposite(3, across3, beside3)
        opposite3 = swap_opposite(total3)
        opposite2, total3 = together(opposite2, total3)
        shard2 = total_here(2, here2, beside2, opposite2)
        last_pack, shard2 = together(last_pack, shard2)
        packs_in = [*side_packs, last_pack]
        backs = peer_frames(packs_in, own_rows, wigner.shape[0], slab.shape[0])
        sides2 = to_sides(shard2)
        beside4, backs, *sides1 = together(beside4, backs, *sides1)
        forward1 = forward(1, sides1)
        total4 = total_opposite(4, across4, beside4)
        opposite4 = swap_opposite(total4)
        opposite3, total4 = together(opposite3, total4)
        shard3 = total_here(3, here3, beside3, opposite3)
        sides3 = to_sides(shard3)
        back, shard3 = together(back, shard3)
        grad_mix = weight_grads(slab, back, backs, packs_in, scale)
        opposite4, *grad_mix = together(opposite4, *grad_mix)
        opposite4, forward1, *sides2 = together(opposite4, forward1, *sides2)
        forward2 = forward(2, sides2)
        shard4 = total_here(4, here4, beside4, opposite4)
        sides4 = to_sides(shard4)
        outs, grads = {}, {}
        whole = {
            3: pieces(1, shard1, sides1, forward1),
            1: pieces(2, shard2, sides2, forward2) + pieces(3, shard3, sides3, forward(3, sides3)),
            0: pieces(0, shard0, sides0, forward0) + pieces(4, shard4, sides4, to_peer(shard4, spaces, 3)),
        }
    else:
        from_prev = lax.ppermute(to_next, "space", up)
        from_next = lax.ppermute(to_prev, "space", down)
        frame, back, slab, *packs = frames(from_prev, from_next)
        packs_in = [to_peer(pack, spaces, k + 1) for k, pack in enumerate(packs)]
        backs = peer_frames(packs_in, own_rows, wigner.shape[0], slab.shape[0])
        grad_mix = weight_grads(slab, back, backs, packs_in, scale)
        outs, grads, whole = {}, {}, {}
        for group, own, parts in ((3, w_two, 2), (1, w_one, 2), (0, w_zero, 1)):
            shard = mixed_general(mixture, own)
            whole[group] = [((0, 0, parts, 0), shard)] + [
                ((k, 0, parts, 0), to_peer(shard, spaces, k)) for k in range(1, spaces)
            ]

    for group, pieces_of in whole.items():
        outs[group], grads[group] = apply_weights(group, place, frame, back, pieces_of, spaces)
    base, returning = leave_back(
        [grads[g] for g in (0, 1, 3)], wigner, sources, grad_out, 2 * ghosts
    )
    back_next = lax.ppermute(returning[:ghosts], "space", down)
    back_prev = lax.ppermute(returning[ghosts:], "space", up)
    updated = leave_forward([outs[g] for g in (0, 1, 3)], wigner, edge_count, targets, features)
    grad_features = settle(base, back_next, back_prev, ghost_index[0])
    grad_mix0, grad_mix1, grad_mix2 = grad_mix
    return (updated, grad_features, grad_mix0[None], grad_mix1[None], grad_mix2[None])


def solution(mesh):
    return jax.shard_map(
        on_device,
        mesh=mesh,
        in_specs=(
            P(("dp", "space"), None),
            P(("dp", "space"), None),
            P(None, ("dp", "space")),
            P(("dp", "space")),
            P(("dp", "space")),
            P(("dp", "space"), None, None),
            P("dp", "space"),
            P(),
            P("dp", "space", None),
            P("dp", None, "space", None),
            P("dp", None, "space", None),
        ),
        out_specs=(
            P(("dp", "space"), None),
            P(("dp", "space"), None),
            P("dp", "space", None),
            P("dp", None, "space", None),
            P("dp", None, "space", None),
        ),
        check_vma=False,
    )
```

time: 822 us -> 159 us (0.19)
  waiting for transfers between devices: 390 us -> 51.2 us
  local copies, waits for them, and re-layouts: 182 us -> 3.96 us
  matrix products: 133 us -> 0 us
  other arithmetic: 85 us -> 4 us
  Pallas kernels: 0 us -> 47.7 us
  starting transfers between devices: 6.27 us -> 49.6 us
  between operations: 17.1 us -> 1.63 us
    all_gather x4 -> x0, waiting for transfers between devices: 385 us -> none  [the longest x1 385 us: on_device(): every_expert = lax.all_gather(local_flat, 'dp', axis=0, tiled=True)]
    dot_general x57 -> x0, matrix products: 133 us -> none  [the longest x1 77.1 us: on_device(): jnp.einsum('ge,gep->gp', mix_row.reshape(-1, per_group), grouped, precisi...]
    unnamed x304 -> x24, local copies, waits for them, and re-layouts: 73.2 us -> 3.95 us
    unnamed x2 -> x0, other arithmetic: 53.8 us -> none
    pallas_call x0 -> x15, Pallas kernels: none -> 47.7 us  [the longest x5 15.9 us: mix(): pl.pallas_call(functools.partial(mix_kernel, offset, other_offset), in_sp...]
    ppermute x4 -> x35, waiting for transfers between devices: 5.15 us -> 51.2 us  [the longest x5 21.3 us: swap_beside(): return lax.ppermute(both, 'dp', BESIDE)]
    ppermute x4 -> x35, starting transfers between devices: 5.8 us -> 49.6 us  [the longest x18 21.3 us: to_peer(): return lax.ppermute(array, 'space', [(i, i ^ k) for i in range(spaces)])]
    dot_general x19 -> x0, local copies, waits for them, and re-layouts: 28.4 us -> none  [the longest x1 16.9 us: on_device(): jnp.einsum('ge,gep->gp', mix_row.reshape(-1, per_group), grouped, precisi...]
  transfers between devices with their start and end apart: 11 -> 35, of which waited for: 3 -> 14; matrix products, arithmetic and copies ran while one was open for 27% -> 3% of each run, Pallas kernels for 0% -> 26%
where the time goes in v1:
time: 159 us; the launch traced here: 158 us
  waiting for transfers between devices  51.2 us (32%)
  starting transfers between devices  49.6 us (31%)
  Pallas kernels  47.7 us (30%)
  other arithmetic  4 us (3%)
  local copies, waits for them, and re-layouts  3.96 us (2%)
  between operations  1.63 us (1%)
    ppermute x5, waiting for transfers between devices, swap_beside(): return lax.ppermute(both, 'dp', BESIDE)  21.3 us
    ppermute x18, starting transfers between devices, to_peer(): return lax.ppermute(array, 'space', [(i, i ^ k) for i in range(spaces)])  21.3 us
    ppermute x18, waiting for transfers between devices, to_peer(): return lax.ppermute(array, 'space', [(i, i ^ k) for i in range(spaces)])  16.8 us
    pallas_call x5, Pallas kernels, mix(): pl.pallas_call(functools.partial(mix_kernel, offset, other_offset), in_sp...  15.9 us
    ppermute x5, starting transfers between devices, swap_opposite(): return lax.ppermute(total, 'dp', OPPOSITE)  11.8 us
    ppermute x5, starting transfers between devices, swap_beside(): return lax.ppermute(both, 'dp', BESIDE)  10.2 us
    ppermute x5, waiting for transfers between devices, swap_opposite(): return lax.ppermute(total, 'dp', OPPOSITE)  8.59 us
    pallas_call x1, Pallas kernels, peer_frames(): pl.pallas_call(functools.partial(peer_frames_kernel, own, wig_rows, slab_...  7.36 us
  transfers between devices with their start and end apart: 35, of which 14 were waited for; matrix products, arithmetic and copies ran while one was open for 3% of the time, Pallas kernels for 26%

profile of v1, /device:TPU:0, one launch (start us, length us, event | category | flops | bytes accessed | tf_op | source)
XLA Modules:
  0.0 158.1 jit_solution(9172574609155722542)
XLA Ops:
  5.6 2.8 %mix.5 = (bf16[224,896]{1,0:T(8,128)(2,1)S(1)}, bf16[112,896]{1,0:T(8,128)(2,1)S(1)}, bf16[112,896]{1,0:T(8,128)(2,1)S(1)}) custom-call(s32[2]{0:T(128)S(1)} %pad_add_fusion.place_ref, f32[8,32]{1,0:T(8,128)S(1)} %copy-done.5, bf16[4,224,896]{2,1,0:T(8,128)(2,1)} %own_ref.3, bf16[4,224,896]{2,1,0:T(8,128)(2,1)S(1)} %collective-permute-done.other_ref), custom_call_target="tpu_custom_call" | custom-call | tf_op jit(solution)/shard_map/mix/pallas_call | solution.py:114
  8.4 2.8 %collective-permute-start.1 = (bf16[224,896]{1,0:T(8,128)(2,1)S(1)}, bf16[224,896]{1,0:T(8,128)(2,1)S(1)}, u32[]{:S(2)}, u32[]{:S(2)}) collective-permute-start(bf16[224,896]{1,0:T(8,128)(2,1)S(1)} %get-tuple-element.102), channel_id=1, source_target_pairs={{0,8},{4,12},{8,0},{12,4},{16,24},{20,28},{24,16},{28,20},{1,9},{5... | collective-permute-start | bytes 1204232 | tf_op jit(solution)/shard_map/ppermute | solution.py:596
  14.1 3.9 %mix.6 = (bf16[640,640]{1,0:T(8,128)(2,1)S(1)}, bf16[320,640]{1,0:T(8,128)(2,1)S(1)}, bf16[320,640]{1,0:T(8,128)(2,1)S(1)}) custom-call(s32[2]{0:T(128)S(1)} %pad_add_fusion.place_ref, f32[8,32]{1,0:T(8,128)S(1)} %copy-done.5, bf16[4,320,640]{2,1,0:T(8,128)(2,1)} %bitcast.16, bf16[4,320,640]{2,1,0:T(8,128)(2,1)S(1)} %collective-permute-done.2.other_ref), custom_call_target="tpu_custom_call" | custom-call | tf_op jit(solution)/shard_map/mix/pallas_call | solution.py:114
  21.7 3.8 %collective-permute-start.5 = (bf16[112,896]{1,0:T(8,128)(2,1)S(1)}, bf16[112,896]{1,0:T(8,128)(2,1)S(1)}, u32[]{:S(2)}, u32[]{:S(2)}) collective-permute-start(bf16[112,896]{1,0:T(8,128)(2,1)S(1)} %add_convert_fusion.9), channel_id=1, source_target_pairs={{0,24},{4,28},{8,16},{12,20},{16,8},{20,12},{24,0},{28,4},{1,25},{... | collective-permute-start | bytes 602120 | tf_op jit(solution)/shard_map/ppermute | solution.py:602
  25.7 5.5 %enter_frame.1 = (bf16[128,3712]{1,0:T(8,128)(2,1)S(1)}, bf16[128,3712]{1,0:T(8,128)(2,1)S(1)}, bf16[928,128]{1,0:T(8,128)(2,1)S(1)}, bf16[2976,128]{1,0:T(8,128...) custom-call(s32[2]{0:T(128)S(1)} %pad_add_fusion.place_ref, s32[1,1]{1,0:T(1,128)S(6)} %copy.16.count_ref, ...), custom_call_target="tpu_custom_call" | custom-call | tf_op jit(solution)/shard_map/enter_frame/pallas_call | solution.py:248
  31.6 3.2 %mix.8 = (bf16[384,768]{1,0:T(8,128)(2,1)S(1)}, bf16[192,768]{1,0:T(8,128)(2,1)S(1)}, bf16[192,768]{1,0:T(8,128)(2,1)S(1)}) custom-call(s32[2]{0:T(128)S(1)} %pad_add_fusion.place_ref, f32[8,32]{1,0:T(8,128)S(1)} %copy-done.6, bf16[4,384,768]{2,1,0:T(8,128)(2,1)} %bitcast.5.own_ref, bf16[4,384,768]{2,1,0:T(8,128)(2,1)S(1)} %collective-permute-done.6.other_ref), custom_call_target="tpu_custom_call" | custom-call | tf_op jit(solution)/shard_map/mix/pallas_call | solution.py:114
  34.9 3.8 %collective-permute-start.7 = (bf16[384,768]{1,0:T(8,128)(2,1)S(1)}, bf16[384,768]{1,0:T(8,128)(2,1)S(1)}, u32[]{:S(2)}, u32[]{:S(2)}) collective-permute-start(bf16[384,768]{1,0:T(8,128)(2,1)S(1)} %get-tuple-element.125), channel_id=1, source_target_pairs={{0,8},{4,12},{8,0},{12,4},{16,24},{20,28},{24,16},{28,20},{1,9},{5... | collective-permute-start | bytes 1769480 | tf_op jit(solution)/shard_map/ppermute | solution.py:596
  42.2 6.9 %collective-permute-done.8 = bf16[640,640]{1,0:T(8,128)(2,1)} collective-permute-done((bf16[640,640]{1,0:T(8,128)(2,1)S(1)}, bf16[640,640]{1,0:T(8,128)(2,1)}, u32[]{:S(2)}, u32[]{:S(2)}) %collective-permute-start.8) | collective-permute-done | bytes 819232 | tf_op jit(solution)/shard_map/ppermute | solution.py:596
  50.6 3.2 %mix.7 = (bf16[384,768]{1,0:T(8,128)(2,1)S(1)}, bf16[192,768]{1,0:T(8,128)(2,1)S(1)}, bf16[192,768]{1,0:T(8,128)(2,1)S(1)}) custom-call(s32[2]{0:T(128)S(1)} %pad_add_fusion.place_ref, f32[8,32]{1,0:T(8,128)S(1)} %copy-done.6, bf16[4,384,768]{2,1,0:T(8,128)(2,1)} %bitcast.5.own_ref, bf16[4,384,768]{2,1,0:T(8,128)(2,1)S(1)} %collective-permute-done.6.other_ref), custom_call_target="tpu_custom_call" | custom-call | tf_op jit(solution)/shard_map/mix/pallas_call | solution.py:114
  57.2 4.5 %collective-permute-done.7 = bf16[384,768]{1,0:T(8,128)(2,1)S(1)} collective-permute-done((bf16[384,768]{1,0:T(8,128)(2,1)S(1)}, bf16[384,768]{1,0:T(8,128)(2,1)S(1)}, u32[]{:S(2)}, u32[]{:S(2)}) %collective-permute-start.7) | collective-permute-done | bytes 589856 | tf_op jit(solution)/shard_map/ppermute | solution.py:596
  63.6 2.8 %mix.9 = (bf16[224,896]{1,0:T(8,128)(2,1)S(1)}, bf16[112,896]{1,0:T(8,128)(2,1)S(1)}, bf16[112,896]{1,0:T(8,128)(2,1)S(1)}) custom-call(s32[2]{0:T(128)S(1)} %pad_add_fusion.place_ref, f32[8,32]{1,0:T(8,128)S(1)} %copy-done.6, bf16[4,224,896]{2,1,0:T(8,128)(2,1)} %own_ref.3, bf16[4,224,896]{2,1,0:T(8,128)(2,1)S(1)} %collective-permute-done.other_ref), custom_call_target="tpu_custom_call" | custom-call | tf_op jit(solution)/shard_map/mix/pallas_call | solution.py:114
  66.7 3.9 %collective-permute-done.12 = bf16[320,640]{1,0:T(8,128)(2,1)S(1)} collective-permute-done((bf16[320,640]{1,0:T(8,128)(2,1)S(1)}, bf16[320,640]{1,0:T(8,128)(2,1)S(1)}, u32[]{:S(2)}, u32[]{:S(2)}) %collective-permute-start.12) | collective-permute-done | bytes 409632 | tf_op jit(solution)/shard_map/ppermute | solution.py:602
  70.6 2.5 %collective-permute-start.17 = (bf16[2976,128]{1,0:T(8,128)(2,1)S(1)}, bf16[2976,128]{1,0:T(8,128)(2,1)S(1)}, u32[]{:S(2)}, u32[]{:S(2)}) collective-permute-start(bf16[2976,128]{1,0:T(8,128)(2,1)S(1)} %get-tuple-element.155), channel_id=1, source_target_pairs={{0,3},{1,2},{2,1},{3,0},{4,7},{5,6},{6,5},{7,4},{8,11},{9,10},{10,... | collective-permute-start | bytes 2285576 | tf_op jit(solution)/shard_map/ppermute | solution.py:532
  75.3 8.0 %collective-permute-done.11 = bf16[384,768]{1,0:T(8,128)(2,1)S(1)} collective-permute-done((bf16[384,768]{1,0:T(8,128)(2,1)S(1)}, bf16[384,768]{1,0:T(8,128)(2,1)S(1)}, u32[]{:S(2)}, u32[]{:S(2)}) %collective-permute-start.11) | collective-permute-done | bytes 589856 | tf_op jit(solution)/shard_map/ppermute | solution.py:596
  85.2 4.3 %collective-permute-done.18 = bf16[192,768]{1,0:T(8,128)(2,1)S(1)} collective-permute-done((bf16[192,768]{1,0:T(8,128)(2,1)S(1)}, bf16[192,768]{1,0:T(8,128)(2,1)S(1)}, u32[]{:S(2)}, u32[]{:S(2)}) %collective-permute-start.18) | collective-permute-done | bytes 294944 | tf_op jit(solution)/shard_map/ppermute | solution.py:602
  89.5 3.7 %collective-permute-start.13 = (bf16[192,768]{1,0:T(8,128)(2,1)S(1)}, bf16[192,768]{1,0:T(8,128)(2,1)S(1)}, u32[]{:S(2)}, u32[]{:S(2)}) collective-permute-start(bf16[192,768]{1,0:T(8,128)(2,1)S(1)} %add_convert_fusion.5), channel_id=1, source_target_pairs={{0,24},{4,28},{8,16},{12,20},{16,8},{20,12},{24,0},{28,4},{1,25},{... | collective-permute-start | bytes 884744 | tf_op jit(solution)/shard_map/ppermute | solution.py:602
  94.9 7.4 %peer_frames.1.backs = bf16[3,128,3712]{2,1,0:T(8,128)(2,1)S(1)} custom-call(bf16[2976,128]{1,0:T(8,128)(2,1)S(1)} %collective-permute-done.15.refs_0_, bf16[2976,128]{1,0:T(8,128)(2,1)S(1)} %collective-permute-done.16.refs_1_, bf16[2976,128]{1,0:T(8,128)(2,1)S(1)} %collective-permute-done.17.refs_2_), custom_call_target="tpu_custom_call" | custom-call | tf_op jit(solution)/shard_map/peer_frames/pallas_call | solution.py:285
  109.4 5.2 %weight_grads.1 = (bf16[224,896]{1,0:T(8,128)(2,1)}, bf16[2,192,768]{2,1,0:T(8,128)(2,1)}, bf16[2,160,640]{2,1,0:T(8,128)(2,1)}) custom-call(bf16[928,128]{1,0:T(8,128)(2,1)S(1)} %get-tuple-element.165.slab_ref, bf16[128,3712]{1,0:T(8,128)(2,1)S(1)} %get-tuple-element.161.back_ref, bf16[3,128,3712]{2,1,0:T(8,128)(2,1)} %copy-done, ...), custom_call_target="tpu_custom_call" | custom-call | tf_op jit(solution)/shard_map/weight_grads/pallas_call | solution.py:323
  116.1 4.3 %collective-permute-done.23.refs_3_ = bf16[320,640]{1,0:T(8,128)(2,1)S(1)} collective-permute-done((bf16[320,640]{1,0:T(8,128)(2,1)S(1)}, bf16[320,640]{1,0:T(8,128)(2,1)S(1)}, u32[]{:S(2)}, u32[]{:S(2)}) %collective-permute-start.23) | collective-permute-done | bytes 409632 | tf_op jit(solution)/shard_map/ppermute | solution.py:532
  132.0 3.1 %collective-permute-done.27.refs_6_ = bf16[112,896]{1,0:T(8,128)(2,1)S(1)} collective-permute-done((bf16[112,896]{1,0:T(8,128)(2,1)S(1)}, bf16[112,896]{1,0:T(8,128)(2,1)S(1)}, u32[]{:S(2)}, u32[]{:S(2)}) %collective-permute-start.27) | collective-permute-done | bytes 200736 | tf_op jit(solution)/shard_map/ppermute | solution.py:532
  135.1 7.0 %collective-permute-done.28.refs_7_ = bf16[112,896]{1,0:T(8,128)(2,1)S(1)} collective-permute-done((bf16[112,896]{1,0:T(8,128)(2,1)S(1)}, bf16[112,896]{1,0:T(8,128)(2,1)S(1)}, u32[]{:S(2)}, u32[]{:S(2)}) %collective-permute-start.28) | collective-permute-done | bytes 200736 | tf_op jit(solution)/shard_map/ppermute | solution.py:532
  143.8 2.7 %apply_weights_1.1 = (bf16[1536,128]{1,0:T(8,128)(2,1)S(1)}, bf16[1536,128]{1,0:T(8,128)(2,1)S(1)}) custom-call(s32[2]{0:T(128)S(1)} %pad_add_fusion.place_ref, bf16[128,3712]{1,0:T(8,128)(2,1)S(1)} %get-tuple-element.121.frame_ref, bf16[128,3712]{1,0:T(8,128)(2,1)S(1)} %get-tuple-element.161.back_ref, bf16[192,768]{1,0:T(8,128)(2,1)S(1)} %add_convert_fusion.3.refs_0_, ...), custom_call_target="tpu_custom_call" | custom-call | tf_op jit(solution)/shard_map/apply_weights_1/pallas_call | solution.py:381
  151.4 2.9 %leave_frame.1 = bf16[32,6272]{1,0:T(8,128)(2,1)} custom-call(bf16[896,128]{1,0:T(8,128)(2,1)S(1)} %get-tuple-element.174.zero_ref, bf16[1536,128]{1,0:T(8,128)(2,1)S(1)} %get-tuple-element.178.one_ref, bf16[1280,128]{1,0:T(8,128)(2,1)S(1)} %get-tuple-element.182.two_ref, bf16[455,128]{1,0:T(8,128)(2,1)S(1)} %copy-done.4, s32[1,1]{1,0:T(1,128)S(6)} %copy.16.count_ref, ...), custom_call_target="tpu_custom_call" | custom-call | tf_op jit(solution)/shard_map/leave_frame/pallas_call | solution.py:476
  154.3 2.6 %collective-permute-done.34.prev_ref = bf16[8,6272]{1,0:T(8,128)(2,1)S(1)} collective-permute-done((bf16[8,6272]{1,0:T(8,128)(2,1)S(1)}, bf16[8,6272]{1,0:T(8,128)(2,1)S(1)}, u32[]{:S(2)}, u32[]{:S(2)}) %collective-permute-start.34) | collective-permute-done | bytes 100384 | tf_op jit(solution)/shard_map/ppermute | solution.py:709
  (98 shorter events, 55.6 us)
Async XLA Ops:
  8.4 12.6 %collective-permute-start.1 = (bf16[224,896]{1,0:T(8,128)(2,1)S(1)}, bf16[224,896]{1,0:T(8,128)(2,1)S(1)}, u32[]{:S(2)}, u32[]{:S(2)}) collective-permute-start(bf16[224,896]{1,0:T(8,128)(2,1)S(1)} %get-tuple-element.102), channel_id=1, source_target_pairs={{0,8},{4,12},{8,0},{12,4},{16,24},{20,28},{24,16},{28,20},{1,9},{5... | collective-permute-start | bytes 1204232 | tf_op jit(solution)/shard_map/ppermute | solution.py:596
  21.0 10.6 %collective-permute-start.6 = (bf16[4,384,768]{2,1,0:T(8,128)(2,1)}, bf16[4,384,768]{2,1,0:T(8,128)(2,1)S(1)}, u32[]{:S(2)}, u32[]{:S(2)}) collective-permute-start(bf16[4,384,768]{2,1,0:T(8,128)(2,1)} %bitcast.5.own_ref), channel_id=1, source_target_pairs={{0,4},{4,0},{8,12},{12,8},{16,20},{20,16},{24,28},{28,24},{1,5},{5... | collective-permute-start | bytes 7077896 | tf_op jit(solution)/shard_map/ppermute | solution.py:589
  25.6 23.5 %collective-permute-start.8 = (bf16[640,640]{1,0:T(8,128)(2,1)S(1)}, bf16[640,640]{1,0:T(8,128)(2,1)}, u32[]{:S(2)}, u32[]{:S(2)}) collective-permute-start(bf16[640,640]{1,0:T(8,128)(2,1)S(1)} %get-tuple-element.126), channel_id=1, source_target_pairs={{0,8},{4,12},{8,0},{12,4},{16,24},{20,28},{24,16},{28,20},{1,9},{5... | collective-permute-start | bytes 2457608 | tf_op jit(solution)/shard_map/ppermute | solution.py:596
  34.9 26.9 %collective-permute-start.7 = (bf16[384,768]{1,0:T(8,128)(2,1)S(1)}, bf16[384,768]{1,0:T(8,128)(2,1)S(1)}, u32[]{:S(2)}, u32[]{:S(2)}) collective-permute-start(bf16[384,768]{1,0:T(8,128)(2,1)S(1)} %get-tuple-element.125), channel_id=1, source_target_pairs={{0,8},{4,12},{8,0},{12,4},{16,24},{20,28},{24,16},{28,20},{1,9},{5... | collective-permute-start | bytes 1769480 | tf_op jit(solution)/shard_map/ppermute | solution.py:596
  38.6 15.2 %collective-permute-start.9 = (bf16[112,896]{1,0:T(8,128)(2,1)S(1)}, bf16[112,896]{1,0:T(8,128)(2,1)S(1)}, u32[]{:S(2)}, u32[]{:S(2)}) collective-permute-start(bf16[112,896]{1,0:T(8,128)(2,1)S(1)} %add_convert_fusion.8.refs_0_), channel_id=1, source_target_pairs={{0,1},{1,0},{2,3},{3,2},{4,5},{5,4},{6,7},{7,6},{8,9},{9,8},{10,11... | collective-permute-start | bytes 602120 | tf_op jit(solution)/shard_map/ppermute | solution.py:532
  40.1 13.7 %collective-permute-start.10 = (bf16[112,896]{1,0:T(8,128)(2,1)S(1)}, bf16[112,896]{1,0:T(8,128)(2,1)S(1)}, u32[]{:S(2)}, u32[]{:S(2)}) collective-permute-start(bf16[112,896]{1,0:T(8,128)(2,1)S(1)} %add_convert_fusion.8.refs_0_), channel_id=1, source_target_pairs={{0,2},{1,3},{2,0},{3,1},{4,6},{5,7},{6,4},{7,5},{8,10},{9,11},{10,... | collective-permute-start | bytes 602120 | tf_op jit(solution)/shard_map/ppermute | solution.py:532
  41.7 28.9 %collective-permute-start.15 = (bf16[2976,128]{1,0:T(8,128)(2,1)S(1)}, bf16[2976,128]{1,0:T(8,128)(2,1)S(1)}, u32[]{:S(2)}, u32[]{:S(2)}) collective-permute-start(bf16[2976,128]{1,0:T(8,128)(2,1)S(1)} %get-tuple-element.151), channel_id=1, source_target_pairs={{0,1},{1,0},{2,3},{3,2},{4,5},{5,4},{6,7},{7,6},{8,9},{9,8},{10,11... | collective-permute-start | bytes 2285576 | tf_op jit(solution)/shard_map/ppermute | solution.py:532
  49.1 21.5 %collective-permute-start.16 = (bf16[2976,128]{1,0:T(8,128)(2,1)S(1)}, bf16[2976,128]{1,0:T(8,128)(2,1)S(1)}, u32[]{:S(2)}, u32[]{:S(2)}) collective-permute-start(bf16[2976,128]{1,0:T(8,128)(2,1)S(1)} %get-tuple-element.152), channel_id=1, source_target_pairs={{0,2},{1,3},{2,0},{3,1},{4,6},{5,7},{6,4},{7,5},{8,10},{9,11},{10,... | collective-permute-start | bytes 2285576 | tf_op jit(solution)/shard_map/ppermute | solution.py:532
  55.0 15.6 %collective-permute-start.12 = (bf16[320,640]{1,0:T(8,128)(2,1)S(1)}, bf16[320,640]{1,0:T(8,128)(2,1)S(1)}, u32[]{:S(2)}, u32[]{:S(2)}) collective-permute-start(bf16[320,640]{1,0:T(8,128)(2,1)S(1)} %add_convert_fusion.1), channel_id=1, source_target_pairs={{0,24},{4,28},{8,16},{12,20},{16,8},{20,12},{24,0},{28,4},{1,25},{... | collective-permute-start | bytes 1228808 | tf_op jit(solution)/shard_map/ppermute | solution.py:602
  61.8 21.5 %collective-permute-start.11 = (bf16[384,768]{1,0:T(8,128)(2,1)S(1)}, bf16[384,768]{1,0:T(8,128)(2,1)S(1)}, u32[]{:S(2)}, u32[]{:S(2)}) collective-permute-start(bf16[384,768]{1,0:T(8,128)(2,1)S(1)} %get-tuple-element.134), channel_id=1, source_target_pairs={{0,8},{4,12},{8,0},{12,4},{16,24},{20,28},{24,16},{28,20},{1,9},{5... | collective-permute-start | bytes 1769480 | tf_op jit(solution)/shard_map/ppermute | solution.py:596
  66.5 23.1 %collective-permute-start.18 = (bf16[192,768]{1,0:T(8,128)(2,1)S(1)}, bf16[192,768]{1,0:T(8,128)(2,1)S(1)}, u32[]{:S(2)}, u32[]{:S(2)}) collective-permute-start(bf16[192,768]{1,0:T(8,128)(2,1)S(1)} %add_convert_fusion.4), channel_id=1, source_target_pairs={{0,24},{4,28},{8,16},{12,20},{16,8},{20,12},{24,0},{28,4},{1,25},{... | collective-permute-start | bytes 884744 | tf_op jit(solution)/shard_map/ppermute | solution.py:602
  70.6 22.8 %collective-permute-start.17 = (bf16[2976,128]{1,0:T(8,128)(2,1)S(1)}, bf16[2976,128]{1,0:T(8,128)(2,1)S(1)}, u32[]{:S(2)}, u32[]{:S(2)}) collective-permute-start(bf16[2976,128]{1,0:T(8,128)(2,1)S(1)} %get-tuple-element.155), channel_id=1, source_target_pairs={{0,3},{1,2},{2,1},{3,0},{4,7},{5,6},{6,5},{7,4},{8,11},{9,10},{10,... | collective-permute-start | bytes 2285576 | tf_op jit(solution)/shard_map/ppermute | solution.py:532
  74.3 29.6 %collective-permute-start.19 = (bf16[320,640]{1,0:T(8,128)(2,1)S(1)}, bf16[320,640]{1,0:T(8,128)(2,1)S(1)}, u32[]{:S(2)}, u32[]{:S(2)}) collective-permute-start(bf16[320,640]{1,0:T(8,128)(2,1)S(1)} %add_convert_fusion.refs_0_), channel_id=1, source_target_pairs={{0,1},{1,0},{2,3},{3,2},{4,5},{5,4},{6,7},{7,6},{8,9},{9,8},{10,11... | collective-permute-start | bytes 1228808 | tf_op jit(solution)/shard_map/ppermute | solution.py:532
  74.9 30.5 %collective-permute-start.20 = (bf16[320,640]{1,0:T(8,128)(2,1)S(1)}, bf16[320,640]{1,0:T(8,128)(2,1)S(1)}, u32[]{:S(2)}, u32[]{:S(2)}) collective-permute-start(bf16[320,640]{1,0:T(8,128)(2,1)S(1)} %add_convert_fusion.refs_0_), channel_id=1, source_target_pairs={{0,2},{1,3},{2,0},{3,1},{4,6},{5,7},{6,4},{7,5},{8,10},{9,11},{10,... | collective-permute-start | bytes 1228808 | tf_op jit(solution)/shard_map/ppermute | solution.py:532
  83.3 22.6 %collective-permute-start.14 = (bf16[224,896]{1,0:T(8,128)(2,1)S(1)}, bf16[224,896]{1,0:T(8,128)(2,1)S(1)}, u32[]{:S(2)}, u32[]{:S(2)}) collective-permute-start(bf16[224,896]{1,0:T(8,128)(2,1)S(1)} %get-tuple-element.147), channel_id=1, source_target_pairs={{0,8},{4,12},{8,0},{12,4},{16,24},{20,28},{24,16},{28,20},{1,9},{5... | collective-permute-start | bytes 1204232 | tf_op jit(solution)/shard_map/ppermute | solution.py:596
  89.5 17.0 %collective-permute-start.13 = (bf16[192,768]{1,0:T(8,128)(2,1)S(1)}, bf16[192,768]{1,0:T(8,128)(2,1)S(1)}, u32[]{:S(2)}, u32[]{:S(2)}) collective-permute-start(bf16[192,768]{1,0:T(8,128)(2,1)S(1)} %add_convert_fusion.5), channel_id=1, source_target_pairs={{0,24},{4,28},{8,16},{12,20},{16,8},{20,12},{24,0},{28,4},{1,25},{... | collective-permute-start | bytes 884744 | tf_op jit(solution)/shard_map/ppermute | solution.py:602
  93.4 32.1 %collective-permute-start.21 = (bf16[112,896]{1,0:T(8,128)(2,1)S(1)}, bf16[112,896]{1,0:T(8,128)(2,1)S(1)}, u32[]{:S(2)}, u32[]{:S(2)}) collective-permute-start(bf16[112,896]{1,0:T(8,128)(2,1)S(1)} %collective-permute-done.9.refs_1_), channel_id=1, source_target_pairs={{0,2},{1,3},{2,0},{3,1},{4,6},{5,7},{6,4},{7,5},{8,10},{9,11},{10,... | collective-permute-start | bytes 602120 | tf_op jit(solution)/shard_map/ppermute | solution.py:532
  103.9 12.2 %collective-permute-start.24 = (bf16[192,768]{1,0:T(8,128)(2,1)S(1)}, bf16[192,768]{1,0:T(8,128)(2,1)S(1)}, u32[]{:S(2)}, u32[]{:S(2)}) collective-permute-start(bf16[192,768]{1,0:T(8,128)(2,1)S(1)} %add_convert_fusion.3.refs_0_), channel_id=1, source_target_pairs={{0,1},{1,0},{2,3},{3,2},{4,5},{5,4},{6,7},{7,6},{8,9},{9,8},{10,11... | collective-permute-start | bytes 884744 | tf_op jit(solution)/shard_map/ppermute | solution.py:532
  105.4 10.7 %collective-permute-start.25 = (bf16[192,768]{1,0:T(8,128)(2,1)S(1)}, bf16[192,768]{1,0:T(8,128)(2,1)S(1)}, u32[]{:S(2)}, u32[]{:S(2)}) collective-permute-start(bf16[192,768]{1,0:T(8,128)(2,1)S(1)} %add_convert_fusion.3.refs_0_), channel_id=1, source_target_pairs={{0,2},{1,3},{2,0},{3,1},{4,6},{5,7},{6,4},{7,5},{8,10},{9,11},{10,... | collective-permute-start | bytes 884744 | tf_op jit(solution)/shard_map/ppermute | solution.py:532
  105.9 14.5 %collective-permute-start.23 = (bf16[320,640]{1,0:T(8,128)(2,1)S(1)}, bf16[320,640]{1,0:T(8,128)(2,1)S(1)}, u32[]{:S(2)}, u32[]{:S(2)}) collective-permute-start(bf16[320,640]{1,0:T(8,128)(2,1)S(1)} %collective-permute-done.20.refs_2_), channel_id=1, source_target_pairs={{0,1},{1,0},{2,3},{3,2},{4,5},{5,4},{6,7},{7,6},{8,9},{9,8},{10,11... | collective-permute-start | bytes 1228808 | tf_op jit(solution)/shard_map/ppermute | solution.py:532
  122.0 21.8 %collective-permute-start.30 = (bf16[192,768]{1,0:T(8,128)(2,1)S(1)}, bf16[192,768]{1,0:T(8,128)(2,1)S(1)}, u32[]{:S(2)}, u32[]{:S(2)}) collective-permute-start(bf16[192,768]{1,0:T(8,128)(2,1)S(1)} %add_convert_fusion.2.refs_4_), channel_id=1, source_target_pairs={{0,1},{1,0},{2,3},{3,2},{4,5},{5,4},{6,7},{7,6},{8,9},{9,8},{10,11... | collective-permute-start | bytes 884744 | tf_op jit(solution)/shard_map/ppermute | solution.py:532
  122.5 21.3 %collective-permute-start.32 = (bf16[192,768]{1,0:T(8,128)(2,1)S(1)}, bf16[192,768]{1,0:T(8,128)(2,1)S(1)}, u32[]{:S(2)}, u32[]{:S(2)}) collective-permute-start(bf16[192,768]{1,0:T(8,128)(2,1)S(1)} %collective-permute-done.31.refs_6_), channel_id=1, source_target_pairs={{0,1},{1,0},{2,3},{3,2},{4,5},{5,4},{6,7},{7,6},{8,9},{9,8},{10,11... | collective-permute-start | bytes 884744 | tf_op jit(solution)/shard_map/ppermute | solution.py:532
  124.0 19.8 %collective-permute-start.29 = (bf16[192,768]{1,0:T(8,128)(2,1)S(1)}, bf16[192,768]{1,0:T(8,128)(2,1)S(1)}, u32[]{:S(2)}, u32[]{:S(2)}) collective-permute-start(bf16[192,768]{1,0:T(8,128)(2,1)S(1)} %collective-permute-done.24.refs_1_), channel_id=1, source_target_pairs={{0,2},{1,3},{2,0},{3,1},{4,6},{5,7},{6,4},{7,5},{8,10},{9,11},{10,... | collective-permute-start | bytes 884744 | tf_op jit(solution)/shard_map/ppermute | solution.py:532
  128.4 13.7 %collective-permute-start.28 = (bf16[112,896]{1,0:T(8,128)(2,1)S(1)}, bf16[112,896]{1,0:T(8,128)(2,1)S(1)}, u32[]{:S(2)}, u32[]{:S(2)}) collective-permute-start(bf16[112,896]{1,0:T(8,128)(2,1)S(1)} %add_convert_fusion.6.refs_4_), channel_id=1, source_target_pairs={{0,3},{1,2},{2,1},{3,0},{4,7},{5,6},{6,5},{7,4},{8,11},{9,10},{10,... | collective-permute-start | bytes 602120 | tf_op jit(solution)/shard_map/ppermute | solution.py:532
  (23 other events, 214.4 us)

commit v2 on v1

--- a/solution.py
+++ b/solution.py
@@ -182,26 +182,53 @@
 BAND = 16
 
 
-def packed_rows(own, wigner_rows, slab_rows):
+def packed_rows(own, wigner_rows):
     rotations = COEFFS * own
     targets = rotations + BAND * -(-wigner_rows // BAND)
-    slab = targets + BAND
-    return rotations, targets, slab, slab + slab_rows
+    return rotations, targets, targets + BAND
+
+
+def live_targets(count_ref, targets_ref):
+    targets = targets_ref[...]
+    live = lax.broadcasted_iota(jnp.int32, targets.shape, 1) < count_ref[0, 0]
+    return jnp.where(live, targets, -1)
+
+
+def pack_kernel(count_ref, grad_ref, targets_ref, wigner_ref, out_ref):
+    own = grad_ref.shape[0]
+    wig_rows, edges = wigner_ref.shape
+    rotations_at, targets_at, end = packed_rows(own, wig_rows)
+    for n in range(COEFFS):
+        out_ref[n * own : (n + 1) * own, :] = grad_ref[:, n * CHANNELS : (n + 1) * CHANNELS]
+    padding = jnp.zeros((targets_at - rotations_at - wig_rows, edges), jnp.float32)
+    rotations = jnp.concatenate([wigner_ref[...].astype(jnp.float32), padding], 0)
+    out_ref[rotations_at:targets_at, :] = rotations.astype(jnp.bfloat16)
+    marks = live_targets(count_ref, targets_ref).astype(jnp.float32)
+    out_ref[targets_at:end, :] = jnp.broadcast_to(marks, (BAND, edges)).astype(jnp.bfloat16)
+
+
+def pack_inputs(count, grad_out, targets, wigner):
+    rows = packed_rows(grad_out.shape[0], wigner.shape[0])[-1]
+    return pl.pallas_call(
+        pack_kernel,
+        in_specs=[SMEM] + [VMEM] * 3,
+        out_specs=VMEM,
+        out_shape=jax.ShapeDtypeStruct((rows, wigner.shape[1]), jnp.bfloat16),
+        compiler_params=PARAMS,
+        name="pack_inputs",
+    )(count, grad_out, targets, wigner)
 
 
 def enter_kernel(
     place_ref, count_ref, features_ref, ghosts_ref, grad_ref, sources_ref, targets_ref, wigner_ref,
-    frame_ref, back_ref, slab_ref, *rest,
+    frame_ref, back_ref, *rest,
 ):
-    packs, (wide, forward, backward, turned, turned_back) = rest[:-5], rest[-5:]
+    slabs, (wide, forward, backward, turned, turned_back) = rest[:-5], rest[-5:]
     own = features_ref.shape[0]
-    edges = sources_ref.shape[1]
     extra = ghosts_ref.shape[0]
-    wig_rows = wigner_ref.shape[0]
     wide[...] = wigner_ref[...].astype(jnp.float32)
     sources = sources_ref[...]
-    live = lax.broadcasted_iota(jnp.int32, (1, edges), 1) < count_ref[0, 0]
-    targets = jnp.where(live, targets_ref[...], -1)
+    targets = live_targets(count_ref, targets_ref)
     from_own = hot_rows(sources, own)
     from_ghost = hot_rows(sources, extra, start=own)
     to_own = hot_rows(targets, own, MESSAGE_SCALE)
@@ -217,39 +244,27 @@
         span = pl.ds(k * CHANNELS, CHANNELS)
         frame_ref[:, span] = dot(eye, turned[span, :], NT).astype(jnp.bfloat16)
         back_ref[:, span] = dot(eye, turned_back[span, :], NT).astype(jnp.bfloat16)
-    spaces = len(packs) + 1
-    rotations_at, targets_at, slab_at, _ = packed_rows(own, wig_rows, slab_ref.shape[0])
-    for peer in range(spaces):
+    spaces = len(slabs)
+    for peer, slab in enumerate(slabs):
         position = lax.bitwise_xor(place_ref[1], jnp.int32(peer))
-        out, at = (slab_ref, 0) if peer == 0 else (packs[peer - 1], slab_at)
-        first = 0
+        at = first = 0
         for blocks in BLOCK_COUNTS:
             rows = blocks * CHANNELS // spaces
             begin = pl.multiple_of(first + position * rows, BAND)
-            out[at : at + rows, :] = turned[pl.ds(begin, rows), :]
+            slab[at : at + rows, :] = turned[pl.ds(begin, rows), :]
             at += rows
             first += blocks * CHANNELS
-    padding = jnp.zeros((targets_at - rotations_at - wig_rows, edges), jnp.float32)
-    rotations = jnp.concatenate([wide[...], padding], 0).astype(jnp.bfloat16)
-    marks = jnp.broadcast_to(targets.astype(jnp.float32), (BAND, edges)).astype(jnp.bfloat16)
-    for pack in packs:
-        for n in range(COEFFS):
-            pack[n * own : (n + 1) * own, :] = grad_ref[:, n * CHANNELS : (n + 1) * CHANNELS]
-        pack[rotations_at:targets_at, :] = rotations
-        pack[targets_at:slab_at, :] = marks
 
 
 def enter(place, count, features, ghosts, grad_out, sources, targets, wigner, spaces):
     edges = sources.shape[1]
     frame = jax.ShapeDtypeStruct((edges, FRAME_W), jnp.bfloat16)
     slab = jax.ShapeDtypeStruct((FRAME_W // spaces, edges), jnp.bfloat16)
-    pack_rows = packed_rows(features.shape[0], wigner.shape[0], FRAME_W // spaces)[-1]
-    pack = jax.ShapeDtypeStruct((pack_rows, edges), jnp.bfloat16)
     return pl.pallas_call(
         enter_kernel,
         in_specs=[SMEM, SMEM] + [VMEM] * 6,
         out_specs=[VMEM] * (2 + spaces),
-        out_shape=[frame, frame, slab] + [pack] * (spaces - 1),
+        out_shape=[frame, frame] + [slab] * spaces,
         scratch_shapes=[
             pltpu.VMEM((wigner.shape[0], edges), jnp.float32),
             pltpu.VMEM((NODE_W, edges), jnp.float32),
@@ -262,13 +277,13 @@
     )(place, count, features, ghosts, grad_out, sources, targets, wigner)
 
 
-def peer_frames_kernel(own, wig_rows, slab_rows, *refs):
+def peer_frames_kernel(own, wig_rows, *refs):
     packs, (out, wide, backward, turned_back) = refs[:-4], refs[-4:]
-    rotations_at, targets_at, slab_at, _ = packed_rows(own, wig_rows, slab_rows)
+    rotations_at, targets_at, end = packed_rows(own, wig_rows)
     eye = identity()
     for peer, pack in enumerate(packs):
         wide[...] = pack[rotations_at:targets_at, :].astype(jnp.float32)
-        targets = pack[targets_at:slab_at, :].astype(jnp.float32)[:1].astype(jnp.int32)
+        targets = pack[targets_at:end, :].astype(jnp.float32)[:1].astype(jnp.int32)
         to_own = hot_rows(targets, own, MESSAGE_SCALE)
         for n in range(COEFFS):
             backward[n * CHANNELS : (n + 1) * CHANNELS, :] = dot(
@@ -280,10 +295,10 @@
             out[peer, :, span] = dot(eye, turned_back[span, :], NT).astype(jnp.bfloat16)
 
 
-def peer_frames(packs, own, wig_rows, slab_rows):
+def peer_frames(packs, own, wig_rows):
     edges = packs[0].shape[1]
     return pl.pallas_call(
-        functools.partial(peer_frames_kernel, own, wig_rows, slab_rows),
+        functools.partial(peer_frames_kernel, own, wig_rows),
         in_specs=[VMEM] * len(packs),
         out_specs=VMEM,
         out_shape=jax.ShapeDtypeStruct((len(packs), edges, FRAME_W), jnp.bfloat16),
@@ -297,11 +312,9 @@
     )(*packs)
 
 
-def weight_grad_kernel(scale, slab_ref, back_ref, backs, *refs):
-    packs, (out_zero, out_one, out_two) = refs[:-3], refs[-3:]
-    spaces = len(packs) + 1
-    end = packs[0].shape[0]
-    all_slabs = [slab_ref] + [pack.at[end - slab_ref.shape[0] : end] for pack in packs]
+def weight_grad_kernel(scale, back_ref, backs, *refs):
+    all_slabs, (out_zero, out_one, out_two) = refs[:-3], refs[-3:]
+    spaces = len(all_slabs)
     all_backs = [back_ref] + [backs.at[k] for k in range(spaces - 1)]
     rows = [blocks * CHANNELS // spaces for blocks in BLOCK_COUNTS]
     widths = [blocks * CHANNELS for blocks in BLOCK_COUNTS]
@@ -317,8 +330,8 @@
         out[1] = (scale * (product(group, group + 1) - product(group + 1, group))).astype(jnp.bfloat16)
 
 
-def weight_grads(slab, back, backs, packs, scale):
-    spaces = len(packs) + 1
+def weight_grads(back, backs, slabs, scale):
+    spaces = len(slabs)
     k0, k1, _, k2, _ = [blocks * CHANNELS for blocks in BLOCK_COUNTS]
     return pl.pallas_call(
         functools.partial(weight_grad_kernel, scale),
@@ -331,18 +344,26 @@
         ],
         compiler_params=PARAMS,
         name="weight_grads",
-    )(slab, back, backs, *packs)
+    )(back, backs, *slabs)
 
 
 def apply_kernel(group, places, local_rows, place_ref, frame_ref, back_ref, *refs):
     shards, (out_ref, grad_ref, full) = refs[:-3], refs[-3:]
     parts = 1 if group == 0 else 2
-    for (peer, first_part, count, offset), shard in zip(places, shards):
+    for (peer, first_part, count, offset, rows, at), shard in zip(places, shards):
         position = lax.bitwise_xor(place_ref[1], jnp.int32(peer))
-        rows = shard.shape[0] // count
         begin = pl.multiple_of(position * local_rows + offset, 16)
         for k in range(count):
-            full[first_part + k, pl.ds(begin, rows), :] = shard[k * rows : (k + 1) * rows, :]
+            if at is None:
+                full[first_part + k, pl.ds(begin, rows), :] = shard[k * rows : (k + 1) * rows, :]
+                continue
+            for column in range(BLOCK_COUNTS[group]):
+                full[
+                    first_part + k,
+                    pl.ds(begin, rows),
+                    column * CHANNELS : (column + 1) * CHANNELS,
+                ] = shard[at : at + rows, :]
+                at += rows
     first = sum(BLOCK_COUNTS[:group]) * CHANNELS
     width = BLOCK_COUNTS[group] * CHANNELS
     eye = identity()
@@ -387,6 +408,34 @@
         compiler_params=PARAMS,
         name=f"apply_weights_{group}",
     )(place, frame, back, *shards)
+
+
+def finish_kernel(*refs):
+    out = refs[-1]
+    at = 0
+    for here, beside, opposite in zip(refs[:-1:3], refs[1:-1:3], refs[2:-1:3]):
+        rows, width = here.shape
+        step = rows if rows < 160 else rows // 2
+        for first in range(0, rows, step):
+            span = slice(first, first + step)
+            for column in range(0, width, CHANNELS):
+                lanes = slice(column, column + CHANNELS)
+                total = sum(r[span, lanes].astype(jnp.float32) for r in (here, beside, opposite))
+                out[at : at + step, :] = total.astype(jnp.bfloat16)
+                at += step
+
+
+def finish(*chunks):
+    arrays = [array for chunk in chunks for array in chunk]
+    rows = sum(here.size // CHANNELS for here, _, _ in chunks)
+    return pl.pallas_call(
+        finish_kernel,
+        in_specs=[VMEM] * len(arrays),
+        out_specs=VMEM,
+        out_shape=jax.ShapeDtypeStruct((rows, CHANNELS), jnp.bfloat16),
+        compiler_params=PARAMS,
+        name="finish_first",
+    )(*arrays)
 
 
 def leave(frames, wigner_ref, wide, turned):
@@ -608,11 +657,15 @@
             return to_peer(shard, spaces, 1), to_peer(shard, spaces, 2)
 
         def forward(j, sides):
-            along = 2 - j % 2
+            along = 1 if j == 1 else 2
             return to_peer(sides[(3 ^ along) - 1], spaces, along)
 
-        def pieces(j, shard, sides, last):
-            return [((k,) + chunks[j][4], a) for k, a in enumerate((shard, *sides, last))]
+        def pieces(j, shard, sides, last, at=None):
+            _, _, _, rows, (part, parts, offset) = chunks[j]
+            return [
+                ((k, part, parts, offset, rows // parts, at), a)
+                for k, a in enumerate((shard, *sides, last))
+            ]
 
         other0 = swap_cores(w_zero)
         other0, to_next, to_prev = together(other0, to_next, to_prev)
@@ -622,6 +675,8 @@
         from_next = lax.ppermute(to_prev, "space", down)
         sent, other0 = together(w_two, other0)
         other1 = swap_cores(sent)
+        raw = pack_inputs(edge_count, grad_out, targets, wigner)
+        raws = [to_peer(raw, spaces, 1), to_peer(raw, spaces, 2)]
         both1, across1, here1 = mix_chunk(1, other1)
         beside1 = swap_beside(both1)
         beside0, here1, from_prev, from_next = together(beside0, here1, from_prev, from_next)
@@ -630,77 +685,85 @@
         sent, other1, here1 = together(w_one, other1, here1)
         other2 = swap_cores(sent)
         total0, from_prev, from_next = together(total0, from_prev, from_next)
-        frame, back, slab, *packs = frames(from_prev, from_next)
-        opposite0, frame = together(opposite0, frame)
-        shard0 = total_here(0, here0, beside0, opposite0)
-        shard0, packs[0], packs[1], other2 = together(shard0, packs[0], packs[1], other2)
-        sides0 = to_sides(shard0)
-        side_packs = [to_peer(packs[0], spaces, 1), to_peer(packs[1], spaces, 2)]
+        frame, back, *slabs = frames(from_prev, from_next)
+        slabs[1], slabs[2], other2, opposite0 = together(slabs[1], slabs[2], other2, opposite0)
+        slabs[1], slabs[2] = to_peer(slabs[1], spaces, 1), to_peer(slabs[2], spaces, 2)
+        raw, frame, *raws = together(raw, frame, *raws)
+        raws.append(to_peer(raw, spaces, 3))
         other2, frame = together(other2, frame)
         both2, across2, here2 = mix_chunk(2, other2)
         beside2 = swap_beside(both2)
         both3, across3, here3 = mix_chunk(3, other2, rows_one)
-        beside1, here2, here3, *sides0 = together(beside1, here2, here3, *sides0)
+        here3, raws[2] = together(here3, raws[2])
+        backs = peer_frames(raws, own_rows, wigner.shape[0])
+        beside1, here2, here3, backs = together(beside1, here2, here3, backs)
         total1 = total_opposite(1, across1, beside1)
         opposite1 = swap_opposite(total1)
-        both3, beside2, here3 = together(both3, beside2, here3)
+        other0, beside1 = together(other0, beside1)
+        both4, across4, here4 = mix_chunk(4, other0, half)
+        both3, beside2, here4 = together(both3, beside2, here4)
         beside3 = swap_beside(both3)
         total2 = total_opposite(2, across2, beside2)
         opposite2 = swap_opposite(total2)
-        last_pack, total2, *side_packs = together(packs[2], total2, *side_packs)
-        last_pack = to_peer(last_pack, spaces, 3)
-        other0, total2 = together(other0, total2)
-        both4, across4, here4 = mix_chunk(4, other0, half)
-        opposite1, here4 = together(opposite1, here4)
-        shard1 = total_here(1, here1, beside1, opposite1)
-        shard1, *sides0 = together(shard1, *sides0)
+        beside2, *slabs[1:] = together(beside2, *slabs[1:])
+        slabs[3] = to_peer(slabs[3], spaces, 3)
+        opposite1, beside2 = together(opposite1, beside2)
+        shard1 = finish((here0, beside0, opposite0), (here1, beside1, opposite1))
         sides1 = to_sides(shard1)
-        forward0 = forward(0, sides0)
-        both4, beside3, here4, shard1 = together(both4, beside3, here4, shard1)
+        both4, beside3, shard1 = together(both4, beside3, shard1)
         beside4 = swap_beside(both4)
         total3 = total_opposite(3, across3, beside3)
         opposite3 = swap_opposite(total3)
-        opposite2, total3 = together(opposite2, total3)
         shard2 = total_here(2, here2, beside2, opposite2)
-        last_pack, shard2 = together(last_pack, shard2)
-        packs_in = [*side_packs, last_pack]
-        backs = peer_frames(packs_in, own_rows, wigner.shape[0], slab.shape[0])
+        shard2, *sides1 = together(shard2, *sides1)
+        forward1 = forward(1, sides1)
         sides2 = to_sides(shard2)
-        beside4, backs, *sides1 = together(beside4, backs, *sides1)
-        forward1 = forward(1, sides1)
+        beside4, shard2, slabs[3] = together(beside4, shard2, slabs[3])
         total4 = total_opposite(4, across4, beside4)
         opposite4 = swap_opposite(total4)
         opposite3, total4 = together(opposite3, total4)
         shard3 = total_here(3, here3, beside3, opposite3)
         sides3 = to_sides(shard3)
-        back, shard3 = together(back, shard3)
-        grad_mix = weight_grads(slab, back, backs, packs_in, scale)
-        opposite4, *grad_mix = together(opposite4, *grad_mix)
-        opposite4, forward1, *sides2 = together(opposite4, forward1, *sides2)
+        opposite4, *sides2 = together(opposite4, *sides2)
+        shard4 = total_here(4, here4, beside4, opposite4)
+        late_back, shard4, slabs[3] = together(back, shard4, slabs[3])
+        grad_mix = weight_grads(late_back, backs, slabs, scale)
+        sides4 = to_sides(shard4)
         forward2 = forward(2, sides2)
         shard4 = total_here(4, here4, beside4, opposite4)
+        late_back, shard4, slabs[3] = together(back, shard4, slabs[3])
+        grad_mix = weight_grads(late_back, backs, slabs, scale)
         sides4 = to_sides(shard4)
         outs, grads = {}, {}
         whole = {
-            3: pieces(1, shard1, sides1, forward1),
+            3: pieces(1, shard1, sides1, forward1, half * BLOCK_COUNTS[0]),
             1: pieces(2, shard2, sides2, forward2) + pieces(3, shard3, sides3, forward(3, sides3)),
-            0: pieces(0, shard0, sides0, forward0) + pieces(4, shard4, sides4, to_peer(shard4, spaces, 3)),
+            0: pieces(0, shard1, sides1, forward1, 0) + pieces(4, shard4, sides4, to_peer(shard4, spaces, 3)),
         }
     else:
         from_prev = lax.ppermute(to_next, "space", up)
         from_next = lax.ppermute(to_prev, "space", down)
-        frame, back, slab, *packs = frames(from_prev, from_next)
-        packs_in = [to_peer(pack, spaces, k + 1) for k, pack in enumerate(packs)]
-        backs = peer_frames(packs_in, own_rows, wigner.shape[0], slab.shape[0])
-        grad_mix = weight_grads(slab, back, backs, packs_in, scale)
+        frame, back, *slabs = frames(from_prev, from_next)
+        slabs = [slabs[0]] + [to_peer(slabs[k], spaces, k) for k in range(1, spaces)]
+        raw = pack_inputs(edge_count, grad_out, targets, wigner)
+        raws = [to_peer(raw, spaces, k) for k in range(1, spaces)]
+        backs = peer_frames(raws, own_rows, wigner.shape[0])
+        grad_mix = weight_grads(back, backs, slabs, scale)
         outs, grads, whole = {}, {}, {}
         for group, own, parts in ((3, w_two, 2), (1, w_one, 2), (0, w_zero, 1)):
             shard = mixed_general(mixture, own)
-            whole[group] = [((0, 0, parts, 0), shard)] + [
-                ((k, 0, parts, 0), to_peer(shard, spaces, k)) for k in range(1, spaces)
+            rows = shard.shape[0] // parts
+
+            def place_of(k):
+                return (k, 0, parts, 0, rows, None)
+
+            whole[group] = [(place_of(0), shard)] + [
+                (place_of(k), to_peer(shard, spaces, k)) for k in range(1, spaces)
             ]
 
     for group, pieces_of in whole.items():
+        if group == 0:
+            frame, grads[1], *grad_mix = together(frame, grads[1], *grad_mix)
         outs[group], grads[group] = apply_weights(group, place, frame, back, pieces_of, spaces)
     base, returning = leave_back(
         [grads[g] for g in (0, 1, 3)], wigner, sources, grad_out, 2 * ghosts

time: 159 us -> 159 us (level)
  the two profiles are of different devices: /device:TPU:0 before, /device:TPU:10 now
where the time goes in v2:
time: 159 us
  waiting for transfers between devices  55.6 us (35%)
  starting transfers between devices  48.2 us (30%)
  Pallas kernels  47.2 us (30%)
  local copies, waits for them, and re-layouts  3.11 us (2%)
  other arithmetic  2.72 us (2%)
  between operations  1.67 us (1%)
    ppermute x5, waiting for transfers between devices, swap_opposite(): return lax.ppermute(total, 'dp', OPPOSITE)  23.9 us
    ppermute x18, starting transfers between devices, to_peer(): return lax.ppermute(array, 'space', [(i, i ^ k) for i in range(spaces)])  21.9 us
    ppermute x18, waiting for transfers between devices, to_peer(): return lax.ppermute(array, 'space', [(i, i ^ k) for i in range(spaces)])  21.9 us
    ppermute x5, starting transfers between devices, swap_beside(): return lax.ppermute(both, 'dp', BESIDE)  18.1 us
    pallas_call x5, Pallas kernels, mix(): pl.pallas_call(functools.partial(mix_kernel, offset, other_offset), in_sp...  17 us
    pallas_call x1, Pallas kernels, peer_frames(): pl.pallas_call(functools.partial(peer_frames_kernel, own, wig_rows), in_s...  7.19 us
    pallas_call x3, Pallas kernels, apply_weights(): pl.pallas_call(functools.partial(apply_kernel, group, places, width // sp...  6.67 us
    pallas_call x1, Pallas kernels, enter(): pl.pallas_call(enter_kernel, in_specs=[SMEM, SMEM] + [VMEM] * 6, out_spec...  5.34 us
  transfers between devices with their start and end apart: 35, of which 17 were waited for; matrix products, arithmetic and copies ran while one was open for 2% of the time, Pallas kernels for 26%

profile of v2, /device:TPU:10, one launch (start us, length us, event | category | flops | bytes accessed | tf_op | source)
XLA Modules:
  0.0 158.6 jit_solution(15813524140162004805)
XLA Ops:
  5.3 2.8 %mix.5 = (bf16[224,896]{1,0:T(8,128)(2,1)S(1)}, bf16[112,896]{1,0:T(8,128)(2,1)S(1)}, bf16[112,896]{1,0:T(8,128)(2,1)S(1)}) custom-call(s32[2]{0:T(128)S(1)} %pad_add_fusion.place_ref, f32[8,32]{1,0:T(8,128)S(1)} %copy-done.4, bf16[4,224,896]{2,1,0:T(8,128)(2,1)} %own_ref.3, bf16[4,224,896]{2,1,0:T(8,128)(2,1)S(1)} %collective-permute-done.other_ref), custom_call_target="tpu_custom_call" | custom-call | tf_op jit(solution)/shard_map/mix/pallas_call | solution.py:114
  10.7 4.9 %mix.6 = (bf16[640,640]{1,0:T(8,128)(2,1)}, bf16[320,640]{1,0:T(8,128)(2,1)S(1)}, bf16[320,640]{1,0:T(8,128)(2,1)S(1)}) custom-call(s32[2]{0:T(128)S(1)} %pad_add_fusion.place_ref, f32[8,32]{1,0:T(8,128)S(1)} %copy-done.4, bf16[4,320,640]{2,1,0:T(8,128)(2,1)} %bitcast.20, bf16[4,320,640]{2,1,0:T(8,128)(2,1)S(1)} %collective-permute-done.2.other_ref), custom_call_target="tpu_custom_call" | custom-call | tf_op jit(solution)/shard_map/mix/pallas_call | solution.py:114
  16.6 3.2 %collective-permute-done.1.refs_1_ = bf16[224,896]{1,0:T(8,128)(2,1)S(1)} collective-permute-done((bf16[224,896]{1,0:T(8,128)(2,1)S(1)}, bf16[224,896]{1,0:T(8,128)(2,1)S(1)}, u32[]{:S(2)}, u32[]{:S(2)}) %collective-permute-start.1) | collective-permute-done | bytes 401440 | tf_op jit(solution)/shard_map/ppermute | solution.py:645
  23.3 5.3 %enter_frame.1 = (bf16[128,3712]{1,0:T(8,128)(2,1)S(1)}, bf16[128,3712]{1,0:T(8,128)(2,1)S(1)}, bf16[928,128]{1,0:T(8,128)(2,1)S(1)}, bf16[928,128]{1,0:T(8,128)...) custom-call(s32[2]{0:T(128)S(1)} %pad_add_fusion.place_ref, s32[1,1]{1,0:T(1,128)S(6)} %copy.16.count_ref, ...), custom_call_target="tpu_custom_call" | custom-call | tf_op jit(solution)/shard_map/enter_frame/pallas_call | solution.py:263
  29.3 5.6 %collective-permute-done.8.refs_1_ = bf16[2048,128]{1,0:T(8,128)(2,1)S(1)} collective-permute-done((bf16[2048,128]{1,0:T(8,128)(2,1)S(1)}, bf16[2048,128]{1,0:T(8,128)(2,1)S(1)}, u32[]{:S(2)}, u32[]{:S(2)}) %collective-permute-start.8) | collective-permute-done | bytes 524320 | tf_op jit(solution)/shard_map/ppermute | solution.py:581
  38.2 4.5 %collective-permute-done.6.refs_2_ = bf16[112,896]{1,0:T(8,128)(2,1)S(1)} collective-permute-done((bf16[112,896]{1,0:T(8,128)(2,1)S(1)}, bf16[112,896]{1,0:T(8,128)(2,1)S(1)}, u32[]{:S(2)}, u32[]{:S(2)}) %collective-permute-start.6) | collective-permute-done | bytes 200736 | tf_op jit(solution)/shard_map/ppermute | solution.py:651
  42.8 3.2 %mix.7 = (bf16[384,768]{1,0:T(8,128)(2,1)S(1)}, bf16[192,768]{1,0:T(8,128)(2,1)S(1)}, bf16[192,768]{1,0:T(8,128)(2,1)S(1)}) custom-call(s32[2]{0:T(128)S(1)} %pad_add_fusion.place_ref, f32[8,32]{1,0:T(8,128)S(1)} %copy-done.4, bf16[4,384,768]{2,1,0:T(8,128)(2,1)} %bitcast.17, bf16[4,384,768]{2,1,0:T(8,128)(2,1)S(1)} %collective-permute-done.5.other_ref), custom_call_target="tpu_custom_call" | custom-call | tf_op jit(solution)/shard_map/mix/pallas_call | solution.py:114
  46.0 7.2 %collective-permute-start.11 = (bf16[384,768]{1,0:T(8,128)(2,1)S(1)}, bf16[384,768]{1,0:T(8,128)(2,1)}, u32[]{:S(2)}, u32[]{:S(2)}) collective-permute-start(bf16[384,768]{1,0:T(8,128)(2,1)S(1)} %get-tuple-element.138), channel_id=1, source_target_pairs={{0,8},{4,12},{8,0},{12,4},{16,24},{20,28},{24,16},{28,20},{1,9},{5... | collective-permute-start | bytes 1769480 | tf_op jit(solution)/shard_map/ppermute | solution.py:645
  53.2 3.2 %mix.8 = (bf16[384,768]{1,0:T(8,128)(2,1)S(1)}, bf16[192,768]{1,0:T(8,128)(2,1)S(1)}, bf16[192,768]{1,0:T(8,128)(2,1)S(1)}) custom-call(s32[2]{0:T(128)S(1)} %pad_add_fusion.place_ref, f32[8,32]{1,0:T(8,128)S(1)} %copy-done.4, bf16[4,384,768]{2,1,0:T(8,128)(2,1)} %bitcast.18, bf16[4,384,768]{2,1,0:T(8,128)(2,1)S(1)} %collective-permute-done.5.other_ref), custom_call_target="tpu_custom_call" | custom-call | tf_op jit(solution)/shard_map/mix/pallas_call | solution.py:114
  56.4 7.2 %peer_frames.1.backs = bf16[3,128,3712]{2,1,0:T(8,128)(2,1)S(1)} custom-call(bf16[2048,128]{1,0:T(8,128)(2,1)S(1)} %collective-permute-done.7.refs_0_, bf16[2048,128]{1,0:T(8,128)(2,1)S(1)} %collective-permute-done.8.refs_1_, bf16[2048,128]{1,0:T(8,128)(2,1)S(1)} %collective-permute-done.10.refs_2_), custom_call_target="tpu_custom_call" | custom-call | tf_op jit(solution)/shard_map/peer_frames/pallas_call | solution.py:300
  64.3 3.0 %mix.9 = (bf16[224,896]{1,0:T(8,128)(2,1)S(1)}, bf16[112,896]{1,0:T(8,128)(2,1)S(1)}, bf16[112,896]{1,0:T(8,128)(2,1)S(1)}) custom-call(s32[2]{0:T(128)S(1)} %pad_add_fusion.place_ref, f32[8,32]{1,0:T(8,128)S(1)} %copy-done.4, bf16[4,224,896]{2,1,0:T(8,128)(2,1)} %own_ref.3, bf16[4,224,896]{2,1,0:T(8,128)(2,1)S(1)} %collective-permute-done.other_ref), custom_call_target="tpu_custom_call" | custom-call | tf_op jit(solution)/shard_map/mix/pallas_call | solution.py:114
  67.3 7.3 %collective-permute-start.12 = (bf16[384,768]{1,0:T(8,128)(2,1)S(1)}, bf16[384,768]{1,0:T(8,128)(2,1)S(1)}, u32[]{:S(2)}, u32[]{:S(2)}) collective-permute-start(bf16[384,768]{1,0:T(8,128)(2,1)S(1)} %get-tuple-element.140), channel_id=1, source_target_pairs={{0,8},{4,12},{8,0},{12,4},{16,24},{20,28},{24,16},{28,20},{1,9},{5... | collective-permute-start | bytes 1769480 | tf_op jit(solution)/shard_map/ppermute | solution.py:645
  76.6 4.1 %collective-permute-done.14.refs_1_ = bf16[928,128]{1,0:T(8,128)(2,1)S(1)} collective-permute-done((bf16[928,128]{1,0:T(8,128)(2,1)S(1)}, bf16[928,128]{1,0:T(8,128)(2,1)S(1)}, u32[]{:S(2)}, u32[]{:S(2)}) %collective-permute-start.14) | collective-permute-done | bytes 237600 | tf_op jit(solution)/shard_map/ppermute | solution.py:581
  89.9 2.6 %collective-permute-start.16 = (bf16[224,896]{1,0:T(8,128)(2,1)S(1)}, bf16[224,896]{1,0:T(8,128)(2,1)S(1)}, u32[]{:S(2)}, u32[]{:S(2)}) collective-permute-start(bf16[224,896]{1,0:T(8,128)(2,1)S(1)} %get-tuple-element.152), channel_id=1, source_target_pairs={{0,8},{4,12},{8,0},{12,4},{16,24},{20,28},{24,16},{28,20},{1,9},{5... | collective-permute-start | bytes 1204232 | tf_op jit(solution)/shard_map/ppermute | solution.py:645
  92.6 6.5 %collective-permute-done.17 = bf16[192,768]{1,0:T(8,128)(2,1)S(1)} collective-permute-done((bf16[192,768]{1,0:T(8,128)(2,1)S(1)}, bf16[192,768]{1,0:T(8,128)(2,1)S(1)}, u32[]{:S(2)}, u32[]{:S(2)}) %collective-permute-start.17) | collective-permute-done | bytes 294944 | tf_op jit(solution)/shard_map/ppermute | solution.py:651
  107.3 8.1 %collective-permute-done.25 = bf16[192,768]{1,0:T(8,128)(2,1)S(1)} collective-permute-done((bf16[192,768]{1,0:T(8,128)(2,1)S(1)}, bf16[192,768]{1,0:T(8,128)(2,1)S(1)}, u32[]{:S(2)}, u32[]{:S(2)}) %collective-permute-start.25) | collective-permute-done | bytes 294944 | tf_op jit(solution)/shard_map/ppermute | solution.py:651
  118.1 4.2 %collective-permute-done.21 = bf16[112,896]{1,0:T(8,128)(2,1)S(1)} collective-permute-done((bf16[112,896]{1,0:T(8,128)(2,1)S(1)}, bf16[112,896]{1,0:T(8,128)(2,1)S(1)}, u32[]{:S(2)}, u32[]{:S(2)}) %collective-permute-start.21) | collective-permute-done | bytes 200736 | tf_op jit(solution)/shard_map/ppermute | solution.py:651
  124.1 4.9 %collective-permute-done.26.refs_5_ = bf16[192,768]{1,0:T(8,128)(2,1)S(1)} collective-permute-done((bf16[192,768]{1,0:T(8,128)(2,1)S(1)}, bf16[192,768]{1,0:T(8,128)(2,1)S(1)}, u32[]{:S(2)}, u32[]{:S(2)}) %collective-permute-start.26) | collective-permute-done | bytes 294944 | tf_op jit(solution)/shard_map/ppermute | solution.py:581
  134.3 3.4 %weight_grads.1 = (bf16[224,896]{1,0:T(8,128)(2,1)}, bf16[2,192,768]{2,1,0:T(8,128)(2,1)}, bf16[2,160,640]{2,1,0:T(8,128)(2,1)}) custom-call(bf16[128,3712]{1,0:T(8,128)(2,1)S(1)} %get-tuple-element.172.back_ref, bf16[3,128,3712]{2,1,0:T(8,128)(2,1)S(1)} %peer_frames.1.backs, bf16[928,128]{1,0:T(8,128)(2,1)S(1)} %get-tuple-element.174.refs_0_, ...), custom_call_target="tpu_custom_call" | custom-call | tf_op jit(solution)/shard_map/weight_grads/pallas_call | solution.py:336
  140.0 2.8 %collective-permute-done.28.refs_7_ = bf16[192,768]{1,0:T(8,128)(2,1)S(1)} collective-permute-done((bf16[192,768]{1,0:T(8,128)(2,1)S(1)}, bf16[192,768]{1,0:T(8,128)(2,1)S(1)}, u32[]{:S(2)}, u32[]{:S(2)}) %collective-permute-start.28) | collective-permute-done | bytes 294944 | tf_op jit(solution)/shard_map/ppermute | solution.py:581
  142.8 2.7 %apply_weights_1.1 = (bf16[1536,128]{1,0:T(8,128)(2,1)S(1)}, bf16[1536,128]{1,0:T(8,128)(2,1)S(1)}) custom-call(s32[2]{0:T(128)S(1)} %pad_add_fusion.place_ref, bf16[128,3712]{1,0:T(8,128)(2,1)S(1)} %get-tuple-element.181.frame_ref, bf16[128,3712]{1,0:T(8,128)(2,1)S(1)} %get-tuple-element.172.back_ref, bf16[192,768]{1,0:T(8,128)(2,1)S(1)} %add_convert_fusion.3.refs_0_, ...), custom_call_target="tpu_custom_call" | custom-call | tf_op jit(solution)/shard_map/apply_weights_1/pallas_call | solution.py:402
  147.2 2.4 %leave_frame_back.1 = (f32[32,6272]{1,0:T(8,128)S(1)}, bf16[16,6272]{1,0:T(8,128)(2,1)S(1)}) custom-call(bf16[896,128]{1,0:T(8,128)(2,1)S(1)} %get-tuple-element.189.zero_ref, bf16[1536,128]{1,0:T(8,128)(2,1)S(1)} %get-tuple-element.190.one_ref, bf16[1280,128]{1,0:T(8,128)(2,1)S(1)} %get-tuple-element.191.two_ref, bf16[455,128]{1,0:T(8,128)(2,1)S(1)} %copy-done.3, ...), custom_call_target="tpu_custom_call" | custom-call | tf_op jit(solution)/shard_map/leave_frame_back/pallas_call | solution.py:510
  152.0 2.9 %leave_frame.1 = bf16[32,6272]{1,0:T(8,128)(2,1)} custom-call(bf16[896,128]{1,0:T(8,128)(2,1)S(1)} %get-tuple-element.186.zero_ref, bf16[1536,128]{1,0:T(8,128)(2,1)S(1)} %get-tuple-element.187.one_ref, bf16[1280,128]{1,0:T(8,128)(2,1)S(1)} %get-tuple-element.188.two_ref, bf16[455,128]{1,0:T(8,128)(2,1)S(1)} %copy-done.3, s32[1,1]{1,0:T(1,128)S(6)} %copy.16.count_ref, ...), custom_call_target="tpu_custom_call" | custom-call | tf_op jit(solution)/shard_map/leave_frame/pallas_call | solution.py:525
  154.9 2.6 %collective-permute-done.33.next_ref = bf16[8,6272]{1,0:T(8,128)(2,1)S(1)} collective-permute-done((bf16[8,6272]{1,0:T(8,128)(2,1)S(1)}, bf16[8,6272]{1,0:T(8,128)(2,1)S(1)}, u32[]{:S(2)}, u32[]{:S(2)}) %collective-permute-start.33) | collective-permute-done | bytes 100384 | tf_op jit(solution)/shard_map/ppermute | solution.py:771
  (100 shorter events, 52.3 us)
Async XLA Ops:
  19.7 23.0 %collective-permute-start.5 = (bf16[4,384,768]{2,1,0:T(8,128)(2,1)}, bf16[4,384,768]{2,1,0:T(8,128)(2,1)S(1)}, u32[]{:S(2)}, u32[]{:S(2)}) collective-permute-start(bf16[4,384,768]{2,1,0:T(8,128)(2,1)} %bitcast.16), channel_id=1, source_target_pairs={{0,4},{4,0},{8,12},{12,8},{16,20},{20,16},{24,28},{28,24},{1,5},{5... | collective-permute-start | bytes 7077896 | tf_op jit(solution)/shard_map/ppermute | solution.py:638
  20.5 14.4 %collective-permute-start.8 = (bf16[2048,128]{1,0:T(8,128)(2,1)S(1)}, bf16[2048,128]{1,0:T(8,128)(2,1)S(1)}, u32[]{:S(2)}, u32[]{:S(2)}) collective-permute-start(bf16[2048,128]{1,0:T(8,128)(2,1)S(1)} %pack_inputs.1), channel_id=1, source_target_pairs={{0,2},{1,3},{2,0},{3,1},{4,6},{5,7},{6,4},{7,5},{8,10},{9,11},{10,... | collective-permute-start | bytes 1572872 | tf_op jit(solution)/shard_map/ppermute | solution.py:581
  22.1 14.1 %collective-permute-start.7 = (bf16[2048,128]{1,0:T(8,128)(2,1)S(1)}, bf16[2048,128]{1,0:T(8,128)(2,1)S(1)}, u32[]{:S(2)}, u32[]{:S(2)}) collective-permute-start(bf16[2048,128]{1,0:T(8,128)(2,1)S(1)} %pack_inputs.1), channel_id=1, source_target_pairs={{0,1},{1,0},{2,3},{3,2},{4,5},{5,4},{6,7},{7,6},{8,9},{9,8},{10,11... | collective-permute-start | bytes 1572872 | tf_op jit(solution)/shard_map/ppermute | solution.py:581
  22.7 40.9 %collective-permute-start.9 = (bf16[640,640]{1,0:T(8,128)(2,1)}, bf16[640,640]{1,0:T(8,128)(2,1)S(1)}, u32[]{:S(2)}, u32[]{:S(2)}) collective-permute-start(bf16[640,640]{1,0:T(8,128)(2,1)} %get-tuple-element.125), channel_id=1, source_target_pairs={{0,8},{4,12},{8,0},{12,4},{16,24},{20,28},{24,16},{28,20},{1,9},{5... | collective-permute-start | bytes 2457608 | tf_op jit(solution)/shard_map/ppermute | solution.py:645
  36.2 20.2 %collective-permute-start.10 = (bf16[2048,128]{1,0:T(8,128)(2,1)S(1)}, bf16[2048,128]{1,0:T(8,128)(2,1)S(1)}, u32[]{:S(2)}, u32[]{:S(2)}) collective-permute-start(bf16[2048,128]{1,0:T(8,128)(2,1)S(1)} %pack_inputs.1), channel_id=1, source_target_pairs={{0,3},{1,2},{2,1},{3,0},{4,7},{5,6},{6,5},{7,4},{8,11},{9,10},{10,... | collective-permute-start | bytes 1572872 | tf_op jit(solution)/shard_map/ppermute | solution.py:581
  46.0 21.3 %collective-permute-start.11 = (bf16[384,768]{1,0:T(8,128)(2,1)S(1)}, bf16[384,768]{1,0:T(8,128)(2,1)}, u32[]{:S(2)}, u32[]{:S(2)}) collective-permute-start(bf16[384,768]{1,0:T(8,128)(2,1)S(1)} %get-tuple-element.138), channel_id=1, source_target_pairs={{0,8},{4,12},{8,0},{12,4},{16,24},{20,28},{24,16},{28,20},{1,9},{5... | collective-permute-start | bytes 1769480 | tf_op jit(solution)/shard_map/ppermute | solution.py:645
  63.7 19.0 %collective-permute-start.13 = (bf16[320,640]{1,0:T(8,128)(2,1)S(1)}, bf16[320,640]{1,0:T(8,128)(2,1)S(1)}, u32[]{:S(2)}, u32[]{:S(2)}) collective-permute-start(bf16[320,640]{1,0:T(8,128)(2,1)S(1)} %add_convert_fusion), channel_id=1, source_target_pairs={{0,24},{4,28},{8,16},{12,20},{16,8},{20,12},{24,0},{28,4},{1,25},{... | collective-permute-start | bytes 1228808 | tf_op jit(solution)/shard_map/ppermute | solution.py:651
  67.3 22.7 %collective-permute-start.12 = (bf16[384,768]{1,0:T(8,128)(2,1)S(1)}, bf16[384,768]{1,0:T(8,128)(2,1)S(1)}, u32[]{:S(2)}, u32[]{:S(2)}) collective-permute-start(bf16[384,768]{1,0:T(8,128)(2,1)S(1)} %get-tuple-element.140), channel_id=1, source_target_pairs={{0,8},{4,12},{8,0},{12,4},{16,24},{20,28},{24,16},{28,20},{1,9},{5... | collective-permute-start | bytes 1769480 | tf_op jit(solution)/shard_map/ppermute | solution.py:645
  83.0 18.2 %collective-permute-start.19 = (bf16[2384,128]{1,0:T(8,128)(2,1)S(1)}, bf16[2384,128]{1,0:T(8,128)(2,1)S(1)}, u32[]{:S(2)}, u32[]{:S(2)}) collective-permute-start(bf16[2384,128]{1,0:T(8,128)(2,1)S(1)} %finish_first.1.refs_0_), channel_id=1, source_target_pairs={{0,2},{1,3},{2,0},{3,1},{4,6},{5,7},{6,4},{7,5},{8,10},{9,11},{10,... | collective-permute-start | bytes 1830920 | tf_op jit(solution)/shard_map/ppermute | solution.py:581
  83.6 17.6 %collective-permute-start.18 = (bf16[2384,128]{1,0:T(8,128)(2,1)S(1)}, bf16[2384,128]{1,0:T(8,128)(2,1)S(1)}, u32[]{:S(2)}, u32[]{:S(2)}) collective-permute-start(bf16[2384,128]{1,0:T(8,128)(2,1)S(1)} %finish_first.1.refs_0_), channel_id=1, source_target_pairs={{0,1},{1,0},{2,3},{3,2},{4,5},{5,4},{6,7},{7,6},{8,9},{9,8},{10,11... | collective-permute-start | bytes 1830920 | tf_op jit(solution)/shard_map/ppermute | solution.py:581
  86.1 13.0 %collective-permute-start.17 = (bf16[192,768]{1,0:T(8,128)(2,1)S(1)}, bf16[192,768]{1,0:T(8,128)(2,1)S(1)}, u32[]{:S(2)}, u32[]{:S(2)}) collective-permute-start(bf16[192,768]{1,0:T(8,128)(2,1)S(1)} %add_convert_fusion.4), channel_id=1, source_target_pairs={{0,24},{4,28},{8,16},{12,20},{16,8},{20,12},{24,0},{28,4},{1,25},{... | collective-permute-start | bytes 884744 | tf_op jit(solution)/shard_map/ppermute | solution.py:651
  86.7 18.3 %collective-permute-start.20 = (bf16[928,128]{1,0:T(8,128)(2,1)S(1)}, bf16[928,128]{1,0:T(8,128)(2,1)S(1)}, u32[]{:S(2)}, u32[]{:S(2)}) collective-permute-start(bf16[928,128]{1,0:T(8,128)(2,1)S(1)} %get-tuple-element.157), channel_id=1, source_target_pairs={{0,3},{1,2},{2,1},{3,0},{4,7},{5,6},{6,5},{7,4},{8,11},{9,10},{10,... | collective-permute-start | bytes 712712 | tf_op jit(solution)/shard_map/ppermute | solution.py:581
  89.9 17.3 %collective-permute-start.16 = (bf16[224,896]{1,0:T(8,128)(2,1)S(1)}, bf16[224,896]{1,0:T(8,128)(2,1)S(1)}, u32[]{:S(2)}, u32[]{:S(2)}) collective-permute-start(bf16[224,896]{1,0:T(8,128)(2,1)S(1)} %get-tuple-element.152), channel_id=1, source_target_pairs={{0,8},{4,12},{8,0},{12,4},{16,24},{20,28},{24,16},{28,20},{1,9},{5... | collective-permute-start | bytes 1204232 | tf_op jit(solution)/shard_map/ppermute | solution.py:645
  99.1 16.3 %collective-permute-start.25 = (bf16[192,768]{1,0:T(8,128)(2,1)S(1)}, bf16[192,768]{1,0:T(8,128)(2,1)S(1)}, u32[]{:S(2)}, u32[]{:S(2)}) collective-permute-start(bf16[192,768]{1,0:T(8,128)(2,1)S(1)} %add_convert_fusion.2), channel_id=1, source_target_pairs={{0,24},{4,28},{8,16},{12,20},{16,8},{20,12},{24,0},{28,4},{1,25},{... | collective-permute-start | bytes 884744 | tf_op jit(solution)/shard_map/ppermute | solution.py:651
  101.2 15.4 %collective-permute-start.23 = (bf16[192,768]{1,0:T(8,128)(2,1)S(1)}, bf16[192,768]{1,0:T(8,128)(2,1)S(1)}, u32[]{:S(2)}, u32[]{:S(2)}) collective-permute-start(bf16[192,768]{1,0:T(8,128)(2,1)S(1)} %add_convert_fusion.3.refs_0_), channel_id=1, source_target_pairs={{0,2},{1,3},{2,0},{3,1},{4,6},{5,7},{6,4},{7,5},{8,10},{9,11},{10,... | collective-permute-start | bytes 884744 | tf_op jit(solution)/shard_map/ppermute | solution.py:581
  102.0 16.2 %collective-permute-start.22 = (bf16[192,768]{1,0:T(8,128)(2,1)S(1)}, bf16[192,768]{1,0:T(8,128)(2,1)S(1)}, u32[]{:S(2)}, u32[]{:S(2)}) collective-permute-start(bf16[192,768]{1,0:T(8,128)(2,1)S(1)} %add_convert_fusion.3.refs_0_), channel_id=1, source_target_pairs={{0,1},{1,0},{2,3},{3,2},{4,5},{5,4},{6,7},{7,6},{8,9},{9,8},{10,11... | collective-permute-start | bytes 884744 | tf_op jit(solution)/shard_map/ppermute | solution.py:581
  105.0 27.2 %collective-permute-start.29 = (bf16[2384,128]{1,0:T(8,128)(2,1)S(1)}, bf16[2384,128]{1,0:T(8,128)(2,1)S(1)}, u32[]{:S(2)}, u32[]{:S(2)}) collective-permute-start(bf16[2384,128]{1,0:T(8,128)(2,1)S(1)} %collective-permute-done.19.refs_2_), channel_id=1, source_target_pairs={{0,1},{1,0},{2,3},{3,2},{4,5},{5,4},{6,7},{7,6},{8,9},{9,8},{10,11... | collective-permute-start | bytes 1830920 | tf_op jit(solution)/shard_map/ppermute | solution.py:581
  115.6 13.5 %collective-permute-start.26 = (bf16[192,768]{1,0:T(8,128)(2,1)S(1)}, bf16[192,768]{1,0:T(8,128)(2,1)S(1)}, u32[]{:S(2)}, u32[]{:S(2)}) collective-permute-start(bf16[192,768]{1,0:T(8,128)(2,1)S(1)} %add_convert_fusion.1.refs_4_), channel_id=1, source_target_pairs={{0,1},{1,0},{2,3},{3,2},{4,5},{5,4},{6,7},{7,6},{8,9},{9,8},{10,11... | collective-permute-start | bytes 884744 | tf_op jit(solution)/shard_map/ppermute | solution.py:581
  116.6 17.1 %collective-permute-start.27 = (bf16[192,768]{1,0:T(8,128)(2,1)S(1)}, bf16[192,768]{1,0:T(8,128)(2,1)S(1)}, u32[]{:S(2)}, u32[]{:S(2)}) collective-permute-start(bf16[192,768]{1,0:T(8,128)(2,1)S(1)} %add_convert_fusion.1.refs_4_), channel_id=1, source_target_pairs={{0,2},{1,3},{2,0},{3,1},{4,6},{5,7},{6,4},{7,5},{8,10},{9,11},{10,... | collective-permute-start | bytes 884744 | tf_op jit(solution)/shard_map/ppermute | solution.py:581
  122.3 17.7 %collective-permute-start.24 = (bf16[192,768]{1,0:T(8,128)(2,1)S(1)}, bf16[192,768]{1,0:T(8,128)(2,1)S(1)}, u32[]{:S(2)}, u32[]{:S(2)}) collective-permute-start(bf16[192,768]{1,0:T(8,128)(2,1)S(1)} %collective-permute-done.22.refs_1_), channel_id=1, source_target_pairs={{0,2},{1,3},{2,0},{3,1},{4,6},{5,7},{6,4},{7,5},{8,10},{9,11},{10,... | collective-permute-start | bytes 884744 | tf_op jit(solution)/shard_map/ppermute | solution.py:581
  129.1 13.7 %collective-permute-start.28 = (bf16[192,768]{1,0:T(8,128)(2,1)S(1)}, bf16[192,768]{1,0:T(8,128)(2,1)S(1)}, u32[]{:S(2)}, u32[]{:S(2)}) collective-permute-start(bf16[192,768]{1,0:T(8,128)(2,1)S(1)} %collective-permute-done.26.refs_5_), channel_id=1, source_target_pairs={{0,2},{1,3},{2,0},{3,1},{4,6},{5,7},{6,4},{7,5},{8,10},{9,11},{10,... | collective-permute-start | bytes 884744 | tf_op jit(solution)/shard_map/ppermute | solution.py:581
  130.7 14.8 %collective-permute-start.32 = (bf16[112,896]{1,0:T(8,128)(2,1)S(1)}, bf16[112,896]{1,0:T(8,128)(2,1)S(1)}, u32[]{:S(2)}, u32[]{:S(2)}) collective-permute-start(bf16[112,896]{1,0:T(8,128)(2,1)S(1)} %add_convert_fusion.5.refs_4_), channel_id=1, source_target_pairs={{0,3},{1,2},{2,1},{3,0},{4,7},{5,6},{6,5},{7,4},{8,11},{9,10},{10,... | collective-permute-start | bytes 602120 | tf_op jit(solution)/shard_map/ppermute | solution.py:581
  132.2 13.3 %collective-permute-start.31 = (bf16[112,896]{1,0:T(8,128)(2,1)S(1)}, bf16[112,896]{1,0:T(8,128)(2,1)S(1)}, u32[]{:S(2)}, u32[]{:S(2)}) collective-permute-start(bf16[112,896]{1,0:T(8,128)(2,1)S(1)} %add_convert_fusion.5.refs_4_), channel_id=1, source_target_pairs={{0,2},{1,3},{2,0},{3,1},{4,6},{5,7},{6,4},{7,5},{8,10},{9,11},{10,... | collective-permute-start | bytes 602120 | tf_op jit(solution)/shard_map/ppermute | solution.py:581
  133.7 11.8 %collective-permute-start.30 = (bf16[112,896]{1,0:T(8,128)(2,1)S(1)}, bf16[112,896]{1,0:T(8,128)(2,1)S(1)}, u32[]{:S(2)}, u32[]{:S(2)}) collective-permute-start(bf16[112,896]{1,0:T(8,128)(2,1)S(1)} %add_convert_fusion.5.refs_4_), channel_id=1, source_target_pairs={{0,1},{1,0},{2,3},{3,2},{4,5},{5,4},{6,7},{7,6},{8,9},{9,8},{10,11... | collective-permute-start | bytes 602120 | tf_op jit(solution)/shard_map/ppermute | solution.py:581
  (24 other events, 175.4 us)

commit v3 on v2

--- a/solution.py
+++ b/solution.py
@@ -686,14 +686,15 @@
         other2 = swap_cores(sent)
         total0, from_prev, from_next = together(total0, from_prev, from_next)
         frame, back, *slabs = frames(from_prev, from_next)
-        slabs[1], slabs[2], other2, opposite0 = together(slabs[1], slabs[2], other2, opposite0)
+        slabs[1], slabs[2], other2 = together(slabs[1], slabs[2], other2)
         slabs[1], slabs[2] = to_peer(slabs[1], spaces, 1), to_peer(slabs[2], spaces, 2)
         raw, frame, *raws = together(raw, frame, *raws)
         raws.append(to_peer(raw, spaces, 3))
         other2, frame = together(other2, frame)
         both2, across2, here2 = mix_chunk(2, other2)
+        both3, across3, here3 = mix_chunk(3, other2, rows_one)
+        both2, here2, here3, opposite0 = together(both2, here2, here3, opposite0)
         beside2 = swap_beside(both2)
-        both3, across3, here3 = mix_chunk(3, other2, rows_one)
         here3, raws[2] = together(here3, raws[2])
         backs = peer_frames(raws, own_rows, wigner.shape[0])
         beside1, here2, here3, backs = together(beside1, here2, here3, backs)

time: 159 us -> 155 us (0.975)
  starting transfers between devices: 48.2 us -> 43.4 us
    ppermute x5, starting transfers between devices: 18.1 us -> 11.3 us  [swap_beside(): return lax.ppermute(both, 'dp', BESIDE)]
    ppermute x5, waiting for transfers between devices: 4.99 us -> 9.34 us  [swap_beside(): return lax.ppermute(both, 'dp', BESIDE)]
    ppermute x5, waiting for transfers between devices: 23.9 us -> 22 us  [swap_opposite(): return lax.ppermute(total, 'dp', OPPOSITE)]
    ppermute x18, waiting for transfers between devices: 21.9 us -> 20.2 us  [to_peer(): return lax.ppermute(array, 'space', [(i, i ^ k) for i in range(spaces)])]
  transfers between devices with their start and end apart: 35 -> 35, of which waited for: 17 -> 14; matrix products, arithmetic and copies ran while one was open for 2% -> 2% of each run, Pallas kernels for 26% -> 28%
where the time goes in v3:
time: 155 us; the launch traced here: 154 us
  waiting for transfers between devices  56.4 us (36%)
  Pallas kernels  47.8 us (31%)
  starting transfers between devices  43.4 us (28%)
  other arithmetic  2.72 us (2%)
  local copies, waits for them, and re-layouts  2.41 us (2%)
  between operations  1.65 us (1%)
    ppermute x5, waiting for transfers between devices, swap_opposite(): return lax.ppermute(total, 'dp', OPPOSITE)  22 us
    ppermute x18, starting transfers between devices, to_peer(): return lax.ppermute(array, 'space', [(i, i ^ k) for i in range(spaces)])  21.8 us
    ppermute x18, waiting for transfers between devices, to_peer(): return lax.ppermute(array, 'space', [(i, i ^ k) for i in range(spaces)])  20.2 us
    pallas_call x5, Pallas kernels, mix(): pl.pallas_call(functools.partial(mix_kernel, offset, other_offset), in_sp...  17.6 us
    ppermute x5, starting transfers between devices, swap_beside(): return lax.ppermute(both, 'dp', BESIDE)  11.3 us
    ppermute x5, waiting for transfers between devices, swap_beside(): return lax.ppermute(both, 'dp', BESIDE)  9.34 us
    pallas_call x1, Pallas kernels, peer_frames(): pl.pallas_call(functools.partial(peer_frames_kernel, own, wig_rows), in_s...  7.19 us
    pallas_call x3, Pallas kernels, apply_weights(): pl.pallas_call(functools.partial(apply_kernel, group, places, width // sp...  6.67 us
  transfers between devices with their start and end apart: 35, of which 14 were waited for; matrix products, arithmetic and copies ran while one was open for 2% of the time, Pallas kernels for 28%

profile of v3, /device:TPU:10, one launch (start us, length us, event | category | flops | bytes accessed | tf_op | source)
XLA Modules:
  0.0 154.4 jit_solution(8373309825303802095)
XLA Ops:
  5.3 2.8 %mix.5 = (bf16[224,896]{1,0:T(8,128)(2,1)S(1)}, bf16[112,896]{1,0:T(8,128)(2,1)S(1)}, bf16[112,896]{1,0:T(8,128)(2,1)S(1)}) custom-call(s32[2]{0:T(128)S(1)} %pad_add_fusion.place_ref, f32[8,32]{1,0:T(8,128)S(1)} %copy-done.4, bf16[4,224,896]{2,1,0:T(8,128)(2,1)} %own_ref.3, bf16[4,224,896]{2,1,0:T(8,128)(2,1)S(1)} %collective-permute-done.other_ref), custom_call_target="tpu_custom_call" | custom-call | tf_op jit(solution)/shard_map/mix/pallas_call | solution.py:114
  10.7 4.9 %mix.6 = (bf16[640,640]{1,0:T(8,128)(2,1)}, bf16[320,640]{1,0:T(8,128)(2,1)S(1)}, bf16[320,640]{1,0:T(8,128)(2,1)S(1)}) custom-call(s32[2]{0:T(128)S(1)} %pad_add_fusion.place_ref, f32[8,32]{1,0:T(8,128)S(1)} %copy-done.4, bf16[4,320,640]{2,1,0:T(8,128)(2,1)} %bitcast.20, bf16[4,320,640]{2,1,0:T(8,128)(2,1)S(1)} %collective-permute-done.2.other_ref), custom_call_target="tpu_custom_call" | custom-call | tf_op jit(solution)/shard_map/mix/pallas_call | solution.py:114
  16.6 3.2 %collective-permute-done.1.refs_1_ = bf16[224,896]{1,0:T(8,128)(2,1)S(1)} collective-permute-done((bf16[224,896]{1,0:T(8,128)(2,1)S(1)}, bf16[224,896]{1,0:T(8,128)(2,1)S(1)}, u32[]{:S(2)}, u32[]{:S(2)}) %collective-permute-start.1) | collective-permute-done | bytes 401440 | tf_op jit(solution)/shard_map/ppermute | solution.py:645
  23.3 5.3 %enter_frame.1 = (bf16[128,3712]{1,0:T(8,128)(2,1)S(1)}, bf16[128,3712]{1,0:T(8,128)(2,1)S(1)}, bf16[928,128]{1,0:T(8,128)(2,1)S(1)}, bf16[928,128]{1,0:T(8,128)...) custom-call(s32[2]{0:T(128)S(1)} %pad_add_fusion.place_ref, s32[1,1]{1,0:T(1,128)S(6)} %copy.16.count_ref, ...), custom_call_target="tpu_custom_call" | custom-call | tf_op jit(solution)/shard_map/enter_frame/pallas_call | solution.py:263
  28.6 6.3 %collective-permute-done.7.refs_1_ = bf16[2048,128]{1,0:T(8,128)(2,1)S(1)} collective-permute-done((bf16[2048,128]{1,0:T(8,128)(2,1)S(1)}, bf16[2048,128]{1,0:T(8,128)(2,1)S(1)}, u32[]{:S(2)}, u32[]{:S(2)}) %collective-permute-start.7) | collective-permute-done | bytes 524320 | tf_op jit(solution)/shard_map/ppermute | solution.py:581
  38.2 3.2 %mix.8 = (bf16[384,768]{1,0:T(8,128)(2,1)S(1)}, bf16[192,768]{1,0:T(8,128)(2,1)S(1)}, bf16[192,768]{1,0:T(8,128)(2,1)S(1)}) custom-call(s32[2]{0:T(128)S(1)} %pad_add_fusion.place_ref, f32[8,32]{1,0:T(8,128)S(1)} %copy-done.4, bf16[4,384,768]{2,1,0:T(8,128)(2,1)} %bitcast.17, bf16[4,384,768]{2,1,0:T(8,128)(2,1)S(1)} %collective-permute-done.5.other_ref), custom_call_target="tpu_custom_call" | custom-call | tf_op jit(solution)/shard_map/mix/pallas_call | solution.py:114
  41.4 3.2 %mix.7 = (bf16[384,768]{1,0:T(8,128)(2,1)S(1)}, bf16[192,768]{1,0:T(8,128)(2,1)S(1)}, bf16[192,768]{1,0:T(8,128)(2,1)S(1)}) custom-call(s32[2]{0:T(128)S(1)} %pad_add_fusion.place_ref, f32[8,32]{1,0:T(8,128)S(1)} %copy-done.4, bf16[4,384,768]{2,1,0:T(8,128)(2,1)} %bitcast.18, bf16[4,384,768]{2,1,0:T(8,128)(2,1)S(1)} %collective-permute-done.5.other_ref), custom_call_target="tpu_custom_call" | custom-call | tf_op jit(solution)/shard_map/mix/pallas_call | solution.py:114
  44.7 5.2 %collective-permute-start.11 = (bf16[384,768]{1,0:T(8,128)(2,1)S(1)}, bf16[384,768]{1,0:T(8,128)(2,1)}, u32[]{:S(2)}, u32[]{:S(2)}) collective-permute-start(bf16[384,768]{1,0:T(8,128)(2,1)S(1)} %get-tuple-element.144), channel_id=1, source_target_pairs={{0,8},{4,12},{8,0},{12,4},{16,24},{20,28},{24,16},{28,20},{1,9},{5... | collective-permute-start | bytes 1769480 | tf_op jit(solution)/shard_map/ppermute | solution.py:645
  50.3 7.2 %peer_frames.1.backs = bf16[3,128,3712]{2,1,0:T(8,128)(2,1)S(1)} custom-call(bf16[2048,128]{1,0:T(8,128)(2,1)S(1)} %collective-permute-done.6.refs_0_, bf16[2048,128]{1,0:T(8,128)(2,1)S(1)} %collective-permute-done.7.refs_1_, bf16[2048,128]{1,0:T(8,128)(2,1)S(1)} %collective-permute-done.10.refs_2_), custom_call_target="tpu_custom_call" | custom-call | tf_op jit(solution)/shard_map/peer_frames/pallas_call | solution.py:300
  59.3 3.5 %mix.9 = (bf16[224,896]{1,0:T(8,128)(2,1)}, bf16[112,896]{1,0:T(8,128)(2,1)S(1)}, bf16[112,896]{1,0:T(8,128)(2,1)S(1)}) custom-call(s32[2]{0:T(128)S(1)} %pad_add_fusion.place_ref, f32[8,32]{1,0:T(8,128)S(1)} %copy-done.4, bf16[4,224,896]{2,1,0:T(8,128)(2,1)} %own_ref.3, bf16[4,224,896]{2,1,0:T(8,128)(2,1)S(1)} %collective-permute-done.other_ref), custom_call_target="tpu_custom_call" | custom-call | tf_op jit(solution)/shard_map/mix/pallas_call | solution.py:114
  62.8 6.2 %collective-permute-done.11 = bf16[384,768]{1,0:T(8,128)(2,1)} collective-permute-done((bf16[384,768]{1,0:T(8,128)(2,1)S(1)}, bf16[384,768]{1,0:T(8,128)(2,1)}, u32[]{:S(2)}, u32[]{:S(2)}) %collective-permute-start.11) | collective-permute-done | bytes 589856 | tf_op jit(solution)/shard_map/ppermute | solution.py:645
  68.9 3.1 %collective-permute-start.12 = (bf16[384,768]{1,0:T(8,128)(2,1)S(1)}, bf16[384,768]{1,0:T(8,128)(2,1)S(1)}, u32[]{:S(2)}, u32[]{:S(2)}) collective-permute-start(bf16[384,768]{1,0:T(8,128)(2,1)S(1)} %get-tuple-element.146), channel_id=1, source_target_pairs={{0,8},{4,12},{8,0},{12,4},{16,24},{20,28},{24,16},{28,20},{1,9},{5... | collective-permute-start | bytes 1769480 | tf_op jit(solution)/shard_map/ppermute | solution.py:645
  74.1 4.4 %collective-permute-done.14.refs_1_ = bf16[928,128]{1,0:T(8,128)(2,1)S(1)} collective-permute-done((bf16[928,128]{1,0:T(8,128)(2,1)S(1)}, bf16[928,128]{1,0:T(8,128)(2,1)S(1)}, u32[]{:S(2)}, u32[]{:S(2)}) %collective-permute-start.14) | collective-permute-done | bytes 237600 | tf_op jit(solution)/shard_map/ppermute | solution.py:581
  78.4 4.2 %collective-permute-done.15.refs_2_ = bf16[928,128]{1,0:T(8,128)(2,1)S(1)} collective-permute-done((bf16[928,128]{1,0:T(8,128)(2,1)S(1)}, bf16[928,128]{1,0:T(8,128)(2,1)S(1)}, u32[]{:S(2)}, u32[]{:S(2)}) %collective-permute-start.15) | collective-permute-done | bytes 237600 | tf_op jit(solution)/shard_map/ppermute | solution.py:581
  84.2 3.5 %collective-permute-start.20 = (bf16[928,128]{1,0:T(8,128)(2,1)S(1)}, bf16[928,128]{1,0:T(8,128)(2,1)S(1)}, u32[]{:S(2)}, u32[]{:S(2)}) collective-permute-start(bf16[928,128]{1,0:T(8,128)(2,1)S(1)} %get-tuple-element.163), channel_id=1, source_target_pairs={{0,3},{1,2},{2,1},{3,0},{4,7},{5,6},{6,5},{7,4},{8,11},{9,10},{10,... | collective-permute-start | bytes 712712 | tf_op jit(solution)/shard_map/ppermute | solution.py:581
  89.7 9.8 %collective-permute-done.17 = bf16[192,768]{1,0:T(8,128)(2,1)S(1)} collective-permute-done((bf16[192,768]{1,0:T(8,128)(2,1)S(1)}, bf16[192,768]{1,0:T(8,128)(2,1)S(1)}, u32[]{:S(2)}, u32[]{:S(2)}) %collective-permute-start.17) | collective-permute-done | bytes 294944 | tf_op jit(solution)/shard_map/ppermute | solution.py:651
  105.2 8.6 %collective-permute-done.25 = bf16[192,768]{1,0:T(8,128)(2,1)S(1)} collective-permute-done((bf16[192,768]{1,0:T(8,128)(2,1)S(1)}, bf16[192,768]{1,0:T(8,128)(2,1)S(1)}, u32[]{:S(2)}, u32[]{:S(2)}) %collective-permute-start.25) | collective-permute-done | bytes 294944 | tf_op jit(solution)/shard_map/ppermute | solution.py:651
  118.4 3.7 %collective-permute-done.21 = bf16[112,896]{1,0:T(8,128)(2,1)S(1)} collective-permute-done((bf16[112,896]{1,0:T(8,128)(2,1)S(1)}, bf16[112,896]{1,0:T(8,128)(2,1)S(1)}, u32[]{:S(2)}, u32[]{:S(2)}) %collective-permute-start.21) | collective-permute-done | bytes 200736 | tf_op jit(solution)/shard_map/ppermute | solution.py:651
  122.8 3.6 %collective-permute-done.26.refs_5_ = bf16[192,768]{1,0:T(8,128)(2,1)S(1)} collective-permute-done((bf16[192,768]{1,0:T(8,128)(2,1)S(1)}, bf16[192,768]{1,0:T(8,128)(2,1)S(1)}, u32[]{:S(2)}, u32[]{:S(2)}) %collective-permute-start.26) | collective-permute-done | bytes 294944 | tf_op jit(solution)/shard_map/ppermute | solution.py:581
  131.3 3.4 %weight_grads.1 = (bf16[224,896]{1,0:T(8,128)(2,1)}, bf16[2,192,768]{2,1,0:T(8,128)(2,1)}, bf16[2,160,640]{2,1,0:T(8,128)(2,1)}) custom-call(bf16[128,3712]{1,0:T(8,128)(2,1)S(1)} %get-tuple-element.178.back_ref, bf16[3,128,3712]{2,1,0:T(8,128)(2,1)S(1)} %peer_frames.1.backs, bf16[928,128]{1,0:T(8,128)(2,1)S(1)} %get-tuple-element.180.refs_0_, ...), custom_call_target="tpu_custom_call" | custom-call | tf_op jit(solution)/shard_map/weight_grads/pallas_call | solution.py:336
  137.1 2.7 %apply_weights_1.1 = (bf16[1536,128]{1,0:T(8,128)(2,1)S(1)}, bf16[1536,128]{1,0:T(8,128)(2,1)S(1)}) custom-call(s32[2]{0:T(128)S(1)} %pad_add_fusion.place_ref, bf16[128,3712]{1,0:T(8,128)(2,1)S(1)} %get-tuple-element.187.frame_ref, bf16[128,3712]{1,0:T(8,128)(2,1)S(1)} %get-tuple-element.178.back_ref, bf16[192,768]{1,0:T(8,128)(2,1)S(1)} %add_convert_fusion.3.refs_0_, ...), custom_call_target="tpu_custom_call" | custom-call | tf_op jit(solution)/shard_map/apply_weights_1/pallas_call | solution.py:402
  143.9 3.8 %collective-permute-start.34 = (bf16[8,6272]{1,0:T(8,128)(2,1)S(1)}, bf16[8,6272]{1,0:T(8,128)(2,1)S(1)}, u32[]{:S(2)}, u32[]{:S(2)}) collective-permute-start(bf16[8,6272]{1,0:T(8,128)(2,1)S(1)} %get-tuple-element.203), channel_id=1, source_target_pairs={{0,1},{1,2},{2,3},{3,0},{4,5},{5,6},{6,7},{7,4},{8,9},{9,10},{10,1... | collective-permute-start | bytes 301064 | tf_op jit(solution)/shard_map/ppermute | solution.py:773
  147.8 2.9 %leave_frame.1 = bf16[32,6272]{1,0:T(8,128)(2,1)} custom-call(bf16[896,128]{1,0:T(8,128)(2,1)S(1)} %get-tuple-element.192.zero_ref, bf16[1536,128]{1,0:T(8,128)(2,1)S(1)} %get-tuple-element.193.one_ref, bf16[1280,128]{1,0:T(8,128)(2,1)S(1)} %get-tuple-element.194.two_ref, bf16[455,128]{1,0:T(8,128)(2,1)S(1)} %copy-done.3, s32[1,1]{1,0:T(1,128)S(6)} %copy.16.count_ref, ...), custom_call_target="tpu_custom_call" | custom-call | tf_op jit(solution)/shard_map/leave_frame/pallas_call | solution.py:525
  150.7 2.6 %collective-permute-done.33.next_ref = bf16[8,6272]{1,0:T(8,128)(2,1)S(1)} collective-permute-done((bf16[8,6272]{1,0:T(8,128)(2,1)S(1)}, bf16[8,6272]{1,0:T(8,128)(2,1)S(1)}, u32[]{:S(2)}, u32[]{:S(2)}) %collective-permute-start.33) | collective-permute-done | bytes 100384 | tf_op jit(solution)/shard_map/ppermute | solution.py:772
  (92 shorter events, 45.6 us)
Async XLA Ops:
  8.1 11.6 %collective-permute-start.1 = (bf16[224,896]{1,0:T(8,128)(2,1)S(1)}, bf16[224,896]{1,0:T(8,128)(2,1)S(1)}, u32[]{:S(2)}, u32[]{:S(2)}) collective-permute-start(bf16[224,896]{1,0:T(8,128)(2,1)S(1)} %get-tuple-element.108), channel_id=1, source_target_pairs={{0,8},{4,12},{8,0},{12,4},{16,24},{20,28},{24,16},{28,20},{1,9},{5... | collective-permute-start | bytes 1204232 | tf_op jit(solution)/shard_map/ppermute | solution.py:645
  19.7 18.5 %collective-permute-start.5 = (bf16[4,384,768]{2,1,0:T(8,128)(2,1)}, bf16[4,384,768]{2,1,0:T(8,128)(2,1)S(1)}, u32[]{:S(2)}, u32[]{:S(2)}) collective-permute-start(bf16[4,384,768]{2,1,0:T(8,128)(2,1)} %bitcast.16), channel_id=1, source_target_pairs={{0,4},{4,0},{8,12},{12,8},{16,20},{20,16},{24,28},{28,24},{1,5},{5... | collective-permute-start | bytes 7077896 | tf_op jit(solution)/shard_map/ppermute | solution.py:638
  20.5 14.4 %collective-permute-start.7 = (bf16[2048,128]{1,0:T(8,128)(2,1)S(1)}, bf16[2048,128]{1,0:T(8,128)(2,1)S(1)}, u32[]{:S(2)}, u32[]{:S(2)}) collective-permute-start(bf16[2048,128]{1,0:T(8,128)(2,1)S(1)} %pack_inputs.1), channel_id=1, source_target_pairs={{0,2},{1,3},{2,0},{3,1},{4,6},{5,7},{6,4},{7,5},{8,10},{9,11},{10,... | collective-permute-start | bytes 1572872 | tf_op jit(solution)/shard_map/ppermute | solution.py:581
  22.1 14.1 %collective-permute-start.6 = (bf16[2048,128]{1,0:T(8,128)(2,1)S(1)}, bf16[2048,128]{1,0:T(8,128)(2,1)S(1)}, u32[]{:S(2)}, u32[]{:S(2)}) collective-permute-start(bf16[2048,128]{1,0:T(8,128)(2,1)S(1)} %pack_inputs.1), channel_id=1, source_target_pairs={{0,1},{1,0},{2,3},{3,2},{4,5},{5,4},{6,7},{7,6},{8,9},{9,8},{10,11... | collective-permute-start | bytes 1572872 | tf_op jit(solution)/shard_map/ppermute | solution.py:581
  22.7 34.8 %collective-permute-start.8 = (bf16[640,640]{1,0:T(8,128)(2,1)}, bf16[640,640]{1,0:T(8,128)(2,1)S(1)}, u32[]{:S(2)}, u32[]{:S(2)}) collective-permute-start(bf16[640,640]{1,0:T(8,128)(2,1)} %get-tuple-element.128), channel_id=1, source_target_pairs={{0,8},{4,12},{8,0},{12,4},{16,24},{20,28},{24,16},{28,20},{1,9},{5... | collective-permute-start | bytes 2457608 | tf_op jit(solution)/shard_map/ppermute | solution.py:645
  36.2 14.1 %collective-permute-start.10 = (bf16[2048,128]{1,0:T(8,128)(2,1)S(1)}, bf16[2048,128]{1,0:T(8,128)(2,1)S(1)}, u32[]{:S(2)}, u32[]{:S(2)}) collective-permute-start(bf16[2048,128]{1,0:T(8,128)(2,1)S(1)} %pack_inputs.1), channel_id=1, source_target_pairs={{0,3},{1,2},{2,1},{3,0},{4,7},{5,6},{6,5},{7,4},{8,11},{9,10},{10,... | collective-permute-start | bytes 1572872 | tf_op jit(solution)/shard_map/ppermute | solution.py:581
  44.7 24.3 %collective-permute-start.11 = (bf16[384,768]{1,0:T(8,128)(2,1)S(1)}, bf16[384,768]{1,0:T(8,128)(2,1)}, u32[]{:S(2)}, u32[]{:S(2)}) collective-permute-start(bf16[384,768]{1,0:T(8,128)(2,1)S(1)} %get-tuple-element.144), channel_id=1, source_target_pairs={{0,8},{4,12},{8,0},{12,4},{16,24},{20,28},{24,16},{28,20},{1,9},{5... | collective-permute-start | bytes 1769480 | tf_op jit(solution)/shard_map/ppermute | solution.py:645
  57.6 25.0 %collective-permute-start.13 = (bf16[320,640]{1,0:T(8,128)(2,1)S(1)}, bf16[320,640]{1,0:T(8,128)(2,1)S(1)}, u32[]{:S(2)}, u32[]{:S(2)}) collective-permute-start(bf16[320,640]{1,0:T(8,128)(2,1)S(1)} %add_convert_fusion), channel_id=1, source_target_pairs={{0,24},{4,28},{8,16},{12,20},{16,8},{20,12},{24,0},{28,4},{1,25},{... | collective-permute-start | bytes 1228808 | tf_op jit(solution)/shard_map/ppermute | solution.py:651
  68.9 18.7 %collective-permute-start.12 = (bf16[384,768]{1,0:T(8,128)(2,1)S(1)}, bf16[384,768]{1,0:T(8,128)(2,1)S(1)}, u32[]{:S(2)}, u32[]{:S(2)}) collective-permute-start(bf16[384,768]{1,0:T(8,128)(2,1)S(1)} %get-tuple-element.146), channel_id=1, source_target_pairs={{0,8},{4,12},{8,0},{12,4},{16,24},{20,28},{24,16},{28,20},{1,9},{5... | collective-permute-start | bytes 1769480 | tf_op jit(solution)/shard_map/ppermute | solution.py:645
  82.9 17.6 %collective-permute-start.19 = (bf16[2384,128]{1,0:T(8,128)(2,1)S(1)}, bf16[2384,128]{1,0:T(8,128)(2,1)S(1)}, u32[]{:S(2)}, u32[]{:S(2)}) collective-permute-start(bf16[2384,128]{1,0:T(8,128)(2,1)S(1)} %finish_first.1.refs_0_), channel_id=1, source_target_pairs={{0,2},{1,3},{2,0},{3,1},{4,6},{5,7},{6,4},{7,5},{8,10},{9,11},{10,... | collective-permute-start | bytes 1830920 | tf_op jit(solution)/shard_map/ppermute | solution.py:581
  83.0 17.6 %collective-permute-start.18 = (bf16[2384,128]{1,0:T(8,128)(2,1)S(1)}, bf16[2384,128]{1,0:T(8,128)(2,1)S(1)}, u32[]{:S(2)}, u32[]{:S(2)}) collective-permute-start(bf16[2384,128]{1,0:T(8,128)(2,1)S(1)} %finish_first.1.refs_0_), channel_id=1, source_target_pairs={{0,1},{1,0},{2,3},{3,2},{4,5},{5,4},{6,7},{7,6},{8,9},{9,8},{10,11... | collective-permute-start | bytes 1830920 | tf_op jit(solution)/shard_map/ppermute | solution.py:581
  84.1 15.3 %collective-permute-start.17 = (bf16[192,768]{1,0:T(8,128)(2,1)S(1)}, bf16[192,768]{1,0:T(8,128)(2,1)S(1)}, u32[]{:S(2)}, u32[]{:S(2)}) collective-permute-start(bf16[192,768]{1,0:T(8,128)(2,1)S(1)} %add_convert_fusion.4), channel_id=1, source_target_pairs={{0,24},{4,28},{8,16},{12,20},{16,8},{20,12},{24,0},{28,4},{1,25},{... | collective-permute-start | bytes 884744 | tf_op jit(solution)/shard_map/ppermute | solution.py:651
  84.2 19.1 %collective-permute-start.20 = (bf16[928,128]{1,0:T(8,128)(2,1)S(1)}, bf16[928,128]{1,0:T(8,128)(2,1)S(1)}, u32[]{:S(2)}, u32[]{:S(2)}) collective-permute-start(bf16[928,128]{1,0:T(8,128)(2,1)S(1)} %get-tuple-element.163), channel_id=1, source_target_pairs={{0,3},{1,2},{2,1},{3,0},{4,7},{5,6},{6,5},{7,4},{8,11},{9,10},{10,... | collective-permute-start | bytes 712712 | tf_op jit(solution)/shard_map/ppermute | solution.py:581
  87.7 17.5 %collective-permute-start.16 = (bf16[224,896]{1,0:T(8,128)(2,1)}, bf16[224,896]{1,0:T(8,128)(2,1)S(1)}, u32[]{:S(2)}, u32[]{:S(2)}) collective-permute-start(bf16[224,896]{1,0:T(8,128)(2,1)} %get-tuple-element.158), channel_id=1, source_target_pairs={{0,8},{4,12},{8,0},{12,4},{16,24},{20,28},{24,16},{28,20},{1,9},{5... | collective-permute-start | bytes 1204232 | tf_op jit(solution)/shard_map/ppermute | solution.py:645
  99.5 14.3 %collective-permute-start.25 = (bf16[192,768]{1,0:T(8,128)(2,1)S(1)}, bf16[192,768]{1,0:T(8,128)(2,1)S(1)}, u32[]{:S(2)}, u32[]{:S(2)}) collective-permute-start(bf16[192,768]{1,0:T(8,128)(2,1)S(1)} %add_convert_fusion.2), channel_id=1, source_target_pairs={{0,24},{4,28},{8,16},{12,20},{16,8},{20,12},{24,0},{28,4},{1,25},{... | collective-permute-start | bytes 884744 | tf_op jit(solution)/shard_map/ppermute | solution.py:651
  100.6 16.9 %collective-permute-start.23 = (bf16[192,768]{1,0:T(8,128)(2,1)S(1)}, bf16[192,768]{1,0:T(8,128)(2,1)S(1)}, u32[]{:S(2)}, u32[]{:S(2)}) collective-permute-start(bf16[192,768]{1,0:T(8,128)(2,1)S(1)} %add_convert_fusion.3.refs_0_), channel_id=1, source_target_pairs={{0,2},{1,3},{2,0},{3,1},{4,6},{5,7},{6,4},{7,5},{8,10},{9,11},{10,... | collective-permute-start | bytes 884744 | tf_op jit(solution)/shard_map/ppermute | solution.py:581
  103.1 15.3 %collective-permute-start.22 = (bf16[192,768]{1,0:T(8,128)(2,1)S(1)}, bf16[192,768]{1,0:T(8,128)(2,1)S(1)}, u32[]{:S(2)}, u32[]{:S(2)}) collective-permute-start(bf16[192,768]{1,0:T(8,128)(2,1)S(1)} %add_convert_fusion.3.refs_0_), channel_id=1, source_target_pairs={{0,1},{1,0},{2,3},{3,2},{4,5},{5,4},{6,7},{7,6},{8,9},{9,8},{10,11... | collective-permute-start | bytes 884744 | tf_op jit(solution)/shard_map/ppermute | solution.py:581
  103.3 26.7 %collective-permute-start.29 = (bf16[2384,128]{1,0:T(8,128)(2,1)S(1)}, bf16[2384,128]{1,0:T(8,128)(2,1)S(1)}, u32[]{:S(2)}, u32[]{:S(2)}) collective-permute-start(bf16[2384,128]{1,0:T(8,128)(2,1)S(1)} %collective-permute-done.19.refs_2_), channel_id=1, source_target_pairs={{0,1},{1,0},{2,3},{3,2},{4,5},{5,4},{6,7},{7,6},{8,9},{9,8},{10,11... | collective-permute-start | bytes 1830920 | tf_op jit(solution)/shard_map/ppermute | solution.py:581
  113.9 12.5 %collective-permute-start.26 = (bf16[192,768]{1,0:T(8,128)(2,1)S(1)}, bf16[192,768]{1,0:T(8,128)(2,1)S(1)}, u32[]{:S(2)}, u32[]{:S(2)}) collective-permute-start(bf16[192,768]{1,0:T(8,128)(2,1)S(1)} %add_convert_fusion.1.refs_4_), channel_id=1, source_target_pairs={{0,1},{1,0},{2,3},{3,2},{4,5},{5,4},{6,7},{7,6},{8,9},{9,8},{10,11... | collective-permute-start | bytes 884744 | tf_op jit(solution)/shard_map/ppermute | solution.py:581
  117.4 12.7 %collective-permute-start.27 = (bf16[192,768]{1,0:T(8,128)(2,1)S(1)}, bf16[192,768]{1,0:T(8,128)(2,1)S(1)}, u32[]{:S(2)}, u32[]{:S(2)}) collective-permute-start(bf16[192,768]{1,0:T(8,128)(2,1)S(1)} %add_convert_fusion.1.refs_4_), channel_id=1, source_target_pairs={{0,2},{1,3},{2,0},{3,1},{4,6},{5,7},{6,4},{7,5},{8,10},{9,11},{10,... | collective-permute-start | bytes 884744 | tf_op jit(solution)/shard_map/ppermute | solution.py:581
  122.1 15.0 %collective-permute-start.24 = (bf16[192,768]{1,0:T(8,128)(2,1)S(1)}, bf16[192,768]{1,0:T(8,128)(2,1)S(1)}, u32[]{:S(2)}, u32[]{:S(2)}) collective-permute-start(bf16[192,768]{1,0:T(8,128)(2,1)S(1)} %collective-permute-done.22.refs_1_), channel_id=1, source_target_pairs={{0,2},{1,3},{2,0},{3,1},{4,6},{5,7},{6,4},{7,5},{8,10},{9,11},{10,... | collective-permute-start | bytes 884744 | tf_op jit(solution)/shard_map/ppermute | solution.py:581
  126.4 10.7 %collective-permute-start.28 = (bf16[192,768]{1,0:T(8,128)(2,1)S(1)}, bf16[192,768]{1,0:T(8,128)(2,1)S(1)}, u32[]{:S(2)}, u32[]{:S(2)}) collective-permute-start(bf16[192,768]{1,0:T(8,128)(2,1)S(1)} %collective-permute-done.26.refs_5_), channel_id=1, source_target_pairs={{0,2},{1,3},{2,0},{3,1},{4,6},{5,7},{6,4},{7,5},{8,10},{9,11},{10,... | collective-permute-start | bytes 884744 | tf_op jit(solution)/shard_map/ppermute | solution.py:581
  127.7 12.0 %collective-permute-start.32 = (bf16[112,896]{1,0:T(8,128)(2,1)S(1)}, bf16[112,896]{1,0:T(8,128)(2,1)S(1)}, u32[]{:S(2)}, u32[]{:S(2)}) collective-permute-start(bf16[112,896]{1,0:T(8,128)(2,1)S(1)} %add_convert_fusion.5.refs_4_), channel_id=1, source_target_pairs={{0,3},{1,2},{2,1},{3,0},{4,7},{5,6},{6,5},{7,4},{8,11},{9,10},{10,... | collective-permute-start | bytes 602120 | tf_op jit(solution)/shard_map/ppermute | solution.py:581
  130.0 9.8 %collective-permute-start.31 = (bf16[112,896]{1,0:T(8,128)(2,1)S(1)}, bf16[112,896]{1,0:T(8,128)(2,1)S(1)}, u32[]{:S(2)}, u32[]{:S(2)}) collective-permute-start(bf16[112,896]{1,0:T(8,128)(2,1)S(1)} %add_convert_fusion.5.refs_4_), channel_id=1, source_target_pairs={{0,2},{1,3},{2,0},{3,1},{4,6},{5,7},{6,4},{7,5},{8,10},{9,11},{10,... | collective-permute-start | bytes 602120 | tf_op jit(solution)/shard_map/ppermute | solution.py:581
  (20 other events, 140.6 us)

commit v4 on v3

--- a/solution.py
+++ b/solution.py
@@ -698,16 +698,16 @@
         here3, raws[2] = together(here3, raws[2])
         backs = peer_frames(raws, own_rows, wigner.shape[0])
         beside1, here2, here3, backs = together(beside1, here2, here3, backs)
+        beside1, *slabs[1:] = together(beside1, *slabs[1:])
+        slabs[3] = to_peer(slabs[3], spaces, 3)
         total1 = total_opposite(1, across1, beside1)
         opposite1 = swap_opposite(total1)
         other0, beside1 = together(other0, beside1)
         both4, across4, here4 = mix_chunk(4, other0, half)
-        both3, beside2, here4 = together(both3, beside2, here4)
+        both3, beside2, here4, slabs[3] = together(both3, beside2, here4, slabs[3])
         beside3 = swap_beside(both3)
         total2 = total_opposite(2, across2, beside2)
         opposite2 = swap_opposite(total2)
-        beside2, *slabs[1:] = together(beside2, *slabs[1:])
-        slabs[3] = to_peer(slabs[3], spaces, 3)
         opposite1, beside2 = together(opposite1, beside2)
         shard1 = finish((here0, beside0, opposite0), (here1, beside1, opposite1))
         sides1 = to_sides(shard1)
@@ -725,15 +725,14 @@
         opposite3, total4 = together(opposite3, total4)
         shard3 = total_here(3, here3, beside3, opposite3)
         sides3 = to_sides(shard3)
+        late_back, beside4 = together(back, beside4)
+        grad_mix = weight_grads(late_back, backs, slabs, scale)
+        opposite4, *grad_mix = together(opposite4, *grad_mix)
         opposite4, *sides2 = together(opposite4, *sides2)
         shard4 = total_here(4, here4, beside4, opposite4)
-        late_back, shard4, slabs[3] = together(back, shard4, slabs[3])
-        grad_mix = weight_grads(late_back, backs, slabs, scale)
         sides4 = to_sides(shard4)
         forward2 = forward(2, sides2)
         shard4 = total_here(4, here4, beside4, opposite4)
-        late_back, shard4, slabs[3] = together(back, shard4, slabs[3])
-        grad_mix = weight_grads(late_back, backs, slabs, scale)
         sides4 = to_sides(shard4)
         outs, grads = {}, {}
         whole = {
@@ -764,7 +763,7 @@
 
     for group, pieces_of in whole.items():
         if group == 0:
-            frame, grads[1], *grad_mix = together(frame, grads[1], *grad_mix)
+            frame, grads[1] = together(frame, grads[1])
         outs[group], grads[group] = apply_weights(group, place, frame, back, pieces_of, spaces)
     base, returning = leave_back(
         [grads[g] for g in (0, 1, 3)], wigner, sources, grad_out, 2 * ghosts

time: 155 us -> 158 us (1.019)
  the two profiles are of different devices: /device:TPU:10 before, /device:TPU:0 now
where the time goes in v4:
time: 158 us; the launch traced here: 157 us
  waiting for transfers between devices  56.6 us (36%)
  Pallas kernels  47.9 us (30%)
  starting transfers between devices  46.1 us (29%)
  other arithmetic  2.73 us (2%)
  local copies, waits for them, and re-layouts  2.41 us (2%)
  between operations  1.63 us (1%)
    ppermute x5, waiting for transfers between devices, swap_beside(): return lax.ppermute(both, 'dp', BESIDE)  27.4 us
    ppermute x18, starting transfers between devices, to_peer(): return lax.ppermute(array, 'space', [(i, i ^ k) for i in range(spaces)])  21.4 us
    ppermute x18, waiting for transfers between devices, to_peer(): return lax.ppermute(array, 'space', [(i, i ^ k) for i in range(spaces)])  19.1 us
    pallas_call x5, Pallas kernels, mix(): pl.pallas_call(functools.partial(mix_kernel, offset, other_offset), in_sp...  17 us
    ppermute x5, starting transfers between devices, swap_opposite(): return lax.ppermute(total, 'dp', OPPOSITE)  13.5 us
    ppermute x5, waiting for transfers between devices, swap_opposite(): return lax.ppermute(total, 'dp', OPPOSITE)  8.64 us
    pallas_call x1, Pallas kernels, peer_frames(): pl.pallas_call(functools.partial(peer_frames_kernel, own, wig_rows), in_s...  7.18 us
    pallas_call x3, Pallas kernels, apply_weights(): pl.pallas_call(functools.partial(apply_kernel, group, places, width // sp...  6.66 us
  transfers between devices with their start and end apart: 35, of which 16 were waited for; matrix products, arithmetic and copies ran while one was open for 2% of the time, Pallas kernels for 27%

profile of v4, /device:TPU:0, one launch (start us, length us, event | category | flops | bytes accessed | tf_op | source)
XLA Modules:
  0.0 157.3 jit_solution(6667107725869249474)
XLA Ops:
  5.6 2.8 %mix.5 = (bf16[224,896]{1,0:T(8,128)(2,1)S(1)}, bf16[112,896]{1,0:T(8,128)(2,1)S(1)}, bf16[112,896]{1,0:T(8,128)(2,1)S(1)}) custom-call(s32[2]{0:T(128)S(1)} %pad_add_fusion.place_ref, f32[8,32]{1,0:T(8,128)S(1)} %copy-done.4, bf16[4,224,896]{2,1,0:T(8,128)(2,1)} %own_ref.3, bf16[4,224,896]{2,1,0:T(8,128)(2,1)S(1)} %collective-permute-done.other_ref), custom_call_target="tpu_custom_call" | custom-call | tf_op jit(solution)/shard_map/mix/pallas_call | solution.py:114
  8.4 2.8 %collective-permute-start.1 = (bf16[224,896]{1,0:T(8,128)(2,1)S(1)}, bf16[224,896]{1,0:T(8,128)(2,1)S(1)}, u32[]{:S(2)}, u32[]{:S(2)}) collective-permute-start(bf16[224,896]{1,0:T(8,128)(2,1)S(1)} %get-tuple-element.108), channel_id=1, source_target_pairs={{0,8},{4,12},{8,0},{12,4},{16,24},{20,28},{24,16},{28,20},{1,9},{5... | collective-permute-start | bytes 1204232 | tf_op jit(solution)/shard_map/ppermute | solution.py:645
  14.1 4.9 %mix.6 = (bf16[640,640]{1,0:T(8,128)(2,1)}, bf16[320,640]{1,0:T(8,128)(2,1)S(1)}, bf16[320,640]{1,0:T(8,128)(2,1)S(1)}) custom-call(s32[2]{0:T(128)S(1)} %pad_add_fusion.place_ref, f32[8,32]{1,0:T(8,128)S(1)} %copy-done.4, bf16[4,320,640]{2,1,0:T(8,128)(2,1)} %bitcast.20, bf16[4,320,640]{2,1,0:T(8,128)(2,1)S(1)} %collective-permute-done.2.other_ref), custom_call_target="tpu_custom_call" | custom-call | tf_op jit(solution)/shard_map/mix/pallas_call | solution.py:114
  26.8 6.0 %enter_frame.1 = (bf16[128,3712]{1,0:T(8,128)(2,1)S(1)}, bf16[128,3712]{1,0:T(8,128)(2,1)S(1)}, bf16[928,128]{1,0:T(8,128)(2,1)S(1)}, bf16[928,128]{1,0:T(8,128)...) custom-call(s32[2]{0:T(128)S(1)} %pad_add_fusion.place_ref, s32[1,1]{1,0:T(1,128)S(6)} %copy.16.count_ref, ...), custom_call_target="tpu_custom_call" | custom-call | tf_op jit(solution)/shard_map/enter_frame/pallas_call | solution.py:263
  32.8 3.4 %collective-permute-done.7.refs_1_ = bf16[2048,128]{1,0:T(8,128)(2,1)S(1)} collective-permute-done((bf16[2048,128]{1,0:T(8,128)(2,1)S(1)}, bf16[2048,128]{1,0:T(8,128)(2,1)S(1)}, u32[]{:S(2)}, u32[]{:S(2)}) %collective-permute-start.7) | collective-permute-done | bytes 524320 | tf_op jit(solution)/shard_map/ppermute | solution.py:581
  39.0 3.6 %collective-permute-start.9 = (bf16[112,896]{1,0:T(8,128)(2,1)S(1)}, bf16[112,896]{1,0:T(8,128)(2,1)S(1)}, u32[]{:S(2)}, u32[]{:S(2)}) collective-permute-start(bf16[112,896]{1,0:T(8,128)(2,1)S(1)} %add_convert_fusion.7), channel_id=1, source_target_pairs={{0,24},{4,28},{8,16},{12,20},{16,8},{20,12},{24,0},{28,4},{1,25},{... | collective-permute-start | bytes 602120 | tf_op jit(solution)/shard_map/ppermute | solution.py:651
  44.7 3.2 %mix.8 = (bf16[384,768]{1,0:T(8,128)(2,1)S(1)}, bf16[192,768]{1,0:T(8,128)(2,1)S(1)}, bf16[192,768]{1,0:T(8,128)(2,1)S(1)}) custom-call(s32[2]{0:T(128)S(1)} %pad_add_fusion.place_ref, f32[8,32]{1,0:T(8,128)S(1)} %copy-done.4, bf16[4,384,768]{2,1,0:T(8,128)(2,1)} %bitcast.17, bf16[4,384,768]{2,1,0:T(8,128)(2,1)S(1)} %collective-permute-done.5.other_ref), custom_call_target="tpu_custom_call" | custom-call | tf_op jit(solution)/shard_map/mix/pallas_call | solution.py:114
  47.9 3.2 %mix.7 = (bf16[384,768]{1,0:T(8,128)(2,1)S(1)}, bf16[192,768]{1,0:T(8,128)(2,1)S(1)}, bf16[192,768]{1,0:T(8,128)(2,1)S(1)}) custom-call(s32[2]{0:T(128)S(1)} %pad_add_fusion.place_ref, f32[8,32]{1,0:T(8,128)S(1)} %copy-done.4, bf16[4,384,768]{2,1,0:T(8,128)(2,1)} %bitcast.18, bf16[4,384,768]{2,1,0:T(8,128)(2,1)S(1)} %collective-permute-done.5.other_ref), custom_call_target="tpu_custom_call" | custom-call | tf_op jit(solution)/shard_map/mix/pallas_call | solution.py:114
  53.4 7.2 %peer_frames.1.backs = bf16[3,128,3712]{2,1,0:T(8,128)(2,1)S(1)} custom-call(bf16[2048,128]{1,0:T(8,128)(2,1)S(1)} %collective-permute-done.6.refs_0_, bf16[2048,128]{1,0:T(8,128)(2,1)S(1)} %collective-permute-done.7.refs_1_, bf16[2048,128]{1,0:T(8,128)(2,1)S(1)} %collective-permute-done.10.refs_2_), custom_call_target="tpu_custom_call" | custom-call | tf_op jit(solution)/shard_map/peer_frames/pallas_call | solution.py:300
  62.3 3.7 %collective-permute-start.16 = (bf16[320,640]{1,0:T(8,128)(2,1)S(1)}, bf16[320,640]{1,0:T(8,128)(2,1)S(1)}, u32[]{:S(2)}, u32[]{:S(2)}) collective-permute-start(bf16[320,640]{1,0:T(8,128)(2,1)S(1)} %add_convert_fusion), channel_id=1, source_target_pairs={{0,24},{4,28},{8,16},{12,20},{16,8},{20,12},{24,0},{28,4},{1,25},{... | collective-permute-start | bytes 1228808 | tf_op jit(solution)/shard_map/ppermute | solution.py:651
  65.9 3.0 %mix.9 = (bf16[224,896]{1,0:T(8,128)(2,1)S(1)}, bf16[112,896]{1,0:T(8,128)(2,1)S(1)}, bf16[112,896]{1,0:T(8,128)(2,1)S(1)}) custom-call(s32[2]{0:T(128)S(1)} %pad_add_fusion.place_ref, f32[8,32]{1,0:T(8,128)S(1)} %copy-done.4, bf16[4,224,896]{2,1,0:T(8,128)(2,1)} %own_ref.3, bf16[4,224,896]{2,1,0:T(8,128)(2,1)S(1)} %collective-permute-done.other_ref), custom_call_target="tpu_custom_call" | custom-call | tf_op jit(solution)/shard_map/mix/pallas_call | solution.py:114
  68.9 4.8 %collective-permute-done.13 = bf16[384,768]{1,0:T(8,128)(2,1)} collective-permute-done((bf16[384,768]{1,0:T(8,128)(2,1)S(1)}, bf16[384,768]{1,0:T(8,128)(2,1)}, u32[]{:S(2)}, u32[]{:S(2)}) %collective-permute-start.13) | collective-permute-done | bytes 589856 | tf_op jit(solution)/shard_map/ppermute | solution.py:645
  73.7 2.9 %collective-permute-done.16.refs_5_ = bf16[320,640]{1,0:T(8,128)(2,1)S(1)} collective-permute-done((bf16[320,640]{1,0:T(8,128)(2,1)S(1)}, bf16[320,640]{1,0:T(8,128)(2,1)S(1)}, u32[]{:S(2)}, u32[]{:S(2)}) %collective-permute-start.16) | collective-permute-done | bytes 409632 | tf_op jit(solution)/shard_map/ppermute | solution.py:651
  79.9 3.7 %collective-permute-start.18 = (bf16[192,768]{1,0:T(8,128)(2,1)S(1)}, bf16[192,768]{1,0:T(8,128)(2,1)S(1)}, u32[]{:S(2)}, u32[]{:S(2)}) collective-permute-start(bf16[192,768]{1,0:T(8,128)(2,1)S(1)} %add_convert_fusion.4), channel_id=1, source_target_pairs={{0,24},{4,28},{8,16},{12,20},{16,8},{20,12},{24,0},{28,4},{1,25},{... | collective-permute-start | bytes 884744 | tf_op jit(solution)/shard_map/ppermute | solution.py:651
  83.6 11.3 %collective-permute-done.15 = bf16[384,768]{1,0:T(8,128)(2,1)S(1)} collective-permute-done((bf16[384,768]{1,0:T(8,128)(2,1)S(1)}, bf16[384,768]{1,0:T(8,128)(2,1)S(1)}, u32[]{:S(2)}, u32[]{:S(2)}) %collective-permute-start.15) | collective-permute-done | bytes 589856 | tf_op jit(solution)/shard_map/ppermute | solution.py:645
  99.5 9.5 %collective-permute-done.17 = bf16[224,896]{1,0:T(8,128)(2,1)S(1)} collective-permute-done((bf16[224,896]{1,0:T(8,128)(2,1)S(1)}, bf16[224,896]{1,0:T(8,128)(2,1)S(1)}, u32[]{:S(2)}, u32[]{:S(2)}) %collective-permute-start.17) | collective-permute-done | bytes 401440 | tf_op jit(solution)/shard_map/ppermute | solution.py:645
  109.6 2.5 %collective-permute-start.21 = (bf16[112,896]{1,0:T(8,128)(2,1)S(1)}, bf16[112,896]{1,0:T(8,128)(2,1)S(1)}, u32[]{:S(2)}, u32[]{:S(2)}) collective-permute-start(bf16[112,896]{1,0:T(8,128)(2,1)S(1)} %add_convert_fusion.6), channel_id=1, source_target_pairs={{0,24},{4,28},{8,16},{12,20},{16,8},{20,12},{24,0},{28,4},{1,25},{... | collective-permute-start | bytes 602120 | tf_op jit(solution)/shard_map/ppermute | solution.py:651
  112.1 5.1 %collective-permute-done.21 = bf16[112,896]{1,0:T(8,128)(2,1)S(1)} collective-permute-done((bf16[112,896]{1,0:T(8,128)(2,1)S(1)}, bf16[112,896]{1,0:T(8,128)(2,1)S(1)}, u32[]{:S(2)}, u32[]{:S(2)}) %collective-permute-start.21) | collective-permute-done | bytes 200736 | tf_op jit(solution)/shard_map/ppermute | solution.py:651
  117.7 3.4 %weight_grads.1 = (bf16[224,896]{1,0:T(8,128)(2,1)}, bf16[2,192,768]{2,1,0:T(8,128)(2,1)}, bf16[2,160,640]{2,1,0:T(8,128)(2,1)}) custom-call(bf16[128,3712]{1,0:T(8,128)(2,1)S(1)} %get-tuple-element.168.back_ref, bf16[3,128,3712]{2,1,0:T(8,128)(2,1)S(1)} %peer_frames.1.backs, bf16[928,128]{1,0:T(8,128)(2,1)S(1)} %get-tuple-element.170.refs_0_, ...), custom_call_target="tpu_custom_call" | custom-call | tf_op jit(solution)/shard_map/weight_grads/pallas_call | solution.py:336
  123.3 2.7 %collective-permute-start.32 = (bf16[112,896]{1,0:T(8,128)(2,1)S(1)}, bf16[112,896]{1,0:T(8,128)(2,1)S(1)}, u32[]{:S(2)}, u32[]{:S(2)}) collective-permute-start(bf16[112,896]{1,0:T(8,128)(2,1)S(1)} %add_convert_fusion.5.refs_4_), channel_id=1, source_target_pairs={{0,3},{1,2},{2,1},{3,0},{4,7},{5,6},{6,5},{7,4},{8,11},{9,10},{10,... | collective-permute-start | bytes 602120 | tf_op jit(solution)/shard_map/ppermute | solution.py:581
  126.3 5.1 %collective-permute-done.27.refs_6_ = bf16[192,768]{1,0:T(8,128)(2,1)S(1)} collective-permute-done((bf16[192,768]{1,0:T(8,128)(2,1)S(1)}, bf16[192,768]{1,0:T(8,128)(2,1)S(1)}, u32[]{:S(2)}, u32[]{:S(2)}) %collective-permute-start.27) | collective-permute-done | bytes 294944 | tf_op jit(solution)/shard_map/ppermute | solution.py:581
  137.7 5.3 %collective-permute-done.28.refs_7_ = bf16[192,768]{1,0:T(8,128)(2,1)S(1)} collective-permute-done((bf16[192,768]{1,0:T(8,128)(2,1)S(1)}, bf16[192,768]{1,0:T(8,128)(2,1)S(1)}, u32[]{:S(2)}, u32[]{:S(2)}) %collective-permute-start.28) | collective-permute-done | bytes 294944 | tf_op jit(solution)/shard_map/ppermute | solution.py:581
  143.0 2.7 %apply_weights_1.1 = (bf16[1536,128]{1,0:T(8,128)(2,1)S(1)}, bf16[1536,128]{1,0:T(8,128)(2,1)S(1)}) custom-call(s32[2]{0:T(128)S(1)} %pad_add_fusion.place_ref, bf16[128,3712]{1,0:T(8,128)(2,1)S(1)} %get-tuple-element.185.frame_ref, bf16[128,3712]{1,0:T(8,128)(2,1)S(1)} %get-tuple-element.168.back_ref, bf16[192,768]{1,0:T(8,128)(2,1)S(1)} %add_convert_fusion.3.refs_0_, ...), custom_call_target="tpu_custom_call" | custom-call | tf_op jit(solution)/shard_map/apply_weights_1/pallas_call | solution.py:402
  152.9 2.9 %leave_frame.1 = bf16[32,6272]{1,0:T(8,128)(2,1)} custom-call(bf16[896,128]{1,0:T(8,128)(2,1)S(1)} %get-tuple-element.192.zero_ref, bf16[1536,128]{1,0:T(8,128)(2,1)S(1)} %get-tuple-element.193.one_ref, bf16[1280,128]{1,0:T(8,128)(2,1)S(1)} %get-tuple-element.194.two_ref, bf16[455,128]{1,0:T(8,128)(2,1)S(1)} %copy-done.3, s32[1,1]{1,0:T(1,128)S(6)} %copy.16.count_ref, ...), custom_call_target="tpu_custom_call" | custom-call | tf_op jit(solution)/shard_map/leave_frame/pallas_call | solution.py:525
  (92 shorter events, 50.2 us)
Async XLA Ops:
  21.0 21.6 %collective-permute-start.5 = (bf16[4,384,768]{2,1,0:T(8,128)(2,1)}, bf16[4,384,768]{2,1,0:T(8,128)(2,1)S(1)}, u32[]{:S(2)}, u32[]{:S(2)}) collective-permute-start(bf16[4,384,768]{2,1,0:T(8,128)(2,1)} %bitcast.16), channel_id=1, source_target_pairs={{0,4},{4,0},{8,12},{12,8},{16,20},{20,16},{24,28},{28,24},{1,5},{5... | collective-permute-start | bytes 7077896 | tf_op jit(solution)/shard_map/ppermute | solution.py:638
  21.8 14.4 %collective-permute-start.7 = (bf16[2048,128]{1,0:T(8,128)(2,1)S(1)}, bf16[2048,128]{1,0:T(8,128)(2,1)S(1)}, u32[]{:S(2)}, u32[]{:S(2)}) collective-permute-start(bf16[2048,128]{1,0:T(8,128)(2,1)S(1)} %pack_inputs.1), channel_id=1, source_target_pairs={{0,2},{1,3},{2,0},{3,1},{4,6},{5,7},{6,4},{7,5},{8,10},{9,11},{10,... | collective-permute-start | bytes 1572872 | tf_op jit(solution)/shard_map/ppermute | solution.py:581
  23.5 14.1 %collective-permute-start.6 = (bf16[2048,128]{1,0:T(8,128)(2,1)S(1)}, bf16[2048,128]{1,0:T(8,128)(2,1)S(1)}, u32[]{:S(2)}, u32[]{:S(2)}) collective-permute-start(bf16[2048,128]{1,0:T(8,128)(2,1)S(1)} %pack_inputs.1), channel_id=1, source_target_pairs={{0,1},{1,0},{2,3},{3,2},{4,5},{5,4},{6,7},{7,6},{8,9},{9,8},{10,11... | collective-permute-start | bytes 1572872 | tf_op jit(solution)/shard_map/ppermute | solution.py:581
  25.1 35.5 %collective-permute-start.8 = (bf16[640,640]{1,0:T(8,128)(2,1)}, bf16[640,640]{1,0:T(8,128)(2,1)S(1)}, u32[]{:S(2)}, u32[]{:S(2)}) collective-permute-start(bf16[640,640]{1,0:T(8,128)(2,1)} %get-tuple-element.128), channel_id=1, source_target_pairs={{0,8},{4,12},{8,0},{12,4},{16,24},{20,28},{24,16},{28,20},{1,9},{5... | collective-permute-start | bytes 2457608 | tf_op jit(solution)/shard_map/ppermute | solution.py:645
  37.6 15.8 %collective-permute-start.10 = (bf16[2048,128]{1,0:T(8,128)(2,1)S(1)}, bf16[2048,128]{1,0:T(8,128)(2,1)S(1)}, u32[]{:S(2)}, u32[]{:S(2)}) collective-permute-start(bf16[2048,128]{1,0:T(8,128)(2,1)S(1)} %pack_inputs.1), channel_id=1, source_target_pairs={{0,3},{1,2},{2,1},{3,0},{4,7},{5,6},{6,5},{7,4},{8,11},{9,10},{10,... | collective-permute-start | bytes 1572872 | tf_op jit(solution)/shard_map/ppermute | solution.py:581
  42.6 18.0 %collective-permute-start.11 = (bf16[928,128]{1,0:T(8,128)(2,1)}, bf16[928,128]{1,0:T(8,128)(2,1)S(1)}, u32[]{:S(2)}, u32[]{:S(2)}) collective-permute-start(bf16[928,128]{1,0:T(8,128)(2,1)} %get-tuple-element.141), channel_id=1, source_target_pairs={{0,1},{1,0},{2,3},{3,2},{4,5},{5,4},{6,7},{7,6},{8,9},{9,8},{10,11... | collective-permute-start | bytes 712712 | tf_op jit(solution)/shard_map/ppermute | solution.py:581
  43.2 17.4 %collective-permute-start.12 = (bf16[928,128]{1,0:T(8,128)(2,1)S(1)}, bf16[928,128]{1,0:T(8,128)(2,1)S(1)}, u32[]{:S(2)}, u32[]{:S(2)}) collective-permute-start(bf16[928,128]{1,0:T(8,128)(2,1)S(1)} %get-tuple-element.142), channel_id=1, source_target_pairs={{0,2},{1,3},{2,0},{3,1},{4,6},{5,7},{6,4},{7,5},{8,10},{9,11},{10,... | collective-permute-start | bytes 712712 | tf_op jit(solution)/shard_map/ppermute | solution.py:581
  51.8 21.9 %collective-permute-start.13 = (bf16[384,768]{1,0:T(8,128)(2,1)S(1)}, bf16[384,768]{1,0:T(8,128)(2,1)}, u32[]{:S(2)}, u32[]{:S(2)}) collective-permute-start(bf16[384,768]{1,0:T(8,128)(2,1)S(1)} %get-tuple-element.148), channel_id=1, source_target_pairs={{0,8},{4,12},{8,0},{12,4},{16,24},{20,28},{24,16},{28,20},{1,9},{5... | collective-permute-start | bytes 1769480 | tf_op jit(solution)/shard_map/ppermute | solution.py:645
  62.3 14.3 %collective-permute-start.16 = (bf16[320,640]{1,0:T(8,128)(2,1)S(1)}, bf16[320,640]{1,0:T(8,128)(2,1)S(1)}, u32[]{:S(2)}, u32[]{:S(2)}) collective-permute-start(bf16[320,640]{1,0:T(8,128)(2,1)S(1)} %add_convert_fusion), channel_id=1, source_target_pairs={{0,24},{4,28},{8,16},{12,20},{16,8},{20,12},{24,0},{28,4},{1,25},{... | collective-permute-start | bytes 1228808 | tf_op jit(solution)/shard_map/ppermute | solution.py:651
  73.7 21.1 %collective-permute-start.15 = (bf16[384,768]{1,0:T(8,128)(2,1)S(1)}, bf16[384,768]{1,0:T(8,128)(2,1)S(1)}, u32[]{:S(2)}, u32[]{:S(2)}) collective-permute-start(bf16[384,768]{1,0:T(8,128)(2,1)S(1)} %get-tuple-element.151), channel_id=1, source_target_pairs={{0,8},{4,12},{8,0},{12,4},{16,24},{20,28},{24,16},{28,20},{1,9},{5... | collective-permute-start | bytes 1769480 | tf_op jit(solution)/shard_map/ppermute | solution.py:645
  76.8 19.3 %collective-permute-start.20 = (bf16[2384,128]{1,0:T(8,128)(2,1)S(1)}, bf16[2384,128]{1,0:T(8,128)(2,1)S(1)}, u32[]{:S(2)}, u32[]{:S(2)}) collective-permute-start(bf16[2384,128]{1,0:T(8,128)(2,1)S(1)} %finish_first.1.refs_0_), channel_id=1, source_target_pairs={{0,2},{1,3},{2,0},{3,1},{4,6},{5,7},{6,4},{7,5},{8,10},{9,11},{10,... | collective-permute-start | bytes 1830920 | tf_op jit(solution)/shard_map/ppermute | solution.py:581
  78.4 17.8 %collective-permute-start.19 = (bf16[2384,128]{1,0:T(8,128)(2,1)S(1)}, bf16[2384,128]{1,0:T(8,128)(2,1)S(1)}, u32[]{:S(2)}, u32[]{:S(2)}) collective-permute-start(bf16[2384,128]{1,0:T(8,128)(2,1)S(1)} %finish_first.1.refs_0_), channel_id=1, source_target_pairs={{0,1},{1,0},{2,3},{3,2},{4,5},{5,4},{6,7},{7,6},{8,9},{9,8},{10,11... | collective-permute-start | bytes 1830920 | tf_op jit(solution)/shard_map/ppermute | solution.py:581
  79.9 15.1 %collective-permute-start.18 = (bf16[192,768]{1,0:T(8,128)(2,1)S(1)}, bf16[192,768]{1,0:T(8,128)(2,1)S(1)}, u32[]{:S(2)}, u32[]{:S(2)}) collective-permute-start(bf16[192,768]{1,0:T(8,128)(2,1)S(1)} %add_convert_fusion.4), channel_id=1, source_target_pairs={{0,24},{4,28},{8,16},{12,20},{16,8},{20,12},{24,0},{28,4},{1,25},{... | collective-permute-start | bytes 884744 | tf_op jit(solution)/shard_map/ppermute | solution.py:651
  94.8 14.2 %collective-permute-start.17 = (bf16[224,896]{1,0:T(8,128)(2,1)S(1)}, bf16[224,896]{1,0:T(8,128)(2,1)S(1)}, u32[]{:S(2)}, u32[]{:S(2)}) collective-permute-start(bf16[224,896]{1,0:T(8,128)(2,1)S(1)} %get-tuple-element.159), channel_id=1, source_target_pairs={{0,8},{4,12},{8,0},{12,4},{16,24},{20,28},{24,16},{28,20},{1,9},{5... | collective-permute-start | bytes 1204232 | tf_op jit(solution)/shard_map/ppermute | solution.py:645
  94.9 14.2 %collective-permute-start.25 = (bf16[192,768]{1,0:T(8,128)(2,1)S(1)}, bf16[192,768]{1,0:T(8,128)(2,1)S(1)}, u32[]{:S(2)}, u32[]{:S(2)}) collective-permute-start(bf16[192,768]{1,0:T(8,128)(2,1)S(1)} %add_convert_fusion.2), channel_id=1, source_target_pairs={{0,24},{4,28},{8,16},{12,20},{16,8},{20,12},{24,0},{28,4},{1,25},{... | collective-permute-start | bytes 884744 | tf_op jit(solution)/shard_map/ppermute | solution.py:651
  96.1 25.0 %collective-permute-start.23 = (bf16[192,768]{1,0:T(8,128)(2,1)S(1)}, bf16[192,768]{1,0:T(8,128)(2,1)S(1)}, u32[]{:S(2)}, u32[]{:S(2)}) collective-permute-start(bf16[192,768]{1,0:T(8,128)(2,1)S(1)} %add_convert_fusion.3.refs_0_), channel_id=1, source_target_pairs={{0,2},{1,3},{2,0},{3,1},{4,6},{5,7},{6,4},{7,5},{8,10},{9,11},{10,... | collective-permute-start | bytes 884744 | tf_op jit(solution)/shard_map/ppermute | solution.py:581
  97.5 23.6 %collective-permute-start.22 = (bf16[192,768]{1,0:T(8,128)(2,1)S(1)}, bf16[192,768]{1,0:T(8,128)(2,1)S(1)}, u32[]{:S(2)}, u32[]{:S(2)}) collective-permute-start(bf16[192,768]{1,0:T(8,128)(2,1)S(1)} %add_convert_fusion.3.refs_0_), channel_id=1, source_target_pairs={{0,1},{1,0},{2,3},{3,2},{4,5},{5,4},{6,7},{7,6},{8,9},{9,8},{10,11... | collective-permute-start | bytes 884744 | tf_op jit(solution)/shard_map/ppermute | solution.py:581
  98.0 28.0 %collective-permute-start.29 = (bf16[2384,128]{1,0:T(8,128)(2,1)S(1)}, bf16[2384,128]{1,0:T(8,128)(2,1)S(1)}, u32[]{:S(2)}, u32[]{:S(2)}) collective-permute-start(bf16[2384,128]{1,0:T(8,128)(2,1)S(1)} %collective-permute-done.20.refs_2_), channel_id=1, source_target_pairs={{0,1},{1,0},{2,3},{3,2},{4,5},{5,4},{6,7},{7,6},{8,9},{9,8},{10,11... | collective-permute-start | bytes 1830920 | tf_op jit(solution)/shard_map/ppermute | solution.py:581
  117.2 14.2 %collective-permute-start.27 = (bf16[192,768]{1,0:T(8,128)(2,1)S(1)}, bf16[192,768]{1,0:T(8,128)(2,1)S(1)}, u32[]{:S(2)}, u32[]{:S(2)}) collective-permute-start(bf16[192,768]{1,0:T(8,128)(2,1)S(1)} %add_convert_fusion.1.refs_4_), channel_id=1, source_target_pairs={{0,2},{1,3},{2,0},{3,1},{4,6},{5,7},{6,4},{7,5},{8,10},{9,11},{10,... | collective-permute-start | bytes 884744 | tf_op jit(solution)/shard_map/ppermute | solution.py:581
  121.2 16.6 %collective-permute-start.24 = (bf16[192,768]{1,0:T(8,128)(2,1)S(1)}, bf16[192,768]{1,0:T(8,128)(2,1)S(1)}, u32[]{:S(2)}, u32[]{:S(2)}) collective-permute-start(bf16[192,768]{1,0:T(8,128)(2,1)S(1)} %collective-permute-done.22.refs_1_), channel_id=1, source_target_pairs={{0,2},{1,3},{2,0},{3,1},{4,6},{5,7},{6,4},{7,5},{8,10},{9,11},{10,... | collective-permute-start | bytes 884744 | tf_op jit(solution)/shard_map/ppermute | solution.py:581
  122.7 20.3 %collective-permute-start.28 = (bf16[192,768]{1,0:T(8,128)(2,1)S(1)}, bf16[192,768]{1,0:T(8,128)(2,1)S(1)}, u32[]{:S(2)}, u32[]{:S(2)}) collective-permute-start(bf16[192,768]{1,0:T(8,128)(2,1)S(1)} %collective-permute-done.26.refs_5_), channel_id=1, source_target_pairs={{0,2},{1,3},{2,0},{3,1},{4,6},{5,7},{6,4},{7,5},{8,10},{9,11},{10,... | collective-permute-start | bytes 884744 | tf_op jit(solution)/shard_map/ppermute | solution.py:581
  123.3 22.4 %collective-permute-start.32 = (bf16[112,896]{1,0:T(8,128)(2,1)S(1)}, bf16[112,896]{1,0:T(8,128)(2,1)S(1)}, u32[]{:S(2)}, u32[]{:S(2)}) collective-permute-start(bf16[112,896]{1,0:T(8,128)(2,1)S(1)} %add_convert_fusion.5.refs_4_), channel_id=1, source_target_pairs={{0,3},{1,2},{2,1},{3,0},{4,7},{5,6},{6,5},{7,4},{8,11},{9,10},{10,... | collective-permute-start | bytes 602120 | tf_op jit(solution)/shard_map/ppermute | solution.py:581
  126.0 19.7 %collective-permute-start.31 = (bf16[112,896]{1,0:T(8,128)(2,1)S(1)}, bf16[112,896]{1,0:T(8,128)(2,1)S(1)}, u32[]{:S(2)}, u32[]{:S(2)}) collective-permute-start(bf16[112,896]{1,0:T(8,128)(2,1)S(1)} %add_convert_fusion.5.refs_4_), channel_id=1, source_target_pairs={{0,2},{1,3},{2,0},{3,1},{4,6},{5,7},{6,4},{7,5},{8,10},{9,11},{10,... | collective-permute-start | bytes 602120 | tf_op jit(solution)/shard_map/ppermute | solution.py:581
  131.4 14.3 %collective-permute-start.30 = (bf16[112,896]{1,0:T(8,128)(2,1)S(1)}, bf16[112,896]{1,0:T(8,128)(2,1)S(1)}, u32[]{:S(2)}, u32[]{:S(2)}) collective-permute-start(bf16[112,896]{1,0:T(8,128)(2,1)S(1)} %add_convert_fusion.5.refs_4_), channel_id=1, source_target_pairs={{0,1},{1,0},{2,3},{3,2},{4,5},{5,4},{6,7},{7,6},{8,9},{9,8},{10,11... | collective-permute-start | bytes 602120 | tf_op jit(solution)/shard_map/ppermute | solution.py:581
  (20 other events, 159.6 us)

commit v5 on v4

--- a/solution.py
+++ b/solution.py
@@ -693,11 +693,10 @@
         other2, frame = together(other2, frame)
         both2, across2, here2 = mix_chunk(2, other2)
         both3, across3, here3 = mix_chunk(3, other2, rows_one)
-        both2, here2, here3, opposite0 = together(both2, here2, here3, opposite0)
         beside2 = swap_beside(both2)
         here3, raws[2] = together(here3, raws[2])
         backs = peer_frames(raws, own_rows, wigner.shape[0])
-        beside1, here2, here3, backs = together(beside1, here2, here3, backs)
+        beside1, here2, here3, backs, opposite0 = together(beside1, here2, here3, backs, opposite0)
         beside1, *slabs[1:] = together(beside1, *slabs[1:])
         slabs[3] = to_peer(slabs[3], spaces, 3)
         total1 = total_opposite(1, across1, beside1)
@@ -724,21 +723,20 @@
         opposite4 = swap_opposite(total4)
         opposite3, total4 = together(opposite3, total4)
         shard3 = total_here(3, here3, beside3, opposite3)
+        shard3, *sides2 = together(shard3, *sides2)
         sides3 = to_sides(shard3)
-        late_back, beside4 = together(back, beside4)
-        grad_mix = weight_grads(late_back, backs, slabs, scale)
-        opposite4, *grad_mix = together(opposite4, *grad_mix)
-        opposite4, *sides2 = together(opposite4, *sides2)
-        shard4 = total_here(4, here4, beside4, opposite4)
-        sides4 = to_sides(shard4)
         forward2 = forward(2, sides2)
         shard4 = total_here(4, here4, beside4, opposite4)
         sides4 = to_sides(shard4)
+        last4 = to_peer(shard4, spaces, 3)
+        late_back, shard4 = together(back, shard4)
+        grad_mix = weight_grads(late_back, backs, slabs, scale)
+        shard4, *sides3 = together(shard4, *sides3)
         outs, grads = {}, {}
         whole = {
             3: pieces(1, shard1, sides1, forward1, half * BLOCK_COUNTS[0]),
             1: pieces(2, shard2, sides2, forward2) + pieces(3, shard3, sides3, forward(3, sides3)),
-            0: pieces(0, shard1, sides1, forward1, 0) + pieces(4, shard4, sides4, to_peer(shard4, spaces, 3)),
+            0: pieces(0, shard1, sides1, forward1, 0) + pieces(4, shard4, sides4, last4),
         }
     else:
         from_prev = lax.ppermute(to_next, "space", up)
@@ -763,7 +761,7 @@
 
     for group, pieces_of in whole.items():
         if group == 0:
-            frame, grads[1] = together(frame, grads[1])
+            frame, grads[1], *grad_mix = together(frame, grads[1], *grad_mix)
         outs[group], grads[group] = apply_weights(group, place, frame, back, pieces_of, spaces)
     base, returning = leave_back(
         [grads[g] for g in (0, 1, 3)], wigner, sources, grad_out, 2 * ghosts

time: 158 us -> 153 us (0.968)
  starting transfers between devices: 46.1 us -> 41.5 us
    ppermute x5, waiting for transfers between devices: 27.4 us -> 17.6 us  [swap_beside(): return lax.ppermute(both, 'dp', BESIDE)]
    ppermute x5, waiting for transfers between devices: 8.64 us -> 17.5 us  [swap_opposite(): return lax.ppermute(total, 'dp', OPPOSITE)]
    ppermute x5, starting transfers between devices: 13.5 us -> 8.38 us  [swap_opposite(): return lax.ppermute(total, 'dp', OPPOSITE)]
  transfers between devices with their start and end apart: 35 -> 35, of which waited for: 16 -> 15; matrix products, arithmetic and copies ran while one was open for 2% -> 2% of each run, Pallas kernels for 27% -> 28%
where the time goes in v5:
time: 153 us; the launch traced here: 152 us
  waiting for transfers between devices  55.4 us (36%)
  Pallas kernels  47.9 us (31%)
  starting transfers between devices  41.5 us (27%)
  other arithmetic  3.4 us (2%)
  local copies, waits for them, and re-layouts  2.41 us (2%)
  between operations  1.66 us (1%)
    ppermute x18, starting transfers between devices, to_peer(): return lax.ppermute(array, 'space', [(i, i ^ k) for i in range(spaces)])  20.3 us
    ppermute x18, waiting for transfers between devices, to_peer(): return lax.ppermute(array, 'space', [(i, i ^ k) for i in range(spaces)])  19.3 us
    ppermute x5, waiting for transfers between devices, swap_beside(): return lax.ppermute(both, 'dp', BESIDE)  17.6 us
    ppermute x5, waiting for transfers between devices, swap_opposite(): return lax.ppermute(total, 'dp', OPPOSITE)  17.5 us
    pallas_call x5, Pallas kernels, mix(): pl.pallas_call(functools.partial(mix_kernel, offset, other_offset), in_sp...  17 us
    ppermute x5, starting transfers between devices, swap_opposite(): return lax.ppermute(total, 'dp', OPPOSITE)  8.38 us
    pallas_call x1, Pallas kernels, peer_frames(): pl.pallas_call(functools.partial(peer_frames_kernel, own, wig_rows), in_s...  7.19 us
    pallas_call x3, Pallas kernels, apply_weights(): pl.pallas_call(functools.partial(apply_kernel, group, places, width // sp...  6.66 us
  transfers between devices with their start and end apart: 35, of which 15 were waited for; matrix products, arithmetic and copies ran while one was open for 2% of the time, Pallas kernels for 28%

profile of v5, /device:TPU:0, one launch (start us, length us, event | category | flops | bytes accessed | tf_op | source)
XLA Modules:
  0.0 152.2 jit_solution(15204146739262053223)
XLA Ops:
  5.6 2.8 %mix.5 = (bf16[224,896]{1,0:T(8,128)(2,1)S(1)}, bf16[112,896]{1,0:T(8,128)(2,1)S(1)}, bf16[112,896]{1,0:T(8,128)(2,1)S(1)}) custom-call(s32[2]{0:T(128)S(1)} %pad_add_fusion.place_ref, f32[8,32]{1,0:T(8,128)S(1)} %copy-done.4, bf16[4,224,896]{2,1,0:T(8,128)(2,1)} %own_ref.3, bf16[4,224,896]{2,1,0:T(8,128)(2,1)S(1)} %collective-permute-done.other_ref), custom_call_target="tpu_custom_call" | custom-call | tf_op jit(solution)/shard_map/mix/pallas_call | solution.py:114
  8.4 2.8 %collective-permute-start.1 = (bf16[224,896]{1,0:T(8,128)(2,1)S(1)}, bf16[224,896]{1,0:T(8,128)(2,1)S(1)}, u32[]{:S(2)}, u32[]{:S(2)}) collective-permute-start(bf16[224,896]{1,0:T(8,128)(2,1)S(1)} %get-tuple-element.107), channel_id=1, source_target_pairs={{0,8},{4,12},{8,0},{12,4},{16,24},{20,28},{24,16},{28,20},{1,9},{5... | collective-permute-start | bytes 1204232 | tf_op jit(solution)/shard_map/ppermute | solution.py:645
  14.1 4.9 %mix.6 = (bf16[640,640]{1,0:T(8,128)(2,1)}, bf16[320,640]{1,0:T(8,128)(2,1)S(1)}, bf16[320,640]{1,0:T(8,128)(2,1)S(1)}) custom-call(s32[2]{0:T(128)S(1)} %pad_add_fusion.place_ref, f32[8,32]{1,0:T(8,128)S(1)} %copy-done.4, bf16[4,320,640]{2,1,0:T(8,128)(2,1)} %bitcast.20, bf16[4,320,640]{2,1,0:T(8,128)(2,1)S(1)} %collective-permute-done.2.other_ref), custom_call_target="tpu_custom_call" | custom-call | tf_op jit(solution)/shard_map/mix/pallas_call | solution.py:114
  27.4 6.0 %enter_frame.1 = (bf16[128,3712]{1,0:T(8,128)(2,1)S(1)}, bf16[128,3712]{1,0:T(8,128)(2,1)S(1)}, bf16[928,128]{1,0:T(8,128)(2,1)S(1)}, bf16[928,128]{1,0:T(8,128)...) custom-call(s32[2]{0:T(128)S(1)} %pad_add_fusion.place_ref, s32[1,1]{1,0:T(1,128)S(6)} %copy.16.count_ref, ...), custom_call_target="tpu_custom_call" | custom-call | tf_op jit(solution)/shard_map/enter_frame/pallas_call | solution.py:263
  33.4 2.8 %collective-permute-done.7.refs_1_ = bf16[2048,128]{1,0:T(8,128)(2,1)S(1)} collective-permute-done((bf16[2048,128]{1,0:T(8,128)(2,1)S(1)}, bf16[2048,128]{1,0:T(8,128)(2,1)S(1)}, u32[]{:S(2)}, u32[]{:S(2)}) %collective-permute-start.7) | collective-permute-done | bytes 524320 | tf_op jit(solution)/shard_map/ppermute | solution.py:581
  41.1 3.2 %mix.7 = (bf16[384,768]{1,0:T(8,128)(2,1)S(1)}, bf16[192,768]{1,0:T(8,128)(2,1)S(1)}, bf16[192,768]{1,0:T(8,128)(2,1)S(1)}) custom-call(s32[2]{0:T(128)S(1)} %pad_add_fusion.place_ref, f32[8,32]{1,0:T(8,128)S(1)} %copy-done.4, bf16[4,384,768]{2,1,0:T(8,128)(2,1)} %bitcast.17, bf16[4,384,768]{2,1,0:T(8,128)(2,1)S(1)} %collective-permute-done.5.other_ref), custom_call_target="tpu_custom_call" | custom-call | tf_op jit(solution)/shard_map/mix/pallas_call | solution.py:114
  46.0 7.4 %collective-permute-done.9.refs_2_ = bf16[2048,128]{1,0:T(8,128)(2,1)S(1)} collective-permute-done((bf16[2048,128]{1,0:T(8,128)(2,1)S(1)}, bf16[2048,128]{1,0:T(8,128)(2,1)S(1)}, u32[]{:S(2)}, u32[]{:S(2)}) %collective-permute-start.9) | collective-permute-done | bytes 524320 | tf_op jit(solution)/shard_map/ppermute | solution.py:581
  53.4 3.6 %collective-permute-start.10 = (bf16[112,896]{1,0:T(8,128)(2,1)}, bf16[112,896]{1,0:T(8,128)(2,1)S(1)}, u32[]{:S(2)}, u32[]{:S(2)}) collective-permute-start(bf16[112,896]{1,0:T(8,128)(2,1)} %add_convert_fusion.7), channel_id=1, source_target_pairs={{0,24},{4,28},{8,16},{12,20},{16,8},{20,12},{24,0},{28,4},{1,25},{... | collective-permute-start | bytes 602120 | tf_op jit(solution)/shard_map/ppermute | solution.py:651
  57.0 3.2 %mix.8 = (bf16[384,768]{1,0:T(8,128)(2,1)S(1)}, bf16[192,768]{1,0:T(8,128)(2,1)S(1)}, bf16[192,768]{1,0:T(8,128)(2,1)S(1)}) custom-call(s32[2]{0:T(128)S(1)} %pad_add_fusion.place_ref, f32[8,32]{1,0:T(8,128)S(1)} %copy-done.4, bf16[4,384,768]{2,1,0:T(8,128)(2,1)} %bitcast.18, bf16[4,384,768]{2,1,0:T(8,128)(2,1)S(1)} %collective-permute-done.5.other_ref), custom_call_target="tpu_custom_call" | custom-call | tf_op jit(solution)/shard_map/mix/pallas_call | solution.py:114
  60.2 7.2 %peer_frames.1.backs = bf16[3,128,3712]{2,1,0:T(8,128)(2,1)S(1)} custom-call(bf16[2048,128]{1,0:T(8,128)(2,1)S(1)} %collective-permute-done.6.refs_0_, bf16[2048,128]{1,0:T(8,128)(2,1)S(1)} %collective-permute-done.7.refs_1_, bf16[2048,128]{1,0:T(8,128)(2,1)S(1)} %collective-permute-done.9.refs_2_), custom_call_target="tpu_custom_call" | custom-call | tf_op jit(solution)/shard_map/peer_frames/pallas_call | solution.py:300
  69.4 3.0 %mix.9 = (bf16[224,896]{1,0:T(8,128)(2,1)S(1)}, bf16[112,896]{1,0:T(8,128)(2,1)S(1)}, bf16[112,896]{1,0:T(8,128)(2,1)S(1)}) custom-call(s32[2]{0:T(128)S(1)} %pad_add_fusion.place_ref, f32[8,32]{1,0:T(8,128)S(1)} %copy-done.4, bf16[4,224,896]{2,1,0:T(8,128)(2,1)} %own_ref.3, bf16[4,224,896]{2,1,0:T(8,128)(2,1)S(1)} %collective-permute-done.other_ref), custom_call_target="tpu_custom_call" | custom-call | tf_op jit(solution)/shard_map/mix/pallas_call | solution.py:114
  74.6 8.8 %collective-permute-done.16.refs_5_ = bf16[320,640]{1,0:T(8,128)(2,1)S(1)} collective-permute-done((bf16[320,640]{1,0:T(8,128)(2,1)S(1)}, bf16[320,640]{1,0:T(8,128)(2,1)S(1)}, u32[]{:S(2)}, u32[]{:S(2)}) %collective-permute-start.16) | collective-permute-done | bytes 409632 | tf_op jit(solution)/shard_map/ppermute | solution.py:651
  87.1 7.7 %collective-permute-done.15 = bf16[384,768]{1,0:T(8,128)(2,1)S(1)} collective-permute-done((bf16[384,768]{1,0:T(8,128)(2,1)S(1)}, bf16[384,768]{1,0:T(8,128)(2,1)S(1)}, u32[]{:S(2)}, u32[]{:S(2)}) %collective-permute-start.15) | collective-permute-done | bytes 589856 | tf_op jit(solution)/shard_map/ppermute | solution.py:645
  94.8 4.1 %collective-permute-start.21 = (bf16[192,768]{1,0:T(8,128)(2,1)S(1)}, bf16[192,768]{1,0:T(8,128)(2,1)S(1)}, u32[]{:S(2)}, u32[]{:S(2)}) collective-permute-start(bf16[192,768]{1,0:T(8,128)(2,1)S(1)} %add_convert_fusion.2), channel_id=1, source_target_pairs={{0,24},{4,28},{8,16},{12,20},{16,8},{20,12},{24,0},{28,4},{1,25},{... | collective-permute-start | bytes 884744 | tf_op jit(solution)/shard_map/ppermute | solution.py:651
  98.9 3.5 %collective-permute-done.18 = bf16[192,768]{1,0:T(8,128)(2,1)S(1)} collective-permute-done((bf16[192,768]{1,0:T(8,128)(2,1)S(1)}, bf16[192,768]{1,0:T(8,128)(2,1)S(1)}, u32[]{:S(2)}, u32[]{:S(2)}) %collective-permute-start.18) | collective-permute-done | bytes 294944 | tf_op jit(solution)/shard_map/ppermute | solution.py:651
  107.2 8.1 %collective-permute-done.17 = bf16[224,896]{1,0:T(8,128)(2,1)S(1)} collective-permute-done((bf16[224,896]{1,0:T(8,128)(2,1)S(1)}, bf16[224,896]{1,0:T(8,128)(2,1)S(1)}, u32[]{:S(2)}, u32[]{:S(2)}) %collective-permute-start.17) | collective-permute-done | bytes 401440 | tf_op jit(solution)/shard_map/ppermute | solution.py:645
  117.8 5.1 %collective-permute-done.25 = bf16[112,896]{1,0:T(8,128)(2,1)S(1)} collective-permute-done((bf16[112,896]{1,0:T(8,128)(2,1)S(1)}, bf16[112,896]{1,0:T(8,128)(2,1)S(1)}, u32[]{:S(2)}, u32[]{:S(2)}) %collective-permute-start.25) | collective-permute-done | bytes 200736 | tf_op jit(solution)/shard_map/ppermute | solution.py:651
  123.0 2.8 %collective-permute-done.26.refs_5_ = bf16[192,768]{1,0:T(8,128)(2,1)S(1)} collective-permute-done((bf16[192,768]{1,0:T(8,128)(2,1)S(1)}, bf16[192,768]{1,0:T(8,128)(2,1)S(1)}, u32[]{:S(2)}, u32[]{:S(2)}) %collective-permute-start.26) | collective-permute-done | bytes 294944 | tf_op jit(solution)/shard_map/ppermute | solution.py:581
  129.9 3.4 %weight_grads.1 = (bf16[224,896]{1,0:T(8,128)(2,1)}, bf16[2,192,768]{2,1,0:T(8,128)(2,1)}, bf16[2,160,640]{2,1,0:T(8,128)(2,1)}) custom-call(bf16[128,3712]{1,0:T(8,128)(2,1)S(1)} %get-tuple-element.176.back_ref, bf16[3,128,3712]{2,1,0:T(8,128)(2,1)S(1)} %peer_frames.1.backs, bf16[928,128]{1,0:T(8,128)(2,1)S(1)} %get-tuple-element.178.refs_0_, ...), custom_call_target="tpu_custom_call" | custom-call | tf_op jit(solution)/shard_map/weight_grads/pallas_call | solution.py:336
  135.6 2.6 %collective-permute-done.28.refs_7_ = bf16[192,768]{1,0:T(8,128)(2,1)S(1)} collective-permute-done((bf16[192,768]{1,0:T(8,128)(2,1)S(1)}, bf16[192,768]{1,0:T(8,128)(2,1)S(1)}, u32[]{:S(2)}, u32[]{:S(2)}) %collective-permute-start.28) | collective-permute-done | bytes 294944 | tf_op jit(solution)/shard_map/ppermute | solution.py:581
  138.3 2.7 %apply_weights_1.1 = (bf16[1536,128]{1,0:T(8,128)(2,1)S(1)}, bf16[1536,128]{1,0:T(8,128)(2,1)S(1)}) custom-call(s32[2]{0:T(128)S(1)} %pad_add_fusion.place_ref, bf16[128,3712]{1,0:T(8,128)(2,1)S(1)} %get-tuple-element.185.frame_ref, bf16[128,3712]{1,0:T(8,128)(2,1)S(1)} %get-tuple-element.176.back_ref, bf16[192,768]{1,0:T(8,128)(2,1)S(1)} %add_convert_fusion.3.refs_0_, ...), custom_call_target="tpu_custom_call" | custom-call | tf_op jit(solution)/shard_map/apply_weights_1/pallas_call | solution.py:402
  142.7 2.4 %leave_frame_back.1 = (f32[32,6272]{1,0:T(8,128)S(1)}, bf16[16,6272]{1,0:T(8,128)(2,1)S(1)}) custom-call(bf16[896,128]{1,0:T(8,128)(2,1)S(1)} %get-tuple-element.193.zero_ref, bf16[1536,128]{1,0:T(8,128)(2,1)S(1)} %get-tuple-element.194.one_ref, bf16[1280,128]{1,0:T(8,128)(2,1)S(1)} %get-tuple-element.195.two_ref, bf16[455,128]{1,0:T(8,128)(2,1)S(1)} %copy-done.3, ...), custom_call_target="tpu_custom_call" | custom-call | tf_op jit(solution)/shard_map/leave_frame_back/pallas_call | solution.py:510
  145.3 2.8 %collective-permute-start.33 = (bf16[8,6272]{1,0:T(8,128)(2,1)S(1)}, bf16[8,6272]{1,0:T(8,128)(2,1)S(1)}, u32[]{:S(2)}, u32[]{:S(2)}) collective-permute-start(bf16[8,6272]{1,0:T(8,128)(2,1)S(1)} %get-tuple-element.202), channel_id=1, source_target_pairs={{1,0},{2,1},{3,2},{0,3},{5,4},{6,5},{7,6},{4,7},{9,8},{10,9},{11,1... | collective-permute-start | bytes 301064 | tf_op jit(solution)/shard_map/ppermute | solution.py:769
  148.1 2.9 %leave_frame.1 = bf16[32,6272]{1,0:T(8,128)(2,1)} custom-call(bf16[896,128]{1,0:T(8,128)(2,1)S(1)} %get-tuple-element.190.zero_ref, bf16[1536,128]{1,0:T(8,128)(2,1)S(1)} %get-tuple-element.191.one_ref, bf16[1280,128]{1,0:T(8,128)(2,1)S(1)} %get-tuple-element.192.two_ref, bf16[455,128]{1,0:T(8,128)(2,1)S(1)} %copy-done.3, s32[1,1]{1,0:T(1,128)S(6)} %copy.16.count_ref, ...), custom_call_target="tpu_custom_call" | custom-call | tf_op jit(solution)/shard_map/leave_frame/pallas_call | solution.py:525
  (92 shorter events, 46.8 us)
Async XLA Ops:
  8.4 12.6 %collective-permute-start.1 = (bf16[224,896]{1,0:T(8,128)(2,1)S(1)}, bf16[224,896]{1,0:T(8,128)(2,1)S(1)}, u32[]{:S(2)}, u32[]{:S(2)}) collective-permute-start(bf16[224,896]{1,0:T(8,128)(2,1)S(1)} %get-tuple-element.107), channel_id=1, source_target_pairs={{0,8},{4,12},{8,0},{12,4},{16,24},{20,28},{24,16},{28,20},{1,9},{5... | collective-permute-start | bytes 1204232 | tf_op jit(solution)/shard_map/ppermute | solution.py:645
  21.0 18.0 %collective-permute-start.5 = (bf16[4,384,768]{2,1,0:T(8,128)(2,1)}, bf16[4,384,768]{2,1,0:T(8,128)(2,1)S(1)}, u32[]{:S(2)}, u32[]{:S(2)}) collective-permute-start(bf16[4,384,768]{2,1,0:T(8,128)(2,1)} %bitcast.16), channel_id=1, source_target_pairs={{0,4},{4,0},{8,12},{12,8},{16,20},{20,16},{24,28},{28,24},{1,5},{5... | collective-permute-start | bytes 7077896 | tf_op jit(solution)/shard_map/ppermute | solution.py:638
  21.8 14.4 %collective-permute-start.7 = (bf16[2048,128]{1,0:T(8,128)(2,1)S(1)}, bf16[2048,128]{1,0:T(8,128)(2,1)S(1)}, u32[]{:S(2)}, u32[]{:S(2)}) collective-permute-start(bf16[2048,128]{1,0:T(8,128)(2,1)S(1)} %pack_inputs.1), channel_id=1, source_target_pairs={{0,2},{1,3},{2,0},{3,1},{4,6},{5,7},{6,4},{7,5},{8,10},{9,11},{10,... | collective-permute-start | bytes 1572872 | tf_op jit(solution)/shard_map/ppermute | solution.py:581
  23.5 14.1 %collective-permute-start.6 = (bf16[2048,128]{1,0:T(8,128)(2,1)S(1)}, bf16[2048,128]{1,0:T(8,128)(2,1)S(1)}, u32[]{:S(2)}, u32[]{:S(2)}) collective-permute-start(bf16[2048,128]{1,0:T(8,128)(2,1)S(1)} %pack_inputs.1), channel_id=1, source_target_pairs={{0,1},{1,0},{2,3},{3,2},{4,5},{5,4},{6,7},{7,6},{8,9},{9,8},{10,11... | collective-permute-start | bytes 1572872 | tf_op jit(solution)/shard_map/ppermute | solution.py:581
  25.8 41.7 %collective-permute-start.8 = (bf16[640,640]{1,0:T(8,128)(2,1)}, bf16[640,640]{1,0:T(8,128)(2,1)S(1)}, u32[]{:S(2)}, u32[]{:S(2)}) collective-permute-start(bf16[640,640]{1,0:T(8,128)(2,1)} %get-tuple-element.127), channel_id=1, source_target_pairs={{0,8},{4,12},{8,0},{12,4},{16,24},{20,28},{24,16},{28,20},{1,9},{5... | collective-permute-start | bytes 2457608 | tf_op jit(solution)/shard_map/ppermute | solution.py:645
  37.6 15.8 %collective-permute-start.9 = (bf16[2048,128]{1,0:T(8,128)(2,1)S(1)}, bf16[2048,128]{1,0:T(8,128)(2,1)S(1)}, u32[]{:S(2)}, u32[]{:S(2)}) collective-permute-start(bf16[2048,128]{1,0:T(8,128)(2,1)S(1)} %pack_inputs.1), channel_id=1, source_target_pairs={{0,3},{1,2},{2,1},{3,0},{4,7},{5,6},{6,5},{7,4},{8,11},{9,10},{10,... | collective-permute-start | bytes 1572872 | tf_op jit(solution)/shard_map/ppermute | solution.py:581
  39.0 28.4 %collective-permute-start.11 = (bf16[928,128]{1,0:T(8,128)(2,1)}, bf16[928,128]{1,0:T(8,128)(2,1)S(1)}, u32[]{:S(2)}, u32[]{:S(2)}) collective-permute-start(bf16[928,128]{1,0:T(8,128)(2,1)} %get-tuple-element.137), channel_id=1, source_target_pairs={{0,1},{1,0},{2,3},{3,2},{4,5},{5,4},{6,7},{7,6},{8,9},{9,8},{10,11... | collective-permute-start | bytes 712712 | tf_op jit(solution)/shard_map/ppermute | solution.py:581
  39.4 28.0 %collective-permute-start.12 = (bf16[928,128]{1,0:T(8,128)(2,1)S(1)}, bf16[928,128]{1,0:T(8,128)(2,1)S(1)}, u32[]{:S(2)}, u32[]{:S(2)}) collective-permute-start(bf16[928,128]{1,0:T(8,128)(2,1)S(1)} %get-tuple-element.138), channel_id=1, source_target_pairs={{0,2},{1,3},{2,0},{3,1},{4,6},{5,7},{6,4},{7,5},{8,10},{9,11},{10,... | collective-permute-start | bytes 712712 | tf_op jit(solution)/shard_map/ppermute | solution.py:581
  44.3 30.2 %collective-permute-start.13 = (bf16[384,768]{1,0:T(8,128)(2,1)S(1)}, bf16[384,768]{1,0:T(8,128)(2,1)}, u32[]{:S(2)}, u32[]{:S(2)}) collective-permute-start(bf16[384,768]{1,0:T(8,128)(2,1)S(1)} %get-tuple-element.144), channel_id=1, source_target_pairs={{0,8},{4,12},{8,0},{12,4},{16,24},{20,28},{24,16},{28,20},{1,9},{5... | collective-permute-start | bytes 1769480 | tf_op jit(solution)/shard_map/ppermute | solution.py:645
  53.4 14.0 %collective-permute-start.10 = (bf16[112,896]{1,0:T(8,128)(2,1)}, bf16[112,896]{1,0:T(8,128)(2,1)S(1)}, u32[]{:S(2)}, u32[]{:S(2)}) collective-permute-start(bf16[112,896]{1,0:T(8,128)(2,1)} %add_convert_fusion.7), channel_id=1, source_target_pairs={{0,24},{4,28},{8,16},{12,20},{16,8},{20,12},{24,0},{28,4},{1,25},{... | collective-permute-start | bytes 602120 | tf_op jit(solution)/shard_map/ppermute | solution.py:651
  69.1 14.3 %collective-permute-start.16 = (bf16[320,640]{1,0:T(8,128)(2,1)S(1)}, bf16[320,640]{1,0:T(8,128)(2,1)S(1)}, u32[]{:S(2)}, u32[]{:S(2)}) collective-permute-start(bf16[320,640]{1,0:T(8,128)(2,1)S(1)} %add_convert_fusion), channel_id=1, source_target_pairs={{0,24},{4,28},{8,16},{12,20},{16,8},{20,12},{24,0},{28,4},{1,25},{... | collective-permute-start | bytes 1228808 | tf_op jit(solution)/shard_map/ppermute | solution.py:651
  74.5 20.2 %collective-permute-start.15 = (bf16[384,768]{1,0:T(8,128)(2,1)S(1)}, bf16[384,768]{1,0:T(8,128)(2,1)S(1)}, u32[]{:S(2)}, u32[]{:S(2)}) collective-permute-start(bf16[384,768]{1,0:T(8,128)(2,1)S(1)} %get-tuple-element.147), channel_id=1, source_target_pairs={{0,8},{4,12},{8,0},{12,4},{16,24},{20,28},{24,16},{28,20},{1,9},{5... | collective-permute-start | bytes 1769480 | tf_op jit(solution)/shard_map/ppermute | solution.py:645
  83.6 19.9 %collective-permute-start.20 = (bf16[2384,128]{1,0:T(8,128)(2,1)S(1)}, bf16[2384,128]{1,0:T(8,128)(2,1)S(1)}, u32[]{:S(2)}, u32[]{:S(2)}) collective-permute-start(bf16[2384,128]{1,0:T(8,128)(2,1)S(1)} %finish_first.1.refs_0_), channel_id=1, source_target_pairs={{0,2},{1,3},{2,0},{3,1},{4,6},{5,7},{6,4},{7,5},{8,10},{9,11},{10,... | collective-permute-start | bytes 1830920 | tf_op jit(solution)/shard_map/ppermute | solution.py:581
  85.2 18.4 %collective-permute-start.19 = (bf16[2384,128]{1,0:T(8,128)(2,1)S(1)}, bf16[2384,128]{1,0:T(8,128)(2,1)S(1)}, u32[]{:S(2)}, u32[]{:S(2)}) collective-permute-start(bf16[2384,128]{1,0:T(8,128)(2,1)S(1)} %finish_first.1.refs_0_), channel_id=1, source_target_pairs={{0,1},{1,0},{2,3},{3,2},{4,5},{5,4},{6,7},{7,6},{8,9},{9,8},{10,11... | collective-permute-start | bytes 1830920 | tf_op jit(solution)/shard_map/ppermute | solution.py:581
  86.8 15.7 %collective-permute-start.18 = (bf16[192,768]{1,0:T(8,128)(2,1)S(1)}, bf16[192,768]{1,0:T(8,128)(2,1)S(1)}, u32[]{:S(2)}, u32[]{:S(2)}) collective-permute-start(bf16[192,768]{1,0:T(8,128)(2,1)S(1)} %add_convert_fusion.4), channel_id=1, source_target_pairs={{0,24},{4,28},{8,16},{12,20},{16,8},{20,12},{24,0},{28,4},{1,25},{... | collective-permute-start | bytes 884744 | tf_op jit(solution)/shard_map/ppermute | solution.py:651
  94.7 20.5 %collective-permute-start.17 = (bf16[224,896]{1,0:T(8,128)(2,1)S(1)}, bf16[224,896]{1,0:T(8,128)(2,1)S(1)}, u32[]{:S(2)}, u32[]{:S(2)}) collective-permute-start(bf16[224,896]{1,0:T(8,128)(2,1)S(1)} %get-tuple-element.155), channel_id=1, source_target_pairs={{0,8},{4,12},{8,0},{12,4},{16,24},{20,28},{24,16},{28,20},{1,9},{5... | collective-permute-start | bytes 1204232 | tf_op jit(solution)/shard_map/ppermute | solution.py:645
  94.8 20.6 %collective-permute-start.21 = (bf16[192,768]{1,0:T(8,128)(2,1)S(1)}, bf16[192,768]{1,0:T(8,128)(2,1)S(1)}, u32[]{:S(2)}, u32[]{:S(2)}) collective-permute-start(bf16[192,768]{1,0:T(8,128)(2,1)S(1)} %add_convert_fusion.2), channel_id=1, source_target_pairs={{0,24},{4,28},{8,16},{12,20},{16,8},{20,12},{24,0},{28,4},{1,25},{... | collective-permute-start | bytes 884744 | tf_op jit(solution)/shard_map/ppermute | solution.py:651
  103.6 12.0 %collective-permute-start.23 = (bf16[192,768]{1,0:T(8,128)(2,1)S(1)}, bf16[192,768]{1,0:T(8,128)(2,1)S(1)}, u32[]{:S(2)}, u32[]{:S(2)}) collective-permute-start(bf16[192,768]{1,0:T(8,128)(2,1)S(1)} %add_convert_fusion.3.refs_0_), channel_id=1, source_target_pairs={{0,2},{1,3},{2,0},{3,1},{4,6},{5,7},{6,4},{7,5},{8,10},{9,11},{10,... | collective-permute-start | bytes 884744 | tf_op jit(solution)/shard_map/ppermute | solution.py:581
  105.7 22.7 %collective-permute-start.29 = (bf16[2384,128]{1,0:T(8,128)(2,1)S(1)}, bf16[2384,128]{1,0:T(8,128)(2,1)S(1)}, u32[]{:S(2)}, u32[]{:S(2)}) collective-permute-start(bf16[2384,128]{1,0:T(8,128)(2,1)S(1)} %collective-permute-done.20.refs_2_), channel_id=1, source_target_pairs={{0,1},{1,0},{2,3},{3,2},{4,5},{5,4},{6,7},{7,6},{8,9},{9,8},{10,11... | collective-permute-start | bytes 1830920 | tf_op jit(solution)/shard_map/ppermute | solution.py:581
  117.3 18.3 %collective-permute-start.24 = (bf16[192,768]{1,0:T(8,128)(2,1)S(1)}, bf16[192,768]{1,0:T(8,128)(2,1)S(1)}, u32[]{:S(2)}, u32[]{:S(2)}) collective-permute-start(bf16[192,768]{1,0:T(8,128)(2,1)S(1)} %collective-permute-done.22.refs_1_), channel_id=1, source_target_pairs={{0,2},{1,3},{2,0},{3,1},{4,6},{5,7},{6,4},{7,5},{8,10},{9,11},{10,... | collective-permute-start | bytes 884744 | tf_op jit(solution)/shard_map/ppermute | solution.py:581
  125.7 12.5 %collective-permute-start.28 = (bf16[192,768]{1,0:T(8,128)(2,1)S(1)}, bf16[192,768]{1,0:T(8,128)(2,1)S(1)}, u32[]{:S(2)}, u32[]{:S(2)}) collective-permute-start(bf16[192,768]{1,0:T(8,128)(2,1)S(1)} %collective-permute-done.26.refs_5_), channel_id=1, source_target_pairs={{0,2},{1,3},{2,0},{3,1},{4,6},{5,7},{6,4},{7,5},{8,10},{9,11},{10,... | collective-permute-start | bytes 884744 | tf_op jit(solution)/shard_map/ppermute | solution.py:581
  126.4 14.6 %collective-permute-start.32 = (bf16[112,896]{1,0:T(8,128)(2,1)S(1)}, bf16[112,896]{1,0:T(8,128)(2,1)S(1)}, u32[]{:S(2)}, u32[]{:S(2)}) collective-permute-start(bf16[112,896]{1,0:T(8,128)(2,1)S(1)} %add_convert_fusion.5.refs_4_), channel_id=1, source_target_pairs={{0,3},{1,2},{2,1},{3,0},{4,7},{5,6},{6,5},{7,4},{8,11},{9,10},{10,... | collective-permute-start | bytes 602120 | tf_op jit(solution)/shard_map/ppermute | solution.py:581
  128.0 13.0 %collective-permute-start.31 = (bf16[112,896]{1,0:T(8,128)(2,1)S(1)}, bf16[112,896]{1,0:T(8,128)(2,1)S(1)}, u32[]{:S(2)}, u32[]{:S(2)}) collective-permute-start(bf16[112,896]{1,0:T(8,128)(2,1)S(1)} %add_convert_fusion.5.refs_4_), channel_id=1, source_target_pairs={{0,2},{1,3},{2,0},{3,1},{4,6},{5,7},{6,4},{7,5},{8,10},{9,11},{10,... | collective-permute-start | bytes 602120 | tf_op jit(solution)/shard_map/ppermute | solution.py:581
  128.4 12.6 %collective-permute-start.30 = (bf16[112,896]{1,0:T(8,128)(2,1)S(1)}, bf16[112,896]{1,0:T(8,128)(2,1)S(1)}, u32[]{:S(2)}, u32[]{:S(2)}) collective-permute-start(bf16[112,896]{1,0:T(8,128)(2,1)S(1)} %add_convert_fusion.5.refs_4_), channel_id=1, source_target_pairs={{0,1},{1,0},{2,3},{3,2},{4,5},{5,4},{6,7},{7,6},{8,9},{9,8},{10,11... | collective-permute-start | bytes 602120 | tf_op jit(solution)/shard_map/ppermute | solution.py:581
  (20 other events, 149.5 us)
